TPU v7x, 32 devices: a whole 2x2x4 slice. The times are simulated.
32 devices in a mesh: expert: 8 (over z, x), dp: 4 (over y, core).
Axes of the slice: x: 2, y: 2, z: 4, core: 2. Of those that a mesh axis runs over, the one named last changes fastest.
Arguments:
- inputs: bfloat16 [4096, 2048], P(('expert', 'dp')), may hold values from -6 to 6
- layer_out: bfloat16 [4096, 2048], P(('expert', 'dp')), may hold values from -6 to 6
- teacher: bfloat16 [4096, 2048], P(('expert', 'dp')), may hold values from -6 to 6
- alignment: bfloat16 [4096, 128], P(('expert', 'dp')), may hold values from 0 to 1.5
- routes: int32 [4096, 2], P(('expert', 'dp')), may hold values from 0 to 7, all different within a row; in each aligned block of 128 rows (0 to 127, 128 to 255, ...) at most 40 rows name the same one
- route_weights: bfloat16 [4096, 2], P(('expert', 'dp')), may hold values from 0.19921875 to 1
- partner: int32 [32], P(('expert', 'dp')), may hold values from 0 to 3
- w_gate: bfloat16 [8, 2048, 1408], P('expert', None, 'dp'), may hold values from -0.125 to 0.125
- w_up: bfloat16 [8, 2048, 1408], P('expert', None, 'dp'), may hold values from -0.125 to 0.125
- w_down: bfloat16 [8, 1408, 2048], P('expert', 'dp'), may hold values from -0.15625 to 0.15625
Outputs:
- grad_inputs: bfloat16 [4096, 2048], P(('expert', 'dp'))
- grad_gate: bfloat16 [8, 2048, 1408], P('expert', None, 'dp')
- grad_up: bfloat16 [8, 2048, 1408], P('expert', None, 'dp')
- grad_down: bfloat16 [8, 1408, 2048], P('expert', 'dp')
Inputs may be any that keep to these rules, and one draw needn't show every extreme that they name: `routes`: each row names 2 different experts. The rows of one device name any one expert at most 40 times, and some device names some expert exactly 40 times.
All inputs are finite; a program needn't handle non-finite values.
Results may differ from a plain program's by a relative error of at most 0.019.
Values may be sent and summed in bfloat16 or wider, within the bound.
No kernel may reach another device: no remote copies, remote signals or barrier semaphores. Data moves between devices by JAX's collectives and lax.ppermute only.
A program may use at most 128 MiB of HBM per device.

v0:
```python
import jax
import jax.numpy as jnp
from jax import lax
from jax.sharding import PartitionSpec as P


def route_slots(routes, expert_count, capacity):
    flat_routes = routes.reshape(-1)
    one_hot = (flat_routes[:, None] == jnp.arange(expert_count, dtype=jnp.int32)[None, :]).astype(
        jnp.int32
    )
    earlier = jnp.cumsum(one_hot, axis=0) - one_hot
    slot_index = jnp.sum(earlier * one_hot, axis=1)
    return flat_routes * capacity + slot_index


def cotangent(block_out, block_align, partner_teacher):
    aligned = jnp.dot(block_align, partner_teacher, preferred_element_type=jnp.float32)
    return (block_out.astype(jnp.float32) - aligned).astype(jnp.bfloat16)


def scaled_rows(block_cot, block_weights):
    product = block_weights[:, :, None].astype(jnp.float32) * block_cot[:, None, :].astype(
        jnp.float32
    )
    return product.astype(jnp.bfloat16).reshape(-1, block_cot.shape[1])


def dispatch_rows(block_inputs, out_grad, destination, route_count, expert_count, capacity):
    features = block_inputs.shape[1]
    empty_rows = jnp.zeros((expert_count * capacity, features), jnp.bfloat16)
    input_rows = jnp.repeat(block_inputs, route_count, axis=0)
    sent_inputs = (
        empty_rows.at[destination].set(input_rows).reshape(expert_count, capacity, features)
    )
    sent_grads = empty_rows.at[destination].set(out_grad).reshape(expert_count, capacity, features)
    return (sent_inputs, sent_grads)


def per_device(
    inputs, layer_out, teacher, alignment, routes, route_weights, partner, w_gate, w_up, w_down
):
    tok_rows, features = inputs.shape
    route_count = routes.shape[1]
    expert_count = lax.axis_size("expert")
    capacity = max(2, (5 * tok_rows * route_count + 4 * expert_count - 1) // (4 * expert_count))
    own_destination = route_slots(routes, expert_count, capacity)
    group_teacher = lax.all_gather(teacher, "dp", axis=0, tiled=True)
    partner_teacher = lax.dynamic_slice_in_dim(group_teacher, partner[0] * tok_rows, tok_rows, 0)
    own_cot = cotangent(layer_out, alignment, partner_teacher)
    send_inputs, send_grads = dispatch_rows(
        inputs,
        scaled_rows(own_cot, route_weights),
        own_destination,
        route_count,
        expert_count,
        capacity,
    )
    got_inputs, got_grads = (
        lax.all_to_all(send_inputs, "expert", split_axis=0, concat_axis=0, tiled=True),
        lax.all_to_all(send_grads, "expert", split_axis=0, concat_axis=0, tiled=True),
    )
    recv_inputs, recv_grads = (
        lax.all_gather(got_inputs, "dp", axis=0, tiled=True),
        lax.all_gather(got_grads, "dp", axis=0, tiled=True),
    )
    expert_inputs = recv_inputs.reshape(-1, features)
    expert_grads = recv_grads.reshape(-1, features)
    gate_weight = w_gate[0]
    up_weight = w_up[0]
    down_weight = w_down[0]
    gate_term = jnp.dot(expert_inputs, gate_weight, preferred_element_type=jnp.float32)
    up_term = jnp.dot(expert_inputs, up_weight, preferred_element_type=jnp.float32)
    sigmoid_gate = jax.nn.sigmoid(gate_term)
    activated = gate_term * sigmoid_gate
    hidden = (activated * up_term).astype(jnp.bfloat16)
    by_columns = (((1,), (1,)), ((), ()))
    by_rows = (((0,), (0,)), ((), ()))
    d_hidden = lax.dot_general(
        expert_grads, down_weight, by_columns, preferred_element_type=jnp.float32
    )
    d_gate = (d_hidden * up_term * (sigmoid_gate + activated * (1.0 - sigmoid_gate))).astype(
        jnp.bfloat16
    )
    d_up = (d_hidden * activated).astype(jnp.bfloat16)
    grad_down = lax.dot_general(hidden, expert_grads, by_rows, preferred_element_type=jnp.float32)
    grad_gate = lax.dot_general(expert_inputs, d_gate, by_rows, preferred_element_type=jnp.float32)
    grad_up = lax.dot_general(expert_inputs, d_up, by_rows, preferred_element_type=jnp.float32)
    term = lax.dot_general(d_gate, gate_weight, by_columns, preferred_element_type=jnp.float32)
    own_rows = lax.psum_scatter(
        (
            term + lax.dot_general(d_up, up_weight, by_columns, preferred_element_type=jnp.float32)
        ).astype(jnp.bfloat16),
        "dp",
        scatter_dimension=0,
        tiled=True,
    )
    returned = lax.all_to_all(
        own_rows.reshape(expert_count, capacity, features),
        "expert",
        split_axis=0,
        concat_axis=0,
        tiled=True,
    )
    picked = returned.reshape(expert_count * capacity, features)[own_destination].astype(
        jnp.float32
    )
    grad_inputs = jnp.sum(picked.reshape(tok_rows, route_count, features), axis=1).astype(
        jnp.bfloat16
    )
    return (
        grad_inputs,
        grad_gate.astype(jnp.bfloat16)[None],
        grad_up.astype(jnp.bfloat16)[None],
        grad_down.astype(jnp.bfloat16)[None],
    )


def solution(mesh):
    in_specs = (
        P(("expert", "dp"), None),
        P(("expert", "dp"), None),
        P(("expert", "dp"), None),
        P(("expert", "dp"), None),
        P(("expert", "dp"), None),
        P(("expert", "dp"), None),
        P(("expert", "dp")),
        P("expert", None, "dp"),
        P("expert", None, "dp"),
        P("expert", "dp", None),
    )
    out_specs = (
        P(("expert", "dp"), None),
        P("expert", None, "dp"),
        P("expert", None, "dp"),
        P("expert", "dp", None),
    )
    return jax.shard_map(
        per_device, mesh=mesh, in_specs=in_specs, out_specs=out_specs, check_vma=False
    )
```

profile of v0, /device:TPU:0, one launch (start us, length us, event | category | flops | bytes accessed | tf_op | source)
XLA Modules:
  0.0 258.6 jit_solution(17256565519601491521)
XLA Ops:
  7.2 0.7 all-gather.4.cloned.1.call-update
  8.0 0.8 copy.23
  9.0 0.7 broadcast_multiply_fusion
  10.0 0.6 reduce-window.6
  10.6 0.2 slice_reduce_fusion
  10.8 1.7 broadcast_in_dim.22
  12.5 1.2 reshape.117
  13.8 3.2 %scatter_custom_fusion.1 = bf16[320,2048]{1,0:T(8,128)(2,1)S(1)} fusion(s32[256]{0:T(256)S(1)} %bitcast.63, bf16[256,2048]{1,0:T(8,128)(2,1)} %reshape.117, bf16[]{:T(256)} %constant.7.clone.1), kind=kCustom, calls=%fused_computation.31 | custom fusion | bytes 1311232 | tf_op jit(solution)/shard_map/scatter | solution.py:34
  17.0 38.7 %all_to_all.15 = bf16[8,40,2048]{2,1,0:T(8,128)(2,1)} all-to-all(bf16[8,40,2048]{2,1,0:T(8,128)(2,1)S(1)} %bitcast.61), channel_id=1, replica_groups=mesh['expert'=8,'dp'=4] {'expert'}, dimensions={0} | all-to-all | bytes 2621440 | tf_op jit(solution)/shard_map/all_to_all | solution.py:60
  56.7 0.3 copy.26
  57.1 1.4 fusion.5
  58.4 0.3 copy.27
  58.8 2.6 mul.72
  61.3 2.8 %mul.73 = f32[256,2048]{1,0:T(8,128)S(1)} reshape(f32[128,2,2048]{2,1,0:T(2,128)} %mul.72) | data formatting | bytes 4194304 | tf_op jit(solution)/shard_map/mul | solution.py:23
  64.2 3.3 %scatter_custom_fusion = bf16[320,2048]{1,0:T(8,128)(2,1)} fusion(s32[256]{0:T(256)S(1)} %bitcast.64, f32[256,2048]{1,0:T(8,128)S(1)} %mul.73, f32[256]{0:T(256)S(1)} %reshape.96, bf16[]{:T(256)} %constant.7.clone.1), kind=kCustom, calls=%fused_computation.29 | custom fusion | flops 1048576 | bytes 3408898 | tf_op jit(solution)/shard_map/scatter | solution.py:36
  67.5 34.8 %all_to_all.16 = bf16[8,40,2048]{2,1,0:T(8,128)(2,1)} all-to-all(bf16[8,40,2048]{2,1,0:T(8,128)(2,1)} %bitcast.60), channel_id=1, replica_groups=mesh['expert'=8,'dp'=4] {'expert'}, dimensions={0} | all-to-all | bytes 2621440 | tf_op jit(solution)/shard_map/all_to_all | solution.py:61
  102.3 0.2 reduce-scatter.2.cloned.1.call-start
  102.6 5.9 %fusion.8 = f32[1280,352]{0,1:T(8,128)} fusion(bf16[1280,2048]{1,0:T(8,128)(2,1)} %bitcast.67, bf16[1,2048,352]{1,2,0:T(8,128)(2,1)S(1)} %copy-done), kind=kOutput, calls=%fused_computation.21 | convolution fusion | flops 1845493760 | bytes 8486912 | tf_op jit(solution)/shard_map/dot_general | solution.py:72
  108.5 3.3 %fusion.11 = f32[1280,352]{0,1:T(8,128)} fusion(bf16[1280,2048]{1,0:T(8,128)(2,1)S(1)} %bitcast.70, bf16[1,2048,352]{1,2,0:T(8,128)(2,1)S(1)} %copy-done.1), kind=kOutput, calls=%fused_computation.24 | convolution fusion | flops 1845493760 | bytes 8486912 | tf_op jit(solution)/shard_map/dot_general | solution.py:73
  111.9 29.9 %all-gather.6.cloned.1.call-done = bf16[32,40,2048]{2,1,0:T(8,128)(2,1)} async-done(((bf16[8,40,2048]{2,1,0:T(8,128)(2,1)}), bf16[32,40,2048]{2,1,0:T(8,128)(2,1)}) %all-gather.6.cloned.1.call-update) | async-done | bytes 5242896 | tf_op jit(solution)/shard_map/all_gather | solution.py:65
  141.8 6.4 %multiply_convert_fusion.2 = (bf16[1280,352]{0,1:T(8,128)(2,1)S(1)}, bf16[1280,352]{0,1:T(8,128)(2,1)S(1)}) fusion(f32[1280,352]{0,1:T(8,128)} %fusion.8, f32[1280,352]{0,1:T(8,128)} %fusion.11, bf16[1280,2048]{1,0:T(8,128)(2,1)} %bitcast.71, bf16[1,352,2048]{2,1,0:T(8,128)(2,1)} %param.19), kind=kOutput, calls=%fused_computation.16 | convolution fusion | flops 1850900480 | bytes 12091392 | tf_op jit(solution)/shard_map/dot_general | solution.py:79
  148.2 2.9 %fusion.6 = f32[1280,2048]{1,0:T(8,128)S(1)} fusion(bf16[1280,352]{0,1:T(8,128)(2,1)S(1)} %get-tuple-element.5, bf16[1,2048,352]{1,2,0:T(8,128)(2,1)S(1)} %copy-done), kind=kOutput, calls=%fused_computation.19 | convolution fusion | flops 1845493760 | bytes 12828672 | tf_op jit(solution)/shard_map/dot_general | solution.py:89
  151.2 4.7 %add_convert_fusion = bf16[1280,2048]{1,0:T(8,128)(2,1)} fusion(f32[1280,2048]{1,0:T(8,128)S(1)} %fusion.6, bf16[1280,352]{0,1:T(8,128)(2,1)S(1)} %get-tuple-element.4, bf16[1,2048,352]{1,2,0:T(8,128)(2,1)S(1)} %copy-done.1), kind=kOutput, calls=%fused_computation.3 | convolution fusion | flops 1850736640 | bytes 18071552 | tf_op jit(solution)/shard_map/dot_general | solution.py:92
  155.9 51.6 %reduce-scatter.2.cloned.1.call-done = bf16[320,2048]{1,0:T(8,128)(2,1)} async-done(((bf16[1280,2048]{1,0:T(8,128)(2,1)}), bf16[320,2048]{1,0:T(8,128)(2,1)}) %reduce-scatter.2.cloned.1.call-update) | async-done | bytes 1310736 | tf_op jit(solution)/shard_map/reduce_scatter | solution.py:90
  207.4 5.5 %all-to-all-start.2 = ((bf16[8,40,2048]{2,1,0:T(8,128)(2,1)}), bf16[8,40,2048]{2,1,0:T(8,128)(2,1)S(1)}, u32[]{:S(2)}, u32[]{:S(2)}) async-start(bf16[8,40,2048]{2,1,0:T(8,128)(2,1)} %bitcast.62), calls=%async_computation.3 | async-start | bytes 2621440 | tf_op jit(solution)/shard_map/all_to_all | solution.py:98
  213.0 6.0 %fusion.2 = bf16[1,2048,352]{1,2,0:T(8,128)(2,1)} fusion(bf16[1280,352]{0,1:T(8,128)(2,1)} %copy-done.2, bf16[1280,2048]{1,0:T(8,128)(2,1)} %bitcast.68), kind=kOutput, calls=%fused_computation.9 | convolution fusion | flops 1846214656 | bytes 7585792 | tf_op jit(solution)/shard_map/dot_general | solution.py:88
  219.0 5.8 %fusion.1 = bf16[1,2048,352]{1,2,0:T(8,128)(2,1)} fusion(bf16[1280,352]{0,1:T(8,128)(2,1)S(1)} %copy-done.4, bf16[1280,2048]{1,0:T(8,128)(2,1)} %bitcast.69), kind=kOutput, calls=%fused_computation.8 | convolution fusion | flops 1846214656 | bytes 7585792 | tf_op jit(solution)/shard_map/dot_general | solution.py:87
  224.9 3.2 %fusion = bf16[1,352,2048]{2,1,0:T(8,128)(2,1)} fusion(bf16[1280,2048]{1,0:T(8,128)(2,1)S(1)} %bitcast.74, f32[1280,352]{0,1:T(8,128)S(1)} %copy-done.10, f32[1280,352]{0,1:T(8,128)S(1)} %copy-done.9), kind=kOutput, calls=%fused_computation.7 | convolution fusion | flops 1848918016 | bytes 10289152 | tf_op jit(solution)/shard_map/dot_general | solution.py:86
  228.2 16.2 %all-to-all-done.2 = bf16[8,40,2048]{2,1,0:T(8,128)(2,1)S(1)} async-done(((bf16[8,40,2048]{2,1,0:T(8,128)(2,1)}), bf16[8,40,2048]{2,1,0:T(8,128)(2,1)S(1)}, u32[]{:S(2)}, u32[]{:S(2)}) %all-to-all-start.2) | async-done | bytes 1310752 | tf_op jit(solution)/shard_map/all_to_all | solution.py:98
  244.3 2.3 gather_fusion
  246.7 1.7 gather.6
  248.4 3.6 %reduce_sum.25 = bf16[128,2048]{1,0:T(8,128)(2,1)} reduce(bf16[128,2,2048]{2,1,0:T(2,128)(2,1)S(1)} %gather.6, bf16[]{:T(256)} %constant.7.clone.1), dimensions={1}, to_apply=%region_6.7 | reduce | flops 262144 | bytes 1572866 | tf_op jit(solution)/shard_map/reduce_sum | solution.py:108
  (47 shorter events, 1.2 us)
Async XLA Ops:
  7.2 95.4 %copy-start = (bf16[1,2048,352]{1,2,0:T(8,128)(2,1)S(1)}, bf16[1,2048,352]{1,2,0:T(8,128)(2,1)}, u32[]{:S(2)}) copy-start(bf16[1,2048,352]{1,2,0:T(8,128)(2,1)} %param.17) | copy-start | bytes 4325380
  7.2 49.9 %all-gather.4.cloned.1.call-start = ((), (), s32[]{:S(2)}) async-start(), calls=%async_computation.4 | async-start | bytes 2621440 | tf_op jit(solution)/shard_map/all_gather | solution.py:48
  7.9 94.7 %all-gather.8.cloned.1.call-start = ((), (), s32[]{:S(2)}) async-start(), calls=%async_computation.6 | async-start | bytes 6553600 | tf_op jit(solution)/shard_map/all_gather | solution.py:64
  17.0 39.4 %copy-start.7 = (bf16[128,2]{0,1:T(2,128)(2,1)S(1)}, bf16[128,2]{0,1:T(2,128)(2,1)}, u32[]{:S(2)}) copy-start(bf16[128,2]{0,1:T(2,128)(2,1)} %param.15) | copy-start | bytes 1540
  17.0 39.7 %copy-start.5 = (bf16[128,2048]{1,0:T(8,128)(2,1)S(1)}, bf16[128,2048]{1,0:T(8,128)(2,1)}, u32[]{:S(2)}) copy-start(bf16[128,2048]{1,0:T(8,128)(2,1)} %param.11) | copy-start | bytes 1572868
  55.7 1.3 copy-start.6
  55.8 86.1 %all-gather.6.cloned.1.call-start = ((), (), s32[]{:S(2)}) async-start(), calls=%async_computation.5 | async-start | bytes 6553600 | tf_op jit(solution)/shard_map/all_gather | solution.py:65
  102.3 105.1 %reduce-scatter.2.cloned.1.call-start = ((), (), s32[]{:S(2)}) async-start(), calls=%async_computation.7 | async-start | bytes 6553600 | tf_op jit(solution)/shard_map/reduce_scatter | solution.py:90
  102.6 6.0 %copy-start.1 = (bf16[1,2048,352]{1,2,0:T(8,128)(2,1)S(1)}, bf16[1,2048,352]{1,2,0:T(8,128)(2,1)}, u32[]{:S(2)}) copy-start(bf16[1,2048,352]{1,2,0:T(8,128)(2,1)} %param.18) | copy-start | bytes 4325380
  102.6 5.9 %copy-start.8 = (bf16[32,40,2048]{2,1,0:T(8,128)(2,1)S(1)}, bf16[32,40,2048]{2,1,0:T(8,128)(2,1)}, u32[]{:S(2)}) copy-start(bf16[32,40,2048]{2,1,0:T(8,128)(2,1)} %all-gather.8.cloned.1.call-done) | copy-start | bytes 15728644
  148.2 3.0 %copy-start.3 = (bf16[1280,352]{0,1:T(8,128)(2,1)}, bf16[1280,352]{0,1:T(8,128)(2,1)S(1)}, u32[]{:S(2)}) copy-start(bf16[1280,352]{0,1:T(8,128)(2,1)S(1)} %get-tuple-element.5) | copy-start | bytes 2703364
  148.2 3.0 %copy-start.2 = (bf16[1280,352]{0,1:T(8,128)(2,1)}, bf16[1280,352]{0,1:T(8,128)(2,1)S(1)}, u32[]{:S(2)}) copy-start(bf16[1280,352]{0,1:T(8,128)(2,1)S(1)} %get-tuple-element.4) | copy-start | bytes 2703364
  207.4 36.9 %all-to-all-start.2 = ((bf16[8,40,2048]{2,1,0:T(8,128)(2,1)}), bf16[8,40,2048]{2,1,0:T(8,128)(2,1)S(1)}, u32[]{:S(2)}, u32[]{:S(2)}) async-start(bf16[8,40,2048]{2,1,0:T(8,128)(2,1)} %bitcast.62), calls=%async_computation.3 | async-start | bytes 2621440 | tf_op jit(solution)/shard_map/all_to_all | solution.py:98
  213.0 6.1 %copy-start.4 = (bf16[1280,352]{0,1:T(8,128)(2,1)S(1)}, bf16[1280,352]{0,1:T(8,128)(2,1)}, u32[]{:S(2)}) copy-start(bf16[1280,352]{0,1:T(8,128)(2,1)} %copy-done.3) | copy-start | bytes 2703364
  213.0 11.9 %slice-start = ((s8[5242880]{0:T(1024)(128)(4,1)}), s8[4194304]{0:T(1024)(128)(4,1)S(1)}, s32[]{:S(2)}) async-start(s8[5242880]{0:T(1024)(128)(4,1)} %bitcast.72), calls=%async_computation.8 | async-start | bytes 8388608
  219.0 5.9 %slice-start.1 = ((s8[5242880]{0:T(1024)(128)(4,1)}), s8[1048576]{0:T(1024)(128)(4,1)S(1)}, s32[]{:S(2)}) async-start(s8[5242880]{0:T(1024)(128)(4,1)} %bitcast.72), calls=%async_computation.9 | async-start | bytes 2097152
  219.0 5.9 %copy-start.9 = (f32[1280,352]{0,1:T(8,128)S(1)}, f32[1280,352]{0,1:T(8,128)}, u32[]{:S(2)}) copy-start(f32[1280,352]{0,1:T(8,128)} %fusion.8) | copy-start | bytes 5406724
  219.0 5.9 %copy-start.10 = (f32[1280,352]{0,1:T(8,128)S(1)}, f32[1280,352]{0,1:T(8,128)}, u32[]{:S(2)}) copy-start(f32[1280,352]{0,1:T(8,128)} %fusion.11) | copy-start | bytes 5406724
Sparse Core Ops, SparseCore 0:
  9.6 25.2 all-gather.3
  55.9 39.4 all-gather.7
  102.4 39.3 all-gather.5
  156.0 51.3 reduce-scatter.1
where the time goes:
time: 259 us
  waiting for transfers between devices  98.4 us (38%)
  blocking collectives  73.5 us (28%)
  matrix products  39.7 us (15%)
  local copies, waits for them, and re-layouts  18 us (7%)
  between operations  14.7 us (6%)
  other arithmetic  8.39 us (3%)
  starting transfers between devices  5.85 us (2%)
    reduce_scatter x1, waiting for transfers between devices, per_device(): lax.psum_scatter((term + lax.dot_general(d_up, up_weight, by_columns, pre...  51.6 us
    all_to_all x1, blocking collectives, per_device(): lax.all_to_all(send_inputs, 'expert', split_axis=0, concat_axis=0, tiled=...  38.7 us
    all_to_all x1, blocking collectives, per_device(): lax.all_to_all(send_grads, 'expert', split_axis=0, concat_axis=0, tiled=T...  34.8 us
    all_gather x1, waiting for transfers between devices, per_device(): lax.all_gather(got_grads, 'dp', axis=0, tiled=True)  29.9 us
    all_to_all x1, waiting for transfers between devices, per_device(): lax.all_to_all(own_rows.reshape(expert_count, capacity, features), 'exper...  16.2 us
    dot_general x1, matrix products, per_device(): lax.dot_general(expert_grads, down_weight, by_columns, preferred_element_...  6.38 us
    dot_general x1, matrix products, per_device(): lax.dot_general(expert_inputs, d_up, by_rows, preferred_element_type=jnp....  6.04 us
    dot_general x1, matrix products, per_device(): jnp.dot(expert_inputs, gate_weight, preferred_element_type=jnp.float32)  5.93 us
  transfers between devices with their start and end apart: 5, of which 3 were waited for; matrix products, arithmetic and copies ran while one was open for 17% of the time, Pallas kernels for 0%

commit v1 on v0

v1 whole, which is shorter than its diff:
```python
import jax
import jax.numpy as jnp
import numpy as np
from jax import lax
from jax.sharding import PartitionSpec as P

F32, BF16 = jnp.float32, jnp.bfloat16


def flip(block, axis, shift):
    if shift == 0:
        return block
    return lax.ppermute(block, axis, [(i, i ^ shift) for i in range(lax.axis_size(axis))])


def by_columns(left, right):
    return lax.dot_general(left, right, (((1,), (1,)), ((), ())), preferred_element_type=F32)


def by_rows(left, right):
    return lax.dot_general(left, right, (((0,), (0,)), ((), ())), preferred_element_type=F32)


def slot_matrices(routes, route_weights, experts, capacity):
    named = routes.T[None] == experts[:, None, None]
    weight = jnp.sum(jnp.where(named, route_weights.T[None].astype(F32), 0.0), axis=1)
    member = jnp.any(named, axis=1)
    tokens = routes.shape[0]
    before = jnp.arange(tokens)[:, None] < jnp.arange(tokens)[None, :]
    earlier = jnp.dot(member.astype(BF16), before.astype(BF16), preferred_element_type=F32)
    slots = jnp.arange(capacity, dtype=F32)[None, :, None]
    filled = member[:, None, :] & (earlier[:, None, :] == slots)
    return filled.astype(BF16), jnp.where(filled, weight[:, None, :], 0.0).astype(BF16)


def exchange_groups(expert_count):
    if expert_count == 8:
        return [(0, 1, 2, 3), (4, 5), (6, 7)]
    return [tuple(range(expert_count))]


def to_experts(blocks, groups, capacity):
    if len(groups) == 1:
        rows = blocks[0]
        got = lax.all_to_all(
            rows.reshape(-1, capacity, rows.shape[-1]), "expert", split_axis=0, concat_axis=0, tiled=True
        )
        return [got.reshape(rows.shape)]
    return [
        jnp.concatenate(
            [flip(block[n * capacity : (n + 1) * capacity], "expert", k) for n, k in enumerate(group)], axis=0
        )
        for block, group in zip(blocks, groups)
    ]


def per_device(
    inputs, layer_out, teacher, alignment, routes, route_weights, partner, w_gate, w_up, w_down
):
    tok_rows, features = inputs.shape
    route_count = routes.shape[1]
    expert_count = lax.axis_size("expert")
    capacity = max(2, (5 * tok_rows * route_count + 4 * expert_count - 1) // (4 * expert_count))
    me = lax.axis_index("expert")
    groups = exchange_groups(expert_count)

    def joined(weight, axis):
        return jnp.concatenate([weight, flip(weight, "dp", 1)], axis=axis)

    gate_weight = joined(w_gate[0], 1)
    up_weight = joined(w_up[0], 1)
    down_weight = joined(w_down[0], 0)
    quarter = w_gate.shape[2]

    order = np.array([k for group in groups for k in group], dtype=np.int32)
    experts = jnp.asarray(order) if len(groups) == 1 else jnp.asarray(order) ^ me
    filled, weighted = slot_matrices(routes, route_weights, experts, capacity)
    edges = np.cumsum([0] + [len(group) for group in groups])
    filled = [filled[a:b].reshape(-1, tok_rows) for a, b in zip(edges[:-1], edges[1:])]
    weighted = [weighted[a:b].reshape(-1, tok_rows) for a, b in zip(edges[:-1], edges[1:])]

    across = flip(teacher, "dp", 2)
    beside, beside_across = flip(teacher, "dp", 1), flip(across, "dp", 1)
    apart = partner[0] ^ lax.axis_index("dp")
    partner_teacher = jnp.where(
        apart < 2,
        jnp.where(apart == 0, teacher, beside),
        jnp.where(apart == 2, across, beside_across),
    )
    aligned = jnp.dot(alignment, partner_teacher, preferred_element_type=F32)
    cotangent = (layer_out.astype(F32) - aligned).astype(BF16)

    sent_inputs = [jnp.dot(m, inputs, preferred_element_type=F32).astype(BF16) for m in filled]
    sent_grads = [jnp.dot(m, cotangent, preferred_element_type=F32).astype(BF16) for m in weighted]
    got_inputs = to_experts(sent_inputs, groups, capacity)
    got_grads = to_experts(sent_grads, groups, capacity)
    expert_inputs = [jnp.concatenate([rows, flip(rows, "dp", 2)], axis=0) for rows in got_inputs]
    expert_grads = [jnp.concatenate([rows, flip(rows, "dp", 2)], axis=0) for rows in got_grads]

    hidden, d_gate, d_up, returned = [], [], [], []
    for rows, grads in zip(expert_inputs, expert_grads):
        gate_term = jnp.dot(rows, gate_weight, preferred_element_type=F32)
        up_term = jnp.dot(rows, up_weight, preferred_element_type=F32)
        sigmoid_gate = jax.nn.sigmoid(gate_term)
        activated = gate_term * sigmoid_gate
        hidden.append((activated * up_term).astype(BF16))
        d_hidden = by_columns(grads, down_weight)
        one_gate = (d_hidden * up_term * (sigmoid_gate + activated * (1.0 - sigmoid_gate))).astype(BF16)
        one_up = (d_hidden * activated).astype(BF16)
        d_gate.append(one_gate)
        d_up.append(one_up)
        row_sums = by_columns(one_gate, gate_weight) + by_columns(one_up, up_weight)
        half = rows.shape[0] // 2
        other = flip(row_sums[half:].astype(BF16), "dp", 2)
        returned.append((row_sums[:half] + other.astype(F32)).astype(BF16))
    back = to_experts(returned, groups, capacity)
    grad_inputs = sum(by_rows(m, rows) for m, rows in zip(filled, back)).astype(BF16)

    inputs_all = jnp.concatenate(expert_inputs, axis=0)
    grads_all = jnp.concatenate(expert_grads, axis=0)
    hidden, d_gate, d_up = (jnp.concatenate(parts, axis=0) for parts in (hidden, d_gate, d_up))

    def summed(own, other):
        return (own + flip(other.astype(BF16), "dp", 1).astype(F32)).astype(BF16)[None]

    grad_gate = summed(by_rows(inputs_all, d_gate[:, :quarter]), by_rows(inputs_all, d_gate[:, quarter:]))
    grad_up = summed(by_rows(inputs_all, d_up[:, :quarter]), by_rows(inputs_all, d_up[:, quarter:]))
    grad_down = summed(by_rows(hidden[:, :quarter], grads_all), by_rows(hidden[:, quarter:], grads_all))
    return grad_inputs, grad_gate, grad_up, grad_down


def solution(mesh):
    tokens = P(("expert", "dp"), None)
    columns, rows = P("expert", None, "dp"), P("expert", "dp", None)
    return jax.shard_map(
        per_device,
        mesh=mesh,
        in_specs=(tokens,) * 6 + (P(("expert", "dp")), columns, columns, rows),
        out_specs=(tokens, columns, columns, rows),
        check_vma=False,
    )
```

time: 259 us -> 199 us (0.77)
  blocking collectives: 73.5 us -> 0 us
  starting transfers between devices: 5.85 us -> 69.3 us
  local copies, waits for them, and re-layouts: 18 us -> 2.37 us
  between operations: 14.7 us -> 2.32 us
  matrix products: 39.7 us -> 32.2 us
  waiting for transfers between devices: 98.4 us -> 90.9 us
  other arithmetic: 8.39 us -> 1.68 us
    ppermute x0 -> x39, waiting for transfers between devices: none -> 90.9 us  [flip(): lax.ppermute(block, axis, [(i, i ^ shift) for i in range(lax.axis_size(ax...]
    all_to_all x2 -> x0, blocking collectives: 73.5 us -> none  [the longest x1 38.7 us: per_device(): lax.all_to_all(send_inputs, 'expert', split_axis=0, concat_axis=0, tiled=...]
    ppermute x0 -> x39, starting transfers between devices: none -> 69.3 us  [flip(): lax.ppermute(block, axis, [(i, i ^ shift) for i in range(lax.axis_size(ax...]
    reduce_scatter x1 -> x0, waiting for transfers between devices: 51.6 us -> none  [per_device(): lax.psum_scatter((term + lax.dot_general(d_up, up_weight, by_columns, pre...]
    all_gather x3 -> x0, waiting for transfers between devices: 30 us -> none  [the longest x1 29.9 us: per_device(): lax.all_gather(got_grads, 'dp', axis=0, tiled=True)]
    all_to_all x1 -> x0, waiting for transfers between devices: 16.2 us -> none  [per_device(): lax.all_to_all(own_rows.reshape(expert_count, capacity, features), 'exper...]
    dot_general x9 -> x32, matrix products: 39.7 us -> 32.2 us  [the longest x9 13.5 us: by_rows(): lax.dot_general(left, right, (((0,), (0,)), ((), ())), preferred_element_...]
    mul x6 -> x0, local copies, waits for them, and re-layouts: 5.89 us -> none  [the longest x4 5.64 us: scaled_rows(): block_weights[:, :, None].astype(jnp.float32)]
  transfers between devices with their start and end apart: 5 -> 39, of which waited for: 3 -> 18; matrix products, arithmetic and copies ran while one was open for 17% -> 17% of each run, Pallas kernels for 0% -> 0%
where the time goes in v1:
time: 199 us
  waiting for transfers between devices  90.9 us (46%)
  starting transfers between devices  69.3 us (35%)
  matrix products  32.2 us (16%)
  local copies, waits for them, and re-layouts  2.37 us (1%)
  between operations  2.32 us (1%)
    ppermute x39, waiting for transfers between devices, flip(): lax.ppermute(block, axis, [(i, i ^ shift) for i in range(lax.axis_size(ax...  90.9 us
    ppermute x39, starting transfers between devices, flip(): lax.ppermute(block, axis, [(i, i ^ shift) for i in range(lax.axis_size(ax...  69.3 us
    dot_general x9, matrix products, by_rows(): lax.dot_general(left, right, (((0,), (0,)), ((), ())), preferred_element_...  13.5 us
    dot_general x9, matrix products, by_columns(): lax.dot_general(left, right, (((1,), (1,)), ((), ())), preferred_element_...  8.37 us
  transfers between devices with their start and end apart: 39, of which 18 were waited for; matrix products, arithmetic and copies ran while one was open for 17% of the time, Pallas kernels for 0%

profile of v1, /device:TPU:0, one launch (start us, length us, event | category | flops | bytes accessed | tf_op | source)
XLA Modules:
  0.0 198.8 jit_solution(10293808825238470614)
XLA Ops:
  0.7 3.0 %collective-permute-start.1 = (bf16[128,2048]{1,0:T(8,128)(2,1)}, bf16[128,2048]{1,0:T(8,128)(2,1)S(1)}, u32[]{:S(2)}, u32[]{:S(2)}) collective-permute-start(bf16[128,2048]{1,0:T(8,128)(2,1)} %param.13), channel_id=1, source_target_pairs={{0,2},{1,3},{2,0},{3,1},{4,6},{5,7},{6,4},{7,5},{8,10},{9,11},{10,... | collective-permute-start | bytes 1572872 | tf_op jit(solution)/shard_map/ppermute | solution.py:13
  12.4 2.6 %collective-permute-start.21 = (bf16[40,2048]{1,0:T(8,128)(2,1)S(1)}, bf16[40,2048]{1,0:T(8,128)(2,1)S(1)}, u32[]{:S(2)}, u32[]{:S(2)}) collective-permute-start(bf16[40,2048]{1,0:T(8,128)(2,1)S(1)} %get-tuple-element.40), channel_id=1, source_target_pairs={{0,16},{4,20},{8,24},{12,28},{16,0},{20,4},{24,8},{28,12},{1,17},{... | collective-permute-start | bytes 491528 | tf_op jit(solution)/shard_map/ppermute | solution.py:13
  16.9 2.6 %collective-permute-done.10 = bf16[40,2048]{1,0:T(8,128)(2,1)S(1)} collective-permute-done((bf16[40,2048]{1,0:T(8,128)(2,1)S(1)}, bf16[40,2048]{1,0:T(8,128)(2,1)S(1)}, u32[]{:S(2)}, u32[]{:S(2)}) %collective-permute-start.10) | collective-permute-done | bytes 163872 | tf_op jit(solution)/shard_map/ppermute | solution.py:13
  19.9 6.8 %collective-permute-done.21 = bf16[40,2048]{1,0:T(8,128)(2,1)S(1)} collective-permute-done((bf16[40,2048]{1,0:T(8,128)(2,1)S(1)}, bf16[40,2048]{1,0:T(8,128)(2,1)S(1)}, u32[]{:S(2)}, u32[]{:S(2)}) %collective-permute-start.21) | collective-permute-done | bytes 163872 | tf_op jit(solution)/shard_map/ppermute | solution.py:13
  26.7 4.0 %collective-permute-start.30 = (bf16[40,2048]{1,0:T(8,128)(2,1)S(1)}, bf16[40,2048]{1,0:T(8,128)(2,1)S(1)}, u32[]{:S(2)}, u32[]{:S(2)}) collective-permute-start(bf16[40,2048]{1,0:T(8,128)(2,1)S(1)} %get-tuple-element.46), channel_id=1, source_target_pairs={{0,24},{4,28},{8,16},{12,20},{16,8},{20,12},{24,0},{28,4},{1,25},{... | collective-permute-start | bytes 491528 | tf_op jit(solution)/shard_map/ppermute | solution.py:13
  30.7 2.8 %collective-permute-done.22 = bf16[40,2048]{1,0:T(8,128)(2,1)S(1)} collective-permute-done((bf16[40,2048]{1,0:T(8,128)(2,1)S(1)}, bf16[40,2048]{1,0:T(8,128)(2,1)S(1)}, u32[]{:S(2)}, u32[]{:S(2)}) %collective-permute-start.22) | collective-permute-done | bytes 163872 | tf_op jit(solution)/shard_map/ppermute | solution.py:13
  33.5 3.4 %collective-permute-start.31 = (bf16[40,2048]{1,0:T(8,128)(2,1)S(1)}, bf16[40,2048]{1,0:T(8,128)(2,1)S(1)}, u32[]{:S(2)}, u32[]{:S(2)}) collective-permute-start(bf16[40,2048]{1,0:T(8,128)(2,1)S(1)} %get-tuple-element.45), channel_id=1, source_target_pairs={{0,28},{4,24},{8,20},{12,16},{16,12},{20,8},{24,4},{28,0},{1,29},{... | collective-permute-start | bytes 491528 | tf_op jit(solution)/shard_map/ppermute | solution.py:13
  37.0 4.6 %collective-permute-done.31 = bf16[40,2048]{1,0:T(8,128)(2,1)S(1)} collective-permute-done((bf16[40,2048]{1,0:T(8,128)(2,1)S(1)}, bf16[40,2048]{1,0:T(8,128)(2,1)S(1)}, u32[]{:S(2)}, u32[]{:S(2)}) %collective-permute-start.31) | collective-permute-done | bytes 163872 | tf_op jit(solution)/shard_map/ppermute | solution.py:13
  42.4 9.4 %collective-permute-done.23 = bf16[80,2048]{1,0:T(8,128)(2,1)S(1)} collective-permute-done((bf16[80,2048]{1,0:T(8,128)(2,1)S(1)}, bf16[80,2048]{1,0:T(8,128)(2,1)S(1)}, u32[]{:S(2)}, u32[]{:S(2)}) %collective-permute-start.23) | collective-permute-done | bytes 327712 | tf_op jit(solution)/shard_map/ppermute | solution.py:13
  52.5 8.7 %collective-permute-done.32 = bf16[80,2048]{1,0:T(8,128)(2,1)S(1)} collective-permute-done((bf16[80,2048]{1,0:T(8,128)(2,1)S(1)}, bf16[80,2048]{1,0:T(8,128)(2,1)S(1)}, u32[]{:S(2)}, u32[]{:S(2)}) %collective-permute-start.32) | collective-permute-done | bytes 327712 | tf_op jit(solution)/shard_map/ppermute | solution.py:13
  63.4 4.4 %collective-permute-start.4 = (bf16[40,2048]{1,0:T(8,128)(2,1)S(1)}, bf16[40,2048]{1,0:T(8,128)(2,1)S(1)}, u32[]{:S(2)}, u32[]{:S(2)}) collective-permute-start(bf16[40,2048]{1,0:T(8,128)(2,1)S(1)} %get-tuple-element.18), channel_id=1, source_target_pairs={{0,8},{4,12},{8,0},{12,4},{16,24},{20,28},{24,16},{28,20},{1,9},{5... | collective-permute-start | bytes 491528 | tf_op jit(solution)/shard_map/ppermute | solution.py:13
  70.0 3.4 %collective-permute-start.5 = (bf16[40,2048]{1,0:T(8,128)(2,1)S(1)}, bf16[40,2048]{1,0:T(8,128)(2,1)S(1)}, u32[]{:S(2)}, u32[]{:S(2)}) collective-permute-start(bf16[40,2048]{1,0:T(8,128)(2,1)S(1)} %get-tuple-element.17), channel_id=1, source_target_pairs={{0,12},{4,8},{8,4},{12,0},{16,28},{20,24},{24,20},{28,16},{1,13},{... | collective-permute-start | bytes 491528 | tf_op jit(solution)/shard_map/ppermute | solution.py:13
  73.4 2.6 %collective-permute-start.18 = (bf16[40,2048]{1,0:T(8,128)(2,1)S(1)}, bf16[40,2048]{1,0:T(8,128)(2,1)S(1)}, u32[]{:S(2)}, u32[]{:S(2)}) collective-permute-start(bf16[40,2048]{1,0:T(8,128)(2,1)S(1)} %get-tuple-element.41), channel_id=1, source_target_pairs={{0,16},{4,20},{8,24},{12,28},{16,0},{20,4},{24,8},{28,12},{1,17},{... | collective-permute-start | bytes 491528 | tf_op jit(solution)/shard_map/ppermute | solution.py:13
  77.0 6.7 %collective-permute-start.19 = (bf16[40,2048]{1,0:T(8,128)(2,1)S(1)}, bf16[40,2048]{1,0:T(8,128)(2,1)S(1)}, u32[]{:S(2)}, u32[]{:S(2)}) collective-permute-start(bf16[40,2048]{1,0:T(8,128)(2,1)S(1)} %get-tuple-element.42), channel_id=1, source_target_pairs={{0,20},{4,16},{8,28},{12,24},{16,4},{20,0},{24,12},{28,8},{1,21},{... | collective-permute-start | bytes 491528 | tf_op jit(solution)/shard_map/ppermute | solution.py:13
  83.8 7.4 %collective-permute-start.27 = (bf16[40,2048]{1,0:T(8,128)(2,1)S(1)}, bf16[40,2048]{1,0:T(8,128)(2,1)S(1)}, u32[]{:S(2)}, u32[]{:S(2)}) collective-permute-start(bf16[40,2048]{1,0:T(8,128)(2,1)S(1)} %get-tuple-element.47), channel_id=1, source_target_pairs={{0,24},{4,28},{8,16},{12,20},{16,8},{20,12},{24,0},{28,4},{1,25},{... | collective-permute-start | bytes 491528 | tf_op jit(solution)/shard_map/ppermute | solution.py:13
  91.2 2.1 %collective-permute-done.19 = bf16[40,2048]{1,0:T(8,128)(2,1)S(1)} collective-permute-done((bf16[40,2048]{1,0:T(8,128)(2,1)S(1)}, bf16[40,2048]{1,0:T(8,128)(2,1)S(1)}, u32[]{:S(2)}, u32[]{:S(2)}) %collective-permute-start.19) | collective-permute-done | bytes 163872 | tf_op jit(solution)/shard_map/ppermute | solution.py:13
  93.3 4.1 %collective-permute-start.28 = (bf16[40,2048]{1,0:T(8,128)(2,1)S(1)}, bf16[40,2048]{1,0:T(8,128)(2,1)S(1)}, u32[]{:S(2)}, u32[]{:S(2)}) collective-permute-start(bf16[40,2048]{1,0:T(8,128)(2,1)S(1)} %get-tuple-element.48), channel_id=1, source_target_pairs={{0,28},{4,24},{8,20},{12,16},{16,12},{20,8},{24,4},{28,0},{1,29},{... | collective-permute-start | bytes 491528 | tf_op jit(solution)/shard_map/ppermute | solution.py:13
  98.3 3.8 %collective-permute-done.28 = bf16[40,2048]{1,0:T(8,128)(2,1)S(1)} collective-permute-done((bf16[40,2048]{1,0:T(8,128)(2,1)S(1)}, bf16[40,2048]{1,0:T(8,128)(2,1)S(1)}, u32[]{:S(2)}, u32[]{:S(2)}) %collective-permute-start.28) | collective-permute-done | bytes 163872 | tf_op jit(solution)/shard_map/ppermute | solution.py:13
  102.2 2.5 %collective-permute-start.20 = (bf16[80,2048]{1,0:T(8,128)(2,1)S(1)}, bf16[80,2048]{1,0:T(8,128)(2,1)S(1)}, u32[]{:S(2)}, u32[]{:S(2)}) collective-permute-start(bf16[80,2048]{1,0:T(8,128)(2,1)S(1)} %pad_maximum_fusion.11), channel_id=1, source_target_pairs={{0,2},{1,3},{2,0},{3,1},{4,6},{5,7},{6,4},{7,5},{8,10},{9,11},{10,... | collective-permute-start | bytes 983048 | tf_op jit(solution)/shard_map/ppermute | solution.py:13
  108.1 14.1 %collective-permute-done.20 = bf16[80,2048]{1,0:T(8,128)(2,1)S(1)} collective-permute-done((bf16[80,2048]{1,0:T(8,128)(2,1)S(1)}, bf16[80,2048]{1,0:T(8,128)(2,1)S(1)}, u32[]{:S(2)}, u32[]{:S(2)}) %collective-permute-start.20) | collective-permute-done | bytes 327712 | tf_op jit(solution)/shard_map/ppermute | solution.py:13
  126.7 2.6 %collective-permute-done.29 = bf16[80,2048]{1,0:T(8,128)(2,1)S(1)} collective-permute-done((bf16[80,2048]{1,0:T(8,128)(2,1)S(1)}, bf16[80,2048]{1,0:T(8,128)(2,1)S(1)}, u32[]{:S(2)}, u32[]{:S(2)}) %collective-permute-start.29) | collective-permute-done | bytes 327712 | tf_op jit(solution)/shard_map/ppermute | solution.py:13
  133.9 2.6 %collective-permute-done.24 = bf16[80,2048]{1,0:T(8,128)(2,1)S(1)} collective-permute-done((bf16[80,2048]{1,0:T(8,128)(2,1)S(1)}, bf16[80,2048]{1,0:T(8,128)(2,1)S(1)}, u32[]{:S(2)}, u32[]{:S(2)}) %collective-permute-start.24) | collective-permute-done | bytes 327712 | tf_op jit(solution)/shard_map/ppermute | solution.py:13
  136.6 4.5 %collective-permute-start.25 = (bf16[40,2048]{1,0:T(8,128)(2,1)S(1)}, bf16[40,2048]{1,0:T(8,128)(2,1)S(1)}, u32[]{:S(2)}, u32[]{:S(2)}) collective-permute-start(bf16[40,2048]{1,0:T(8,128)(2,1)S(1)} %get-tuple-element.37), channel_id=1, source_target_pairs={{0,16},{4,20},{8,24},{12,28},{16,0},{20,4},{24,8},{28,12},{1,17},{... | collective-permute-start | bytes 491528 | tf_op jit(solution)/shard_map/ppermute | solution.py:13
  141.4 3.1 %collective-permute-start.34 = (bf16[40,2048]{1,0:T(8,128)(2,1)S(1)}, bf16[40,2048]{1,0:T(8,128)(2,1)S(1)}, u32[]{:S(2)}, u32[]{:S(2)}) collective-permute-start(bf16[40,2048]{1,0:T(8,128)(2,1)S(1)} %get-tuple-element.43), channel_id=1, source_target_pairs={{0,24},{4,28},{8,16},{12,20},{16,8},{20,12},{24,0},{28,4},{1,25},{... | collective-permute-start | bytes 491528 | tf_op jit(solution)/shard_map/ppermute | solution.py:13
  154.9 14.0 %collective-permute-done.14 = bf16[160,2048]{1,0:T(8,128)(2,1)S(1)} collective-permute-done((bf16[160,2048]{1,0:T(8,128)(2,1)S(1)}, bf16[160,2048]{1,0:T(8,128)(2,1)S(1)}, u32[]{:S(2)}, u32[]{:S(2)}) %collective-permute-start.14) | collective-permute-done | bytes 655392 | tf_op jit(solution)/shard_map/ppermute | solution.py:13
  172.1 6.6 %collective-permute-done.35 = bf16[40,2048]{1,0:T(8,128)(2,1)S(1)} collective-permute-done((bf16[40,2048]{1,0:T(8,128)(2,1)S(1)}, bf16[40,2048]{1,0:T(8,128)(2,1)S(1)}, u32[]{:S(2)}, u32[]{:S(2)}) %collective-permute-start.35) | collective-permute-done | bytes 163872 | tf_op jit(solution)/shard_map/ppermute | solution.py:13
  178.7 4.0 %collective-permute-start.16 = (bf16[40,2048]{1,0:T(8,128)(2,1)S(1)}, bf16[40,2048]{1,0:T(8,128)(2,1)S(1)}, u32[]{:S(2)}, u32[]{:S(2)}) collective-permute-start(bf16[40,2048]{1,0:T(8,128)(2,1)S(1)} %get-tuple-element.31), channel_id=1, source_target_pairs={{0,8},{4,12},{8,0},{12,4},{16,24},{20,28},{24,16},{28,20},{1,9},{5... | collective-permute-start | bytes 491528 | tf_op jit(solution)/shard_map/ppermute | solution.py:13
  183.8 4.0 %collective-permute-done.16 = bf16[40,2048]{1,0:T(8,128)(2,1)S(1)} collective-permute-done((bf16[40,2048]{1,0:T(8,128)(2,1)S(1)}, bf16[40,2048]{1,0:T(8,128)(2,1)S(1)}, u32[]{:S(2)}, u32[]{:S(2)}) %collective-permute-start.16) | collective-permute-done | bytes 163872 | tf_op jit(solution)/shard_map/ppermute | solution.py:13
  187.7 2.4 %collective-permute-done.17 = bf16[40,2048]{1,0:T(8,128)(2,1)S(1)} collective-permute-done((bf16[40,2048]{1,0:T(8,128)(2,1)S(1)}, bf16[40,2048]{1,0:T(8,128)(2,1)S(1)}, u32[]{:S(2)}, u32[]{:S(2)}) %collective-permute-start.17) | collective-permute-done | bytes 163872 | tf_op jit(solution)/shard_map/ppermute | solution.py:13
  191.3 2.6 %fusion.3 = bf16[1,352,2048]{2,1,0:T(8,128)(2,1)} fusion(bf16[352,2048]{1,0:T(8,128)(2,1)S(1)} %collective-permute-done.38, bf16[640,2048]{1,0:T(8,128)(2,1)S(1)} %constant_dynamic-update-slice_fusion.27, bf16[640,704]{1,0:T(8,128)(2,1)S(1)} %pad_maximum_fusion.5), kind=kOutput, calls=%fused_computation.13 | convolution fusion | flops 924909568 | bytes 5996544 | tf_op jit(solution)/shard_map/dot_general | solution.py:21
  193.9 2.4 %fusion.4 = bf16[1,2048,352]{1,2,0:T(8,128)(2,1)} fusion(bf16[2048,352]{0,1:T(8,128)(2,1)S(1)} %collective-permute-done.37, bf16[640,2048]{1,0:T(8,128)(2,1)S(1)} %get-tuple-element.33, bf16[640,704]{1,0:T(8,128)(2,1)S(1)} %pad_maximum_fusion.4), kind=kOutput, calls=%fused_computation.14 | convolution fusion | flops 924909568 | bytes 5996544 | tf_op jit(solution)/shard_map/dot_general | solution.py:21
  196.4 2.4 %fusion.5 = bf16[1,2048,352]{1,2,0:T(8,128)(2,1)} fusion(bf16[2048,352]{0,1:T(8,128)(2,1)S(1)} %collective-permute-done.36, bf16[640,2048]{1,0:T(8,128)(2,1)S(1)} %get-tuple-element.33, bf16[640,704]{1,0:T(8,128)(2,1)S(1)} %pad_maximum_fusion.3), kind=kOutput, calls=%fused_computation.15 | convolution fusion | flops 924909568 | bytes 5996544 | tf_op jit(solution)/shard_map/dot_general | solution.py:21
  (160 shorter events, 46.3 us)
Async XLA Ops:
  0.7 51.7 %collective-permute-start.1 = (bf16[128,2048]{1,0:T(8,128)(2,1)}, bf16[128,2048]{1,0:T(8,128)(2,1)S(1)}, u32[]{:S(2)}, u32[]{:S(2)}) collective-permute-start(bf16[128,2048]{1,0:T(8,128)(2,1)} %param.13), channel_id=1, source_target_pairs={{0,2},{1,3},{2,0},{3,1},{4,6},{5,7},{6,4},{7,5},{8,10},{9,11},{10,... | collective-permute-start | bytes 1572872 | tf_op jit(solution)/shard_map/ppermute | solution.py:13
  3.7 57.5 %collective-permute-start = (bf16[128,2048]{1,0:T(8,128)(2,1)}, bf16[128,2048]{1,0:T(8,128)(2,1)}, u32[]{:S(2)}, u32[]{:S(2)}) collective-permute-start(bf16[128,2048]{1,0:T(8,128)(2,1)} %param.13), channel_id=1, source_target_pairs={{0,1},{1,0},{2,3},{3,2},{4,5},{5,4},{6,7},{7,6},{8,9},{9,8},{10,11... | collective-permute-start | bytes 1572872 | tf_op jit(solution)/shard_map/ppermute | solution.py:13
  8.9 10.6 %collective-permute-start.10 = (bf16[40,2048]{1,0:T(8,128)(2,1)S(1)}, bf16[40,2048]{1,0:T(8,128)(2,1)S(1)}, u32[]{:S(2)}, u32[]{:S(2)}) collective-permute-start(bf16[40,2048]{1,0:T(8,128)(2,1)S(1)} %get-tuple-element.25), channel_id=1, source_target_pairs={{0,12},{4,8},{8,4},{12,0},{16,28},{20,24},{24,20},{28,16},{1,13},{... | collective-permute-start | bytes 491528 | tf_op jit(solution)/shard_map/ppermute | solution.py:13
  12.4 14.3 %collective-permute-start.21 = (bf16[40,2048]{1,0:T(8,128)(2,1)S(1)}, bf16[40,2048]{1,0:T(8,128)(2,1)S(1)}, u32[]{:S(2)}, u32[]{:S(2)}) collective-permute-start(bf16[40,2048]{1,0:T(8,128)(2,1)S(1)} %get-tuple-element.40), channel_id=1, source_target_pairs={{0,16},{4,20},{8,24},{12,28},{16,0},{20,4},{24,8},{28,12},{1,17},{... | collective-permute-start | bytes 491528 | tf_op jit(solution)/shard_map/ppermute | solution.py:13
  15.0 18.5 %collective-permute-start.22 = (bf16[40,2048]{1,0:T(8,128)(2,1)S(1)}, bf16[40,2048]{1,0:T(8,128)(2,1)S(1)}, u32[]{:S(2)}, u32[]{:S(2)}) collective-permute-start(bf16[40,2048]{1,0:T(8,128)(2,1)S(1)} %get-tuple-element.39), channel_id=1, source_target_pairs={{0,20},{4,16},{8,28},{12,24},{16,4},{20,0},{24,12},{28,8},{1,21},{... | collective-permute-start | bytes 491528 | tf_op jit(solution)/shard_map/ppermute | solution.py:13
  19.5 22.1 %collective-permute-start.11 = (bf16[160,2048]{1,0:T(8,128)(2,1)S(1)}, bf16[160,2048]{1,0:T(8,128)(2,1)S(1)}, u32[]{:S(2)}, u32[]{:S(2)}) collective-permute-start(bf16[160,2048]{1,0:T(8,128)(2,1)S(1)} %pad_maximum_fusion.10), channel_id=1, source_target_pairs={{0,2},{1,3},{2,0},{3,1},{4,6},{5,7},{6,4},{7,5},{8,10},{9,11},{10,... | collective-permute-start | bytes 1966088 | tf_op jit(solution)/shard_map/ppermute | solution.py:13
  26.7 10.2 %collective-permute-start.30 = (bf16[40,2048]{1,0:T(8,128)(2,1)S(1)}, bf16[40,2048]{1,0:T(8,128)(2,1)S(1)}, u32[]{:S(2)}, u32[]{:S(2)}) collective-permute-start(bf16[40,2048]{1,0:T(8,128)(2,1)S(1)} %get-tuple-element.46), channel_id=1, source_target_pairs={{0,24},{4,28},{8,16},{12,20},{16,8},{20,12},{24,0},{28,4},{1,25},{... | collective-permute-start | bytes 491528 | tf_op jit(solution)/shard_map/ppermute | solution.py:13
  36.9 71.1 %collective-permute-start.7 = (bf16[352,2048]{1,0:T(8,128)(2,1)}, bf16[352,2048]{1,0:T(8,128)(2,1)S(1)}, u32[]{:S(2)}, u32[]{:S(2)}) collective-permute-start(bf16[352,2048]{1,0:T(8,128)(2,1)} %bitcast.80), channel_id=1, source_target_pairs={{0,1},{1,0},{2,3},{3,2},{4,5},{5,4},{6,7},{7,6},{8,9},{9,8},{10,11... | collective-permute-start | bytes 4325384 | tf_op jit(solution)/shard_map/ppermute | solution.py:13
  41.6 63.1 %collective-permute-start.13 = (bf16[2048,352]{0,1:T(8,128)(2,1)S(1)}, bf16[2048,352]{0,1:T(8,128)(2,1)S(1)}, u32[]{:S(2)}, u32[]{:S(2)}) collective-permute-start(bf16[2048,352]{0,1:T(8,128)(2,1)S(1)} %bitcast.62), channel_id=1, source_target_pairs={{0,1},{1,0},{2,3},{3,2},{4,5},{5,4},{6,7},{7,6},{8,9},{9,8},{10,11... | collective-permute-start | bytes 4325384 | tf_op jit(solution)/shard_map/ppermute | solution.py:13
  41.6 10.2 %collective-permute-start.23 = (bf16[80,2048]{1,0:T(8,128)(2,1)S(1)}, bf16[80,2048]{1,0:T(8,128)(2,1)S(1)}, u32[]{:S(2)}, u32[]{:S(2)}) collective-permute-start(bf16[80,2048]{1,0:T(8,128)(2,1)S(1)} %pad_maximum_fusion.12), channel_id=1, source_target_pairs={{0,2},{1,3},{2,0},{3,1},{4,6},{5,7},{6,4},{7,5},{8,10},{9,11},{10,... | collective-permute-start | bytes 983048 | tf_op jit(solution)/shard_map/ppermute | solution.py:13
  51.8 9.3 %collective-permute-start.32 = (bf16[80,2048]{1,0:T(8,128)(2,1)S(1)}, bf16[80,2048]{1,0:T(8,128)(2,1)S(1)}, u32[]{:S(2)}, u32[]{:S(2)}) collective-permute-start(bf16[80,2048]{1,0:T(8,128)(2,1)S(1)} %pad_maximum_fusion.14), channel_id=1, source_target_pairs={{0,2},{1,3},{2,0},{3,1},{4,6},{5,7},{6,4},{7,5},{8,10},{9,11},{10,... | collective-permute-start | bytes 983048 | tf_op jit(solution)/shard_map/ppermute | solution.py:13
  52.3 8.9 %collective-permute-start.2 = (bf16[128,2048]{1,0:T(8,128)(2,1)S(1)}, bf16[128,2048]{1,0:T(8,128)(2,1)S(1)}, u32[]{:S(2)}, u32[]{:S(2)}) collective-permute-start(bf16[128,2048]{1,0:T(8,128)(2,1)S(1)} %collective-permute-done.1), channel_id=1, source_target_pairs={{0,1},{1,0},{2,3},{3,2},{4,5},{5,4},{6,7},{7,6},{8,9},{9,8},{10,11... | collective-permute-start | bytes 1572872 | tf_op jit(solution)/shard_map/ppermute | solution.py:13
  61.2 62.0 %collective-permute-start.12 = (bf16[2048,352]{0,1:T(8,128)(2,1)S(1)}, bf16[2048,352]{0,1:T(8,128)(2,1)S(1)}, u32[]{:S(2)}, u32[]{:S(2)}) collective-permute-start(bf16[2048,352]{0,1:T(8,128)(2,1)S(1)} %bitcast.84), channel_id=1, source_target_pairs={{0,1},{1,0},{2,3},{3,2},{4,5},{5,4},{6,7},{7,6},{8,9},{9,8},{10,11... | collective-permute-start | bytes 4325384 | tf_op jit(solution)/shard_map/ppermute | solution.py:13
  63.4 10.0 %collective-permute-start.4 = (bf16[40,2048]{1,0:T(8,128)(2,1)S(1)}, bf16[40,2048]{1,0:T(8,128)(2,1)S(1)}, u32[]{:S(2)}, u32[]{:S(2)}) collective-permute-start(bf16[40,2048]{1,0:T(8,128)(2,1)S(1)} %get-tuple-element.18), channel_id=1, source_target_pairs={{0,8},{4,12},{8,0},{12,4},{16,24},{20,28},{24,16},{28,20},{1,9},{5... | collective-permute-start | bytes 491528 | tf_op jit(solution)/shard_map/ppermute | solution.py:13
  73.4 10.4 %collective-permute-start.18 = (bf16[40,2048]{1,0:T(8,128)(2,1)S(1)}, bf16[40,2048]{1,0:T(8,128)(2,1)S(1)}, u32[]{:S(2)}, u32[]{:S(2)}) collective-permute-start(bf16[40,2048]{1,0:T(8,128)(2,1)S(1)} %get-tuple-element.41), channel_id=1, source_target_pairs={{0,16},{4,20},{8,24},{12,28},{16,0},{20,4},{24,8},{28,12},{1,17},{... | collective-permute-start | bytes 491528 | tf_op jit(solution)/shard_map/ppermute | solution.py:13
  77.0 16.3 %collective-permute-start.19 = (bf16[40,2048]{1,0:T(8,128)(2,1)S(1)}, bf16[40,2048]{1,0:T(8,128)(2,1)S(1)}, u32[]{:S(2)}, u32[]{:S(2)}) collective-permute-start(bf16[40,2048]{1,0:T(8,128)(2,1)S(1)} %get-tuple-element.42), channel_id=1, source_target_pairs={{0,20},{4,16},{8,28},{12,24},{16,4},{20,0},{24,12},{28,8},{1,21},{... | collective-permute-start | bytes 491528 | tf_op jit(solution)/shard_map/ppermute | solution.py:13
  83.8 13.6 %collective-permute-start.27 = (bf16[40,2048]{1,0:T(8,128)(2,1)S(1)}, bf16[40,2048]{1,0:T(8,128)(2,1)S(1)}, u32[]{:S(2)}, u32[]{:S(2)}) collective-permute-start(bf16[40,2048]{1,0:T(8,128)(2,1)S(1)} %get-tuple-element.47), channel_id=1, source_target_pairs={{0,24},{4,28},{8,16},{12,20},{16,8},{20,12},{24,0},{28,4},{1,25},{... | collective-permute-start | bytes 491528 | tf_op jit(solution)/shard_map/ppermute | solution.py:13
  93.3 8.9 %collective-permute-start.28 = (bf16[40,2048]{1,0:T(8,128)(2,1)S(1)}, bf16[40,2048]{1,0:T(8,128)(2,1)S(1)}, u32[]{:S(2)}, u32[]{:S(2)}) collective-permute-start(bf16[40,2048]{1,0:T(8,128)(2,1)S(1)} %get-tuple-element.48), channel_id=1, source_target_pairs={{0,28},{4,24},{8,20},{12,16},{16,12},{20,8},{24,4},{28,0},{1,29},{... | collective-permute-start | bytes 491528 | tf_op jit(solution)/shard_map/ppermute | solution.py:13
  97.4 47.1 %collective-permute-start.6 = (bf16[160,2048]{1,0:T(8,128)(2,1)S(1)}, bf16[160,2048]{1,0:T(8,128)(2,1)S(1)}, u32[]{:S(2)}, u32[]{:S(2)}) collective-permute-start(bf16[160,2048]{1,0:T(8,128)(2,1)S(1)} %pad_maximum_fusion.9), channel_id=1, source_target_pairs={{0,2},{1,3},{2,0},{3,1},{4,6},{5,7},{6,4},{7,5},{8,10},{9,11},{10,... | collective-permute-start | bytes 1966088 | tf_op jit(solution)/shard_map/ppermute | solution.py:13
  102.2 20.0 %collective-permute-start.20 = (bf16[80,2048]{1,0:T(8,128)(2,1)S(1)}, bf16[80,2048]{1,0:T(8,128)(2,1)S(1)}, u32[]{:S(2)}, u32[]{:S(2)}) collective-permute-start(bf16[80,2048]{1,0:T(8,128)(2,1)S(1)} %pad_maximum_fusion.11), channel_id=1, source_target_pairs={{0,2},{1,3},{2,0},{3,1},{4,6},{5,7},{6,4},{7,5},{8,10},{9,11},{10,... | collective-permute-start | bytes 983048 | tf_op jit(solution)/shard_map/ppermute | solution.py:13
  104.7 24.5 %collective-permute-start.29 = (bf16[80,2048]{1,0:T(8,128)(2,1)S(1)}, bf16[80,2048]{1,0:T(8,128)(2,1)S(1)}, u32[]{:S(2)}, u32[]{:S(2)}) collective-permute-start(bf16[80,2048]{1,0:T(8,128)(2,1)S(1)} %pad_maximum_fusion.13), channel_id=1, source_target_pairs={{0,2},{1,3},{2,0},{3,1},{4,6},{5,7},{6,4},{7,5},{8,10},{9,11},{10,... | collective-permute-start | bytes 983048 | tf_op jit(solution)/shard_map/ppermute | solution.py:13
  125.7 10.7 %collective-permute-start.24 = (bf16[80,2048]{1,0:T(8,128)(2,1)S(1)}, bf16[80,2048]{1,0:T(8,128)(2,1)S(1)}, u32[]{:S(2)}, u32[]{:S(2)}) collective-permute-start(bf16[80,2048]{1,0:T(8,128)(2,1)S(1)} %slice.243), channel_id=1, source_target_pairs={{0,2},{1,3},{2,0},{3,1},{4,6},{5,7},{6,4},{7,5},{8,10},{9,11},{10,... | collective-permute-start | bytes 983048 | tf_op jit(solution)/shard_map/ppermute | solution.py:13
  136.6 32.6 %collective-permute-start.25 = (bf16[40,2048]{1,0:T(8,128)(2,1)S(1)}, bf16[40,2048]{1,0:T(8,128)(2,1)S(1)}, u32[]{:S(2)}, u32[]{:S(2)}) collective-permute-start(bf16[40,2048]{1,0:T(8,128)(2,1)S(1)} %get-tuple-element.37), channel_id=1, source_target_pairs={{0,16},{4,20},{8,24},{12,28},{16,0},{20,4},{24,8},{28,12},{1,17},{... | collective-permute-start | bytes 491528 | tf_op jit(solution)/shard_map/ppermute | solution.py:13
  141.0 30.2 %collective-permute-start.26 = (bf16[40,2048]{1,0:T(8,128)(2,1)S(1)}, bf16[40,2048]{1,0:T(8,128)(2,1)S(1)}, u32[]{:S(2)}, u32[]{:S(2)}) collective-permute-start(bf16[40,2048]{1,0:T(8,128)(2,1)S(1)} %get-tuple-element.38), channel_id=1, source_target_pairs={{0,20},{4,16},{8,28},{12,24},{16,4},{20,0},{24,12},{28,8},{1,21},{... | collective-permute-start | bytes 491528 | tf_op jit(solution)/shard_map/ppermute | solution.py:13
  141.4 30.0 %collective-permute-start.34 = (bf16[40,2048]{1,0:T(8,128)(2,1)S(1)}, bf16[40,2048]{1,0:T(8,128)(2,1)S(1)}, u32[]{:S(2)}, u32[]{:S(2)}) collective-permute-start(bf16[40,2048]{1,0:T(8,128)(2,1)S(1)} %get-tuple-element.43), channel_id=1, source_target_pairs={{0,24},{4,28},{8,16},{12,20},{16,8},{20,12},{24,0},{28,4},{1,25},{... | collective-permute-start | bytes 491528 | tf_op jit(solution)/shard_map/ppermute | solution.py:13
  149.0 42.3 %collective-permute-start.38 = (bf16[352,2048]{1,0:T(8,128)(2,1)S(1)}, bf16[352,2048]{1,0:T(8,128)(2,1)S(1)}, u32[]{:S(2)}, u32[]{:S(2)}) collective-permute-start(bf16[352,2048]{1,0:T(8,128)(2,1)S(1)} %convolution_convert_fusion), channel_id=1, source_target_pairs={{0,1},{1,0},{2,3},{3,2},{4,5},{5,4},{6,7},{7,6},{8,9},{9,8},{10,11... | collective-permute-start | bytes 4325384 | tf_op jit(solution)/shard_map/ppermute | solution.py:13
  151.7 17.2 %collective-permute-start.14 = (bf16[160,2048]{1,0:T(8,128)(2,1)S(1)}, bf16[160,2048]{1,0:T(8,128)(2,1)S(1)}, u32[]{:S(2)}, u32[]{:S(2)}) collective-permute-start(bf16[160,2048]{1,0:T(8,128)(2,1)S(1)} %slice.241), channel_id=1, source_target_pairs={{0,2},{1,3},{2,0},{3,1},{4,6},{5,7},{6,4},{7,5},{8,10},{9,11},{10,... | collective-permute-start | bytes 1966088 | tf_op jit(solution)/shard_map/ppermute | solution.py:13
  168.9 25.0 %collective-permute-start.37 = (bf16[2048,352]{0,1:T(8,128)(2,1)S(1)}, bf16[2048,352]{0,1:T(8,128)(2,1)S(1)}, u32[]{:S(2)}, u32[]{:S(2)}) collective-permute-start(bf16[2048,352]{0,1:T(8,128)(2,1)S(1)} %convolution_convert_fusion.1), channel_id=1, source_target_pairs={{0,1},{1,0},{2,3},{3,2},{4,5},{5,4},{6,7},{7,6},{8,9},{9,8},{10,11... | collective-permute-start | bytes 4325384 | tf_op jit(solution)/shard_map/ppermute | solution.py:13
  169.2 9.5 %collective-permute-start.35 = (bf16[40,2048]{1,0:T(8,128)(2,1)S(1)}, bf16[40,2048]{1,0:T(8,128)(2,1)S(1)}, u32[]{:S(2)}, u32[]{:S(2)}) collective-permute-start(bf16[40,2048]{1,0:T(8,128)(2,1)S(1)} %get-tuple-element.44), channel_id=1, source_target_pairs={{0,28},{4,24},{8,20},{12,16},{16,12},{20,8},{24,4},{28,0},{1,29},{... | collective-permute-start | bytes 491528 | tf_op jit(solution)/shard_map/ppermute | solution.py:13
  171.2 25.1 %collective-permute-start.36 = (bf16[2048,352]{0,1:T(8,128)(2,1)S(1)}, bf16[2048,352]{0,1:T(8,128)(2,1)S(1)}, u32[]{:S(2)}, u32[]{:S(2)}) collective-permute-start(bf16[2048,352]{0,1:T(8,128)(2,1)S(1)} %convolution_convert_fusion.2), channel_id=1, source_target_pairs={{0,1},{1,0},{2,3},{3,2},{4,5},{5,4},{6,7},{7,6},{8,9},{9,8},{10,11... | collective-permute-start | bytes 4325384 | tf_op jit(solution)/shard_map/ppermute | solution.py:13
  171.5 11.3 %collective-permute-start.15 = (bf16[40,2048]{1,0:T(8,128)(2,1)S(1)}, bf16[40,2048]{1,0:T(8,128)(2,1)S(1)}, u32[]{:S(2)}, u32[]{:S(2)}) collective-permute-start(bf16[40,2048]{1,0:T(8,128)(2,1)S(1)} %get-tuple-element.32), channel_id=1, source_target_pairs={{0,4},{4,0},{8,12},{12,8},{16,20},{20,16},{24,28},{28,24},{1,5},{5... | collective-permute-start | bytes 491528 | tf_op jit(solution)/shard_map/ppermute | solution.py:13
  178.7 9.0 %collective-permute-start.16 = (bf16[40,2048]{1,0:T(8,128)(2,1)S(1)}, bf16[40,2048]{1,0:T(8,128)(2,1)S(1)}, u32[]{:S(2)}, u32[]{:S(2)}) collective-permute-start(bf16[40,2048]{1,0:T(8,128)(2,1)S(1)} %get-tuple-element.31), channel_id=1, source_target_pairs={{0,8},{4,12},{8,0},{12,4},{16,24},{20,28},{24,16},{28,20},{1,9},{5... | collective-permute-start | bytes 491528 | tf_op jit(solution)/shard_map/ppermute | solution.py:13
  (21 other events, 231.3 us)

commit v2 on v1

v2 whole, which is shorter than its diff:
```python
import jax
import jax.numpy as jnp
import numpy as np
from jax import lax
from jax.sharding import PartitionSpec as P

F32, BF16 = jnp.float32, jnp.bfloat16


def flip(block, axis, shift, name="rows"):
    with jax.named_scope(name):
        return lax.ppermute(block, axis, [(i, i ^ shift) for i in range(lax.axis_size(axis))])


def by_columns(left, right):
    return lax.dot_general(left, right, (((1,), (1,)), ((), ())), preferred_element_type=F32)


def by_rows(left, right):
    return lax.dot_general(left, right, (((0,), (0,)), ((), ())), preferred_element_type=F32)


def slot_matrices(routes, route_weights, experts, capacity):
    named = routes.T[None] == experts[:, None, None]
    weight = jnp.sum(jnp.where(named, route_weights.T[None].astype(F32), 0.0), axis=1)
    member = jnp.any(named, axis=1)
    tokens = routes.shape[0]
    before = jnp.arange(tokens)[:, None] < jnp.arange(tokens)[None, :]
    earlier = jnp.dot(member.astype(BF16), before.astype(BF16), preferred_element_type=F32)
    slots = jnp.arange(capacity, dtype=F32)[None, :, None]
    filled = member[:, None, :] & (earlier[:, None, :] == slots)
    return filled.astype(BF16), jnp.where(filled, weight[:, None, :], 0.0).astype(BF16)


def after(block, *earlier):
    return lax.optimization_barrier((block, earlier))[0]


def partner_rows(teacher, across, beside, partner):
    tok_rows = teacher.shape[0]
    apart = partner[0] ^ lax.axis_index("dp")
    return jnp.where(
        apart < 2,
        jnp.where(apart == 0, teacher, beside[:tok_rows]),
        jnp.where(apart == 2, across, beside[tok_rows:]),
    )


def spread(matrices, rows):
    return jnp.dot(matrices, rows, preferred_element_type=F32).astype(BF16)


def grad_halves(inputs, grads, kept):
    inputs, grads = jnp.concatenate(inputs, axis=0), jnp.concatenate(grads, axis=0)
    hidden, d_gate, d_up = (jnp.concatenate(parts, axis=0) for parts in zip(*kept))
    quarter = hidden.shape[1] // 2
    own, other = slice(0, quarter), slice(quarter, None)
    side = by_rows(jnp.concatenate([d_gate[:, other], d_up[:, other]], axis=1), inputs).astype(BF16)
    down = by_rows(hidden[:, other], grads).astype(BF16)
    return (
        ((d_gate[:, own], inputs), (d_up[:, own], inputs), (hidden[:, own], grads)),
        jnp.concatenate([side, down], axis=0),
    )


def grad_totals(own, other):
    parts = jnp.split(other, 3, axis=0)
    gate, up, down = ((by_rows(*mine) + part.astype(F32)).astype(BF16) for mine, part in zip(own, parts))
    return gate.T[None], up.T[None], down[None]


def per_device(
    inputs, layer_out, teacher, alignment, routes, route_weights, partner, w_gate, w_up, w_down
):
    tok_rows, features = inputs.shape
    route_count = routes.shape[1]
    expert_count = lax.axis_size("expert")
    capacity = max(2, (5 * tok_rows * route_count + 4 * expert_count - 1) // (4 * expert_count))
    me = lax.axis_index("expert")
    quarter = w_gate.shape[2]
    small = expert_count == 8

    across = flip(teacher, "dp", 2, "teacher_across")

    experts = jnp.arange(expert_count, dtype=jnp.int32)
    filled, weighted = slot_matrices(routes, route_weights, experts ^ me if small else experts, capacity)

    def pick(matrices, shifts):
        return jnp.concatenate([matrices[k] for k in shifts], axis=0)

    def expert_rows(rows, half, grads):
        gate_term = jnp.dot(rows, gate_weight, preferred_element_type=F32)
        up_term = jnp.dot(rows, up_weight, preferred_element_type=F32)
        sigmoid_gate = jax.nn.sigmoid(gate_term)
        activated = gate_term * sigmoid_gate
        hidden = (activated * up_term).astype(BF16)
        d_hidden = by_columns(grads, down_weight)
        d_gate = (d_hidden * up_term * (sigmoid_gate + activated * (1.0 - sigmoid_gate))).astype(BF16)
        d_up = (d_hidden * activated).astype(BF16)
        sums = by_columns(d_gate, gate_weight) + by_columns(d_up, up_weight)
        return (hidden, d_gate, d_up), sums[:half], sums[half:].astype(BF16)

    def both(rows, other):
        return jnp.concatenate([rows, other], axis=0)

    def total(own, other):
        return (own + other.astype(F32)).astype(BF16)

    def join_weights(gate_other, up_other, down_other):
        return (
            jnp.concatenate([w_gate[0], gate_other], axis=1),
            jnp.concatenate([w_up[0], up_other], axis=1),
            jnp.concatenate([w_down[0], down_other], axis=0),
        )

    if small:
        c = capacity

        x_side = flip(spread(pick(filled, (1, 3, 7)), inputs), "expert", 1, "inputs_side")
        x_far = [flip(spread(filled[k], inputs), "expert", k, f"inputs_far_{k}") for k in (4, 5)]
        beside = flip(jnp.concatenate([teacher, across], axis=0), "dp", 1, "teacher_beside")

        x_own, near2, near6 = [spread(after(filled[k], across), inputs) for k in (0, 2, 6)]
        xa = jnp.concatenate([x_own, x_side[:c]] + x_far, axis=0)
        partner_teacher = partner_rows(teacher, across, beside, partner)
        aligned = jnp.dot(alignment, partner_teacher, preferred_element_type=F32)
        cotangent = (layer_out.astype(F32) - aligned).astype(BF16)
        g_send = spread(pick(weighted, (1, 3, 5, 7)), cotangent)
        g_side = flip(g_send, "expert", 1, "grads_side")
        ya = flip(after(xa, g_send), "dp", 2, "inputs_a")
        x_z3 = flip(after(jnp.concatenate([near6, x_side[2 * c :]], axis=0), x_far, g_send), "expert", 6, "inputs_z3")
        x_z1 = flip(after(jnp.concatenate([near2, x_side[c : 2 * c]], axis=0), x_far, g_send), "expert", 2, "inputs_z1")
        g_own, gear2, gear4, gear6 = [spread(weighted[k], cotangent) for k in (0, 2, 4, 6)]
        gate_other = flip(after(w_gate[0], cotangent), "dp", 1, "gate_weight")
        xb = jnp.concatenate([x_z1, x_z3], axis=0)

        yb = flip(after(xb, ya, g_side), "dp", 2, "inputs_b")
        g_z2 = flip(after(jnp.concatenate([gear4, g_side[2 * c : 3 * c]], axis=0), x_z3, x_z1), "expert", 4, "grads_z2")
        g_z1 = flip(after(jnp.concatenate([gear2, g_side[c : 2 * c]], axis=0), x_z3, x_z1), "expert", 2, "grads_z1")
        up_other = flip(after(w_up[0], gate_other, x_z3), "dp", 1, "up_weight")

        ga = jnp.concatenate([g_own, g_side[:c], g_z2], axis=0)
        ha = flip(after(ga, yb), "dp", 2, "grads_a")
        g_z3 = flip(after(jnp.concatenate([gear6, g_side[3 * c :]], axis=0), g_z2), "expert", 6, "grads_z3")
        down_other = flip(after(w_down[0], up_other, yb), "dp", 1, "down_weight")
        gate_weight, up_weight, down_weight = join_weights(gate_other, up_other, down_other)

        gb = jnp.concatenate([g_z1, g_z3], axis=0)
        hb = flip(after(gb, ha, down_other), "dp", 2, "grads_b")
        expert_inputs = [both(xa, ya), both(xb, yb)]
        expert_grads = [both(ga, ha), both(gb, hb)]
        kept, own_sums, other_sums = zip(
            *[expert_rows(r, r.shape[0] // 2, g) for r, g in zip(expert_inputs, expert_grads)]
        )

        sa = flip(after(other_sums[0], hb), "dp", 2, "sums_a")
        ra = total(own_sums[0], sa)

        step = (sa, other_sums[1])
        sb = flip(after(other_sums[1], step), "dp", 2, "sums_b")
        back = {0: ra[:c]}
        for n, k in enumerate((1, 4, 5), 1):
            back[k] = flip(after(ra[n * c : (n + 1) * c], step), "expert", k, f"returned_{k}")
        rb = total(own_sums[1], sb)
        own, other = grad_halves(expert_inputs, expert_grads, after(kept, step))
        step = (sb, back[1], back[4], back[5], other)

        for n, k in enumerate((2, 3, 6, 7)):
            back[k] = flip(after(rb[n * c : (n + 1) * c], step), "expert", k, f"returned_{k}")
        own, other = after((own, other), step)
        grads = grad_totals(own, flip(other, "dp", 1, "weight_grads"))
        grad_inputs = sum(
            by_rows(after(pick(filled, ks), needed), jnp.concatenate([back[k] for k in ks], axis=0))
            for ks, needed in (((0, 1, 4, 5), ()), ((2, 3, 6, 7), grads))
        ).astype(BF16)
    else:
        def exchange(rows):
            got = lax.all_to_all(
                rows.reshape(expert_count, capacity, features), "expert", split_axis=0, concat_axis=0, tiled=True
            )
            return got.reshape(-1, features)

        gate_weight, up_weight, down_weight = join_weights(*(flip(w[0], "dp", 1) for w in (w_gate, w_up, w_down)))
        beside = flip(jnp.concatenate([teacher, across], axis=0), "dp", 1)
        partner_teacher = partner_rows(teacher, across, beside, partner)
        aligned = jnp.dot(alignment, partner_teacher, preferred_element_type=F32)
        cotangent = (layer_out.astype(F32) - aligned).astype(BF16)
        x_rows = exchange(spread(filled.reshape(-1, tok_rows), inputs))
        g_rows = exchange(spread(weighted.reshape(-1, tok_rows), cotangent))
        expert_inputs = [both(x_rows, flip(x_rows, "dp", 2))]
        expert_grads = [both(g_rows, flip(g_rows, "dp", 2))]
        one, own, other = expert_rows(expert_inputs[0], x_rows.shape[0], expert_grads[0])
        kept = [one]
        back = exchange(total(own, flip(other, "dp", 2)))
        grad_inputs = by_rows(filled.reshape(-1, tok_rows), back).astype(BF16)
        own, other = grad_halves(expert_inputs, expert_grads, kept)
        grads = grad_totals(own, flip(other, "dp", 1))
    return grad_inputs, *grads


def solution(mesh):
    tokens = P(("expert", "dp"), None)
    columns, rows = P("expert", None, "dp"), P("expert", "dp", None)
    return jax.shard_map(
        per_device,
        mesh=mesh,
        in_specs=(tokens,) * 6 + (P(("expert", "dp")), columns, columns, rows),
        out_specs=(tokens, columns, columns, rows),
        check_vma=False,
    )
```

time: 199 us -> 157 us (0.79)
  starting transfers between devices: 69.3 us -> 39.3 us
  waiting for transfers between devices: 90.9 us -> 78 us
    ppermute x39 -> x28, starting transfers between devices: 69.3 us -> 39.3 us  [flip(): lax.ppermute(block, axis, [(i, i ^ shift) for i in range(lax.axis_size(ax...]
    ppermute x39 -> x28, waiting for transfers between devices: 90.9 us -> 78 us  [flip(): lax.ppermute(block, axis, [(i, i ^ shift) for i in range(lax.axis_size(ax...]
    dot_general x12 -> x15, matrix products: 8.65 us -> 10.5 us  [the longest x11 5.44 us: spread(): return jnp.dot(matrices, rows, preferred_element_type=F32).astype(BF16)]
    dot_general x9 -> x7, matrix products: 13.5 us -> 12.6 us  [by_rows(): lax.dot_general(left, right, (((0,), (0,)), ((), ())), preferred_element_...]
    dot_general x9 -> x6, matrix products: 8.37 us -> 7.85 us  [by_columns(): lax.dot_general(left, right, (((1,), (1,)), ((), ())), preferred_element_...]
  transfers between devices with their start and end apart: 39 -> 28, of which waited for: 18 -> 17; matrix products, arithmetic and copies ran while one was open for 17% -> 20% of each run, Pallas kernels for 0% -> 0%
where the time goes in v2:
time: 157 us
  waiting for transfers between devices  78 us (50%)
  starting transfers between devices  39.3 us (25%)
  matrix products  31.6 us (20%)
  other arithmetic  3.57 us (2%)
  local copies, waits for them, and re-layouts  2.58 us (2%)
  between operations  1.99 us (1%)
    ppermute x28, waiting for transfers between devices, flip(): lax.ppermute(block, axis, [(i, i ^ shift) for i in range(lax.axis_size(ax...  78 us
    ppermute x28, starting transfers between devices, flip(): lax.ppermute(block, axis, [(i, i ^ shift) for i in range(lax.axis_size(ax...  39.3 us
    dot_general x7, matrix products, by_rows(): lax.dot_general(left, right, (((0,), (0,)), ((), ())), preferred_element_...  12.6 us
    dot_general x6, matrix products, by_columns(): lax.dot_general(left, right, (((1,), (1,)), ((), ())), preferred_element_...  7.85 us
    dot_general x11, matrix products, spread(): return jnp.dot(matrices, rows, preferred_element_type=F32).astype(BF16)  5.44 us
  transfers between devices with their start and end apart: 28, of which 17 were waited for; matrix products, arithmetic and copies ran while one was open for 20% of the time, Pallas kernels for 0%

profile of v2, /device:TPU:0, one launch (start us, length us, event | category | flops | bytes accessed | tf_op | source)
XLA Modules:
  0.0 157.1 jit_solution(9963702458026624557)
XLA Ops:
  2.9 4.0 %collective-permute-start.4 = (bf16[40,2048]{1,0:T(8,128)(2,1)}, bf16[40,2048]{1,0:T(8,128)(2,1)S(1)}, u32[]{:S(2)}, u32[]{:S(2)}) collective-permute-start(bf16[40,2048]{1,0:T(8,128)(2,1)} %convolution_convert_fusion.9), channel_id=1, source_target_pairs={{0,16},{4,20},{8,24},{12,28},{16,0},{20,4},{24,8},{28,12},{1,17},{... | collective-permute-start | bytes 491528 | tf_op jit(solution)/shard_map/inputs_far_4/ppermute | solution.py:12
  10.4 1.8 %collective-permute-start = (bf16[128,2048]{1,0:T(8,128)(2,1)S(1)}, bf16[128,2048]{1,0:T(8,128)(2,1)S(1)}, u32[]{:S(2)}, u32[]{:S(2)}) collective-permute-start(bf16[128,2048]{1,0:T(8,128)(2,1)S(1)} %copy-done.4), channel_id=1, source_target_pairs={{0,2},{1,3},{2,0},{3,1},{4,6},{5,7},{6,4},{7,5},{8,10},{9,11},{10,... | collective-permute-start | bytes 1572872 | tf_op jit(solution)/shard_map/teacher_across/ppermute | solution.py:12
  14.6 8.9 %collective-permute-done = bf16[128,2048]{1,0:T(8,128)(2,1)S(1)} collective-permute-done((bf16[128,2048]{1,0:T(8,128)(2,1)S(1)}, bf16[128,2048]{1,0:T(8,128)(2,1)S(1)}, u32[]{:S(2)}, u32[]{:S(2)}) %collective-permute-start) | collective-permute-done | bytes 524320 | tf_op jit(solution)/shard_map/teacher_across/ppermute | solution.py:12
  23.9 2.4 %collective-permute-done.3 = bf16[120,2048]{1,0:T(8,128)(2,1)S(1)} collective-permute-done((bf16[120,2048]{1,0:T(8,128)(2,1)}, bf16[120,2048]{1,0:T(8,128)(2,1)S(1)}, u32[]{:S(2)}, u32[]{:S(2)}) %collective-permute-start.3) | collective-permute-done | bytes 491552 | tf_op jit(solution)/shard_map/inputs_side/ppermute | solution.py:12
  29.6 1.6 %collective-permute-start.7 = (bf16[80,2048]{1,0:T(8,128)(2,1)S(1)}, bf16[80,2048]{1,0:T(8,128)(2,1)S(1)}, u32[]{:S(2)}, u32[]{:S(2)}) collective-permute-start(bf16[80,2048]{1,0:T(8,128)(2,1)S(1)} %get-tuple-element.45), channel_id=1, source_target_pairs={{0,8},{4,12},{8,0},{12,4},{16,24},{20,28},{24,16},{28,20},{1,9},{5... | collective-permute-start | bytes 983048 | tf_op jit(solution)/shard_map/inputs_z1/ppermute | solution.py:12
  31.2 2.5 %collective-permute-start.6 = (bf16[80,2048]{1,0:T(8,128)(2,1)S(1)}, bf16[80,2048]{1,0:T(8,128)(2,1)S(1)}, u32[]{:S(2)}, u32[]{:S(2)}) collective-permute-start(bf16[80,2048]{1,0:T(8,128)(2,1)S(1)} %get-tuple-element.43), channel_id=1, source_target_pairs={{0,24},{4,28},{8,16},{12,20},{16,8},{20,12},{24,0},{28,4},{1,25},{... | collective-permute-start | bytes 983048 | tf_op jit(solution)/shard_map/inputs_z3/ppermute | solution.py:12
  34.1 1.6 %collective-permute-start.9 = (bf16[160,2048]{1,0:T(8,128)(2,1)S(1)}, bf16[160,2048]{1,0:T(8,128)(2,1)S(1)}, u32[]{:S(2)}, u32[]{:S(2)}) collective-permute-start(bf16[160,2048]{1,0:T(8,128)(2,1)S(1)} %pad_maximum_fusion.9), channel_id=1, source_target_pairs={{0,2},{1,3},{2,0},{3,1},{4,6},{5,7},{6,4},{7,5},{8,10},{9,11},{10,... | collective-permute-start | bytes 1966088 | tf_op jit(solution)/shard_map/inputs_a/ppermute | solution.py:12
  36.2 3.1 %collective-permute-done.7 = bf16[80,2048]{1,0:T(8,128)(2,1)S(1)} collective-permute-done((bf16[80,2048]{1,0:T(8,128)(2,1)S(1)}, bf16[80,2048]{1,0:T(8,128)(2,1)S(1)}, u32[]{:S(2)}, u32[]{:S(2)}) %collective-permute-start.7) | collective-permute-done | bytes 327712 | tf_op jit(solution)/shard_map/inputs_z1/ppermute | solution.py:12
  39.3 8.9 %collective-permute-done.6 = bf16[80,2048]{1,0:T(8,128)(2,1)S(1)} collective-permute-done((bf16[80,2048]{1,0:T(8,128)(2,1)S(1)}, bf16[80,2048]{1,0:T(8,128)(2,1)S(1)}, u32[]{:S(2)}, u32[]{:S(2)}) %collective-permute-start.6) | collective-permute-done | bytes 327712 | tf_op jit(solution)/shard_map/inputs_z3/ppermute | solution.py:12
  48.4 1.8 %collective-permute-start.8 = (bf16[80,2048]{1,0:T(8,128)(2,1)S(1)}, bf16[80,2048]{1,0:T(8,128)(2,1)S(1)}, u32[]{:S(2)}, u32[]{:S(2)}) collective-permute-start(bf16[80,2048]{1,0:T(8,128)(2,1)S(1)} %get-tuple-element.46), channel_id=1, source_target_pairs={{0,16},{4,20},{8,24},{12,28},{16,0},{20,4},{24,8},{28,12},{1,17},{... | collective-permute-start | bytes 983048 | tf_op jit(solution)/shard_map/grads_z2/ppermute | solution.py:12
  51.3 1.5 collective-permute-start.10
  53.2 10.6 %collective-permute-done.8 = bf16[80,2048]{1,0:T(8,128)(2,1)S(1)} collective-permute-done((bf16[80,2048]{1,0:T(8,128)(2,1)S(1)}, bf16[80,2048]{1,0:T(8,128)(2,1)S(1)}, u32[]{:S(2)}, u32[]{:S(2)}) %collective-permute-start.8) | collective-permute-done | bytes 327712 | tf_op jit(solution)/shard_map/grads_z2/ppermute | solution.py:12
  63.8 2.5 %collective-permute-start.16 = (bf16[80,2048]{1,0:T(8,128)(2,1)S(1)}, bf16[80,2048]{1,0:T(8,128)(2,1)S(1)}, u32[]{:S(2)}, u32[]{:S(2)}) collective-permute-start(bf16[80,2048]{1,0:T(8,128)(2,1)S(1)} %pad_maximum_fusion.15), channel_id=1, source_target_pairs={{0,24},{4,28},{8,16},{12,20},{16,8},{20,12},{24,0},{28,4},{1,25},{... | collective-permute-start | bytes 983048 | tf_op jit(solution)/shard_map/grads_z3/ppermute | solution.py:12
  69.1 6.1 %collective-permute-done.16 = bf16[80,2048]{1,0:T(8,128)(2,1)S(1)} collective-permute-done((bf16[80,2048]{1,0:T(8,128)(2,1)S(1)}, bf16[80,2048]{1,0:T(8,128)(2,1)S(1)}, u32[]{:S(2)}, u32[]{:S(2)}) %collective-permute-start.16) | collective-permute-done | bytes 327712 | tf_op jit(solution)/shard_map/grads_z3/ppermute | solution.py:12
  78.1 4.9 %collective-permute-done.11 = bf16[160,2048]{1,0:T(8,128)(2,1)S(1)} collective-permute-done((bf16[160,2048]{1,0:T(8,128)(2,1)S(1)}, bf16[160,2048]{1,0:T(8,128)(2,1)S(1)}, u32[]{:S(2)}, u32[]{:S(2)}) %collective-permute-start.11) | collective-permute-done | bytes 655392 | tf_op jit(solution)/shard_map/grads_a/ppermute | solution.py:12
  85.7 1.6 %collective-permute-start.17 = (bf16[160,2048]{1,0:T(8,128)(2,1)S(1)}, bf16[160,2048]{1,0:T(8,128)(2,1)S(1)}, u32[]{:S(2)}, u32[]{:S(2)}) collective-permute-start(bf16[160,2048]{1,0:T(8,128)(2,1)S(1)} %pad_maximum_fusion.10), channel_id=1, source_target_pairs={{0,2},{1,3},{2,0},{3,1},{4,6},{5,7},{6,4},{7,5},{8,10},{9,11},{10,... | collective-permute-start | bytes 1966088 | tf_op jit(solution)/shard_map/grads_b/ppermute | solution.py:12
  91.3 9.3 %collective-permute-done.17 = bf16[160,2048]{1,0:T(8,128)(2,1)S(1)} collective-permute-done((bf16[160,2048]{1,0:T(8,128)(2,1)S(1)}, bf16[160,2048]{1,0:T(8,128)(2,1)S(1)}, u32[]{:S(2)}, u32[]{:S(2)}) %collective-permute-start.17) | collective-permute-done | bytes 655392 | tf_op jit(solution)/shard_map/grads_b/ppermute | solution.py:12
  106.2 8.1 %collective-permute-done.18 = bf16[160,2048]{1,0:T(8,128)(2,1)S(1)} collective-permute-done((bf16[160,2048]{1,0:T(8,128)(2,1)S(1)}, bf16[160,2048]{1,0:T(8,128)(2,1)S(1)}, u32[]{:S(2)}, u32[]{:S(2)}) %collective-permute-start.18) | collective-permute-done | bytes 655392 | tf_op jit(solution)/shard_map/sums_a/ppermute | solution.py:12
  115.4 3.9 %collective-permute-start.20 = (bf16[40,2048]{1,0:T(8,128)(2,1)S(1)}, bf16[40,2048]{1,0:T(8,128)(2,1)S(1)}, u32[]{:S(2)}, u32[]{:S(2)}) collective-permute-start(bf16[40,2048]{1,0:T(8,128)(2,1)S(1)} %get-tuple-element.59), channel_id=1, source_target_pairs={{0,16},{4,20},{8,24},{12,28},{16,0},{20,4},{24,8},{28,12},{1,17},{... | collective-permute-start | bytes 491528 | tf_op jit(solution)/shard_map/returned_4/ppermute | solution.py:12
  121.1 1.6 %collective-permute-start.22 = (bf16[160,2048]{1,0:T(8,128)(2,1)S(1)}, bf16[160,2048]{1,0:T(8,128)(2,1)S(1)}, u32[]{:S(2)}, u32[]{:S(2)}) collective-permute-start(bf16[160,2048]{1,0:T(8,128)(2,1)S(1)} %slice.278), channel_id=1, source_target_pairs={{0,2},{1,3},{2,0},{3,1},{4,6},{5,7},{6,4},{7,5},{8,10},{9,11},{10,... | collective-permute-start | bytes 1966088 | tf_op jit(solution)/shard_map/sums_b/ppermute | solution.py:12
  124.5 2.6 %convolution_convert_fusion = bf16[704,2048]{1,0:T(8,128)(2,1)S(1)} fusion(bf16[640,2048]{1,0:T(8,128)(2,1)S(1)} %get-tuple-element.72, bf16[640,352]{1,0:T(8,128)(2,1)S(1)} %get-tuple-element.88, bf16[640,352]{1,0:T(8,128)(2,1)S(1)} %get-tuple-element.86), kind=kOutput, calls=%fused_computation.1 | convolution fusion | flops 1848737792 | bytes 6406144 | tf_op jit(solution)/shard_map/dot_general | solution.py:20
  127.7 3.0 %collective-permute-done.20 = bf16[40,2048]{1,0:T(8,128)(2,1)S(1)} collective-permute-done((bf16[40,2048]{1,0:T(8,128)(2,1)S(1)}, bf16[40,2048]{1,0:T(8,128)(2,1)S(1)}, u32[]{:S(2)}, u32[]{:S(2)}) %collective-permute-start.20) | collective-permute-done | bytes 163872 | tf_op jit(solution)/shard_map/returned_4/ppermute | solution.py:12
  130.7 3.5 %collective-permute-done.21 = bf16[40,2048]{1,0:T(8,128)(2,1)S(1)} collective-permute-done((bf16[40,2048]{1,0:T(8,128)(2,1)S(1)}, bf16[40,2048]{1,0:T(8,128)(2,1)S(1)}, u32[]{:S(2)}, u32[]{:S(2)}) %collective-permute-start.21) | collective-permute-done | bytes 163872 | tf_op jit(solution)/shard_map/returned_5/ppermute | solution.py:12
  134.2 1.9 %collective-permute-done.22 = bf16[160,2048]{1,0:T(8,128)(2,1)S(1)} collective-permute-done((bf16[160,2048]{1,0:T(8,128)(2,1)S(1)}, bf16[160,2048]{1,0:T(8,128)(2,1)S(1)}, u32[]{:S(2)}, u32[]{:S(2)}) %collective-permute-start.22) | collective-permute-done | bytes 655392 | tf_op jit(solution)/shard_map/sums_b/ppermute | solution.py:12
  136.3 1.6 %collective-permute-start.24 = (bf16[40,2048]{1,0:T(8,128)(2,1)S(1)}, bf16[40,2048]{1,0:T(8,128)(2,1)S(1)}, u32[]{:S(2)}, u32[]{:S(2)}) collective-permute-start(bf16[40,2048]{1,0:T(8,128)(2,1)S(1)} %get-tuple-element.76), channel_id=1, source_target_pairs={{0,8},{4,12},{8,0},{12,4},{16,24},{20,28},{24,16},{28,20},{1,9},{5... | collective-permute-start | bytes 491528 | tf_op jit(solution)/shard_map/returned_2/ppermute | solution.py:12
  138.4 2.1 %collective-permute-start.26 = (bf16[40,2048]{1,0:T(8,128)(2,1)S(1)}, bf16[40,2048]{1,0:T(8,128)(2,1)S(1)}, u32[]{:S(2)}, u32[]{:S(2)}) collective-permute-start(bf16[40,2048]{1,0:T(8,128)(2,1)S(1)} %get-tuple-element.78), channel_id=1, source_target_pairs={{0,24},{4,28},{8,16},{12,20},{16,8},{20,12},{24,0},{28,4},{1,25},{... | collective-permute-start | bytes 491528 | tf_op jit(solution)/shard_map/returned_6/ppermute | solution.py:12
  140.5 2.6 %collective-permute-start.27 = (bf16[40,2048]{1,0:T(8,128)(2,1)S(1)}, bf16[40,2048]{1,0:T(8,128)(2,1)S(1)}, u32[]{:S(2)}, u32[]{:S(2)}) collective-permute-start(bf16[40,2048]{1,0:T(8,128)(2,1)S(1)} %get-tuple-element.79), channel_id=1, source_target_pairs={{0,28},{4,24},{8,20},{12,16},{16,12},{20,8},{24,4},{28,0},{1,29},{... | collective-permute-start | bytes 491528 | tf_op jit(solution)/shard_map/returned_7/ppermute | solution.py:12
  143.4 2.4 %fusion.3 = bf16[1,352,2048]{2,1,0:T(8,128)(2,1)} fusion(bf16[640,352]{1,0:T(8,128)(2,1)S(1)} %slice.224, bf16[640,2048]{1,0:T(8,128)(2,1)S(1)} %constant_dynamic-update-slice_fusion.22, bf16[1056,2048]{1,0:T(8,128)(2,1)S(1)} %collective-permute-done.23), kind=kOutput, calls=%fused_computation.14 | convolution fusion | flops 924909568 | bytes 5955584 | tf_op jit(solution)/shard_map/dot_general | solution.py:20
  145.8 2.4 %fusion.4 = bf16[1,2048,352]{1,2,0:T(8,128)(2,1)} fusion(bf16[640,352]{1,0:T(8,128)(2,1)S(1)} %get-tuple-element.71, bf16[640,2048]{1,0:T(8,128)(2,1)S(1)} %get-tuple-element.72, bf16[1056,2048]{1,0:T(8,128)(2,1)S(1)} %collective-permute-done.23), kind=kOutput, calls=%fused_computation.15 | convolution fusion | flops 924909568 | bytes 5955584 | tf_op jit(solution)/shard_map/dot_general | solution.py:20
  148.2 2.4 %fusion.5 = bf16[1,2048,352]{1,2,0:T(8,128)(2,1)} fusion(bf16[640,352]{1,0:T(8,128)(2,1)S(1)} %get-tuple-element.68, bf16[640,2048]{1,0:T(8,128)(2,1)S(1)} %get-tuple-element.72, bf16[1056,2048]{1,0:T(8,128)(2,1)S(1)} %collective-permute-done.23), kind=kOutput, calls=%fused_computation.16 | convolution fusion | flops 924909568 | bytes 5955584 | tf_op jit(solution)/shard_map/dot_general | solution.py:20
  150.7 3.0 %collective-permute-done.26 = bf16[40,2048]{1,0:T(8,128)(2,1)S(1)} collective-permute-done((bf16[40,2048]{1,0:T(8,128)(2,1)S(1)}, bf16[40,2048]{1,0:T(8,128)(2,1)S(1)}, u32[]{:S(2)}, u32[]{:S(2)}) %collective-permute-start.26) | collective-permute-done | bytes 163872 | tf_op jit(solution)/shard_map/returned_6/ppermute | solution.py:12
  153.7 2.0 %collective-permute-done.27 = bf16[40,2048]{1,0:T(8,128)(2,1)S(1)} collective-permute-done((bf16[40,2048]{1,0:T(8,128)(2,1)S(1)}, bf16[40,2048]{1,0:T(8,128)(2,1)S(1)}, u32[]{:S(2)}, u32[]{:S(2)}) %collective-permute-start.27) | collective-permute-done | bytes 163872 | tf_op jit(solution)/shard_map/returned_7/ppermute | solution.py:12
  (122 shorter events, 38.9 us)
Async XLA Ops:
  0.6 13.1 %copy-start.5 = (s32[128,2]{0,1:T(2,128)S(1)}, s32[128,2]{0,1:T(2,128)}, u32[]{:S(2)}) copy-start(s32[128,2]{0,1:T(2,128)} %param.14) | copy-start | bytes 3076
  0.7 9.7 %copy-start.4 = (bf16[128,2048]{1,0:T(8,128)(2,1)S(1)}, bf16[128,2048]{1,0:T(8,128)(2,1)}, u32[]{:S(2)}) copy-start(bf16[128,2048]{1,0:T(8,128)(2,1)} %param.12) | copy-start | bytes 1572868
  0.7 12.2 %copy-start.9 = (bf16[128,2]{0,1:T(2,128)(2,1)S(1)}, bf16[128,2]{0,1:T(2,128)(2,1)}, u32[]{:S(2)}) copy-start(bf16[128,2]{0,1:T(2,128)(2,1)} %param.15) | copy-start | bytes 1540
  0.7 12.8 %copy-start.3 = (bf16[128,2048]{1,0:T(8,128)(2,1)S(1)}, bf16[128,2048]{1,0:T(8,128)(2,1)}, u32[]{:S(2)}) copy-start(bf16[128,2048]{1,0:T(8,128)(2,1)} %param.11) | copy-start | bytes 1572868
  2.9 23.5 %collective-permute-start.4 = (bf16[40,2048]{1,0:T(8,128)(2,1)}, bf16[40,2048]{1,0:T(8,128)(2,1)S(1)}, u32[]{:S(2)}, u32[]{:S(2)}) collective-permute-start(bf16[40,2048]{1,0:T(8,128)(2,1)} %convolution_convert_fusion.9), channel_id=1, source_target_pairs={{0,16},{4,20},{8,24},{12,28},{16,0},{20,4},{24,8},{28,12},{1,17},{... | collective-permute-start | bytes 491528 | tf_op jit(solution)/shard_map/inputs_far_4/ppermute | solution.py:12
  7.8 18.6 %collective-permute-start.5 = (bf16[40,2048]{1,0:T(8,128)(2,1)}, bf16[40,2048]{1,0:T(8,128)(2,1)S(1)}, u32[]{:S(2)}, u32[]{:S(2)}) collective-permute-start(bf16[40,2048]{1,0:T(8,128)(2,1)} %convolution_convert_fusion.8), channel_id=1, source_target_pairs={{0,20},{4,16},{8,28},{12,24},{16,4},{20,0},{24,12},{28,8},{1,21},{... | collective-permute-start | bytes 491528 | tf_op jit(solution)/shard_map/inputs_far_5/ppermute | solution.py:12
  10.1 16.1 %collective-permute-start.3 = (bf16[120,2048]{1,0:T(8,128)(2,1)}, bf16[120,2048]{1,0:T(8,128)(2,1)S(1)}, u32[]{:S(2)}, u32[]{:S(2)}) collective-permute-start(bf16[120,2048]{1,0:T(8,128)(2,1)} %convolution_convert_fusion.3), channel_id=1, source_target_pairs={{0,4},{4,0},{8,12},{12,8},{16,20},{20,16},{24,28},{28,24},{1,5},{5... | collective-permute-start | bytes 1474568 | tf_op jit(solution)/shard_map/inputs_side/ppermute | solution.py:12
  10.4 13.1 %collective-permute-start = (bf16[128,2048]{1,0:T(8,128)(2,1)S(1)}, bf16[128,2048]{1,0:T(8,128)(2,1)S(1)}, u32[]{:S(2)}, u32[]{:S(2)}) collective-permute-start(bf16[128,2048]{1,0:T(8,128)(2,1)S(1)} %copy-done.4), channel_id=1, source_target_pairs={{0,2},{1,3},{2,0},{3,1},{4,6},{5,7},{6,4},{7,5},{8,10},{9,11},{10,... | collective-permute-start | bytes 1572872 | tf_op jit(solution)/shard_map/teacher_across/ppermute | solution.py:12
  23.6 3.5 %collective-permute-start.1 = (bf16[256,2048]{1,0:T(8,128)(2,1)S(1)}, bf16[256,2048]{1,0:T(8,128)(2,1)S(1)}, u32[]{:S(2)}, u32[]{:S(2)}) collective-permute-start(bf16[256,2048]{1,0:T(8,128)(2,1)S(1)} %pad_maximum_fusion.6), channel_id=1, source_target_pairs={{0,1},{1,0},{2,3},{3,2},{4,5},{5,4},{6,7},{7,6},{8,9},{9,8},{10,11... | collective-permute-start | bytes 3145736 | tf_op jit(solution)/shard_map/teacher_beside/ppermute | solution.py:12
  28.8 19.4 %collective-permute-start.2 = (bf16[160,2048]{1,0:T(8,128)(2,1)S(1)}, bf16[160,2048]{1,0:T(8,128)(2,1)S(1)}, u32[]{:S(2)}, u32[]{:S(2)}) collective-permute-start(bf16[160,2048]{1,0:T(8,128)(2,1)S(1)} %convolution_convert_fusion.2), channel_id=1, source_target_pairs={{0,4},{4,0},{8,12},{12,8},{16,20},{20,16},{24,28},{28,24},{1,5},{5... | collective-permute-start | bytes 1966088 | tf_op jit(solution)/shard_map/grads_side/ppermute | solution.py:12
  29.6 9.7 %collective-permute-start.7 = (bf16[80,2048]{1,0:T(8,128)(2,1)S(1)}, bf16[80,2048]{1,0:T(8,128)(2,1)S(1)}, u32[]{:S(2)}, u32[]{:S(2)}) collective-permute-start(bf16[80,2048]{1,0:T(8,128)(2,1)S(1)} %get-tuple-element.45), channel_id=1, source_target_pairs={{0,8},{4,12},{8,0},{12,4},{16,24},{20,28},{24,16},{28,20},{1,9},{5... | collective-permute-start | bytes 983048 | tf_op jit(solution)/shard_map/inputs_z1/ppermute | solution.py:12
  31.2 17.0 %collective-permute-start.6 = (bf16[80,2048]{1,0:T(8,128)(2,1)S(1)}, bf16[80,2048]{1,0:T(8,128)(2,1)S(1)}, u32[]{:S(2)}, u32[]{:S(2)}) collective-permute-start(bf16[80,2048]{1,0:T(8,128)(2,1)S(1)} %get-tuple-element.43), channel_id=1, source_target_pairs={{0,24},{4,28},{8,16},{12,20},{16,8},{20,12},{24,0},{28,4},{1,25},{... | collective-permute-start | bytes 983048 | tf_op jit(solution)/shard_map/inputs_z3/ppermute | solution.py:12
  34.1 19.0 %collective-permute-start.12 = (bf16[2048,352]{0,1:T(8,128)(2,1)S(1)}, bf16[2048,352]{0,1:T(8,128)(2,1)S(1)}, u32[]{:S(2)}, u32[]{:S(2)}) collective-permute-start(bf16[2048,352]{0,1:T(8,128)(2,1)S(1)} %bitcast.102), channel_id=1, source_target_pairs={{0,1},{1,0},{2,3},{3,2},{4,5},{5,4},{6,7},{7,6},{8,9},{9,8},{10,11... | collective-permute-start | bytes 4325384 | tf_op jit(solution)/shard_map/gate_weight/ppermute | solution.py:12
  34.1 17.1 %collective-permute-start.9 = (bf16[160,2048]{1,0:T(8,128)(2,1)S(1)}, bf16[160,2048]{1,0:T(8,128)(2,1)S(1)}, u32[]{:S(2)}, u32[]{:S(2)}) collective-permute-start(bf16[160,2048]{1,0:T(8,128)(2,1)S(1)} %pad_maximum_fusion.9), channel_id=1, source_target_pairs={{0,2},{1,3},{2,0},{3,1},{4,6},{5,7},{6,4},{7,5},{8,10},{9,11},{10,... | collective-permute-start | bytes 1966088 | tf_op jit(solution)/shard_map/inputs_a/ppermute | solution.py:12
  48.4 15.3 %collective-permute-start.8 = (bf16[80,2048]{1,0:T(8,128)(2,1)S(1)}, bf16[80,2048]{1,0:T(8,128)(2,1)S(1)}, u32[]{:S(2)}, u32[]{:S(2)}) collective-permute-start(bf16[80,2048]{1,0:T(8,128)(2,1)S(1)} %get-tuple-element.46), channel_id=1, source_target_pairs={{0,16},{4,20},{8,24},{12,28},{16,0},{20,4},{24,8},{28,12},{1,17},{... | collective-permute-start | bytes 983048 | tf_op jit(solution)/shard_map/grads_z2/ppermute | solution.py:12
  50.2 18.9 %collective-permute-start.15 = (bf16[80,2048]{1,0:T(8,128)(2,1)S(1)}, bf16[80,2048]{1,0:T(8,128)(2,1)S(1)}, u32[]{:S(2)}, u32[]{:S(2)}) collective-permute-start(bf16[80,2048]{1,0:T(8,128)(2,1)S(1)} %get-tuple-element.54), channel_id=1, source_target_pairs={{0,8},{4,12},{8,0},{12,4},{16,24},{20,28},{24,16},{28,20},{1,9},{5... | collective-permute-start | bytes 983048 | tf_op jit(solution)/shard_map/grads_z1/ppermute | solution.py:12
  51.3 16.3 %collective-permute-start.10 = (bf16[160,2048]{1,0:T(8,128)(2,1)S(1)}, bf16[160,2048]{1,0:T(8,128)(2,1)S(1)}, u32[]{:S(2)}, u32[]{:S(2)}) collective-permute-start(bf16[160,2048]{1,0:T(8,128)(2,1)S(1)} %pad_maximum_fusion.8), channel_id=1, source_target_pairs={{0,2},{1,3},{2,0},{3,1},{4,6},{5,7},{6,4},{7,5},{8,10},{9,11},{10,... | collective-permute-start | bytes 1966088 | tf_op jit(solution)/shard_map/inputs_b/ppermute | solution.py:12
  53.1 23.5 %collective-permute-start.13 = (bf16[2048,352]{0,1:T(8,128)(2,1)S(1)}, bf16[2048,352]{0,1:T(8,128)(2,1)S(1)}, u32[]{:S(2)}, u32[]{:S(2)}) collective-permute-start(bf16[2048,352]{0,1:T(8,128)(2,1)S(1)} %bitcast.112), channel_id=1, source_target_pairs={{0,1},{1,0},{2,3},{3,2},{4,5},{5,4},{6,7},{7,6},{8,9},{9,8},{10,11... | collective-permute-start | bytes 4325384 | tf_op jit(solution)/shard_map/up_weight/ppermute | solution.py:12
  63.8 11.5 %collective-permute-start.16 = (bf16[80,2048]{1,0:T(8,128)(2,1)S(1)}, bf16[80,2048]{1,0:T(8,128)(2,1)S(1)}, u32[]{:S(2)}, u32[]{:S(2)}) collective-permute-start(bf16[80,2048]{1,0:T(8,128)(2,1)S(1)} %pad_maximum_fusion.15), channel_id=1, source_target_pairs={{0,24},{4,28},{8,16},{12,20},{16,8},{20,12},{24,0},{28,4},{1,25},{... | collective-permute-start | bytes 983048 | tf_op jit(solution)/shard_map/grads_z3/ppermute | solution.py:12
  67.6 15.4 %collective-permute-start.11 = (bf16[160,2048]{1,0:T(8,128)(2,1)S(1)}, bf16[160,2048]{1,0:T(8,128)(2,1)S(1)}, u32[]{:S(2)}, u32[]{:S(2)}) collective-permute-start(bf16[160,2048]{1,0:T(8,128)(2,1)S(1)} %pad_maximum_fusion.7), channel_id=1, source_target_pairs={{0,2},{1,3},{2,0},{3,1},{4,6},{5,7},{6,4},{7,5},{8,10},{9,11},{10,... | collective-permute-start | bytes 1966088 | tf_op jit(solution)/shard_map/grads_a/ppermute | solution.py:12
  76.8 8.9 %collective-permute-start.14 = (bf16[352,2048]{1,0:T(8,128)(2,1)S(1)}, bf16[352,2048]{1,0:T(8,128)(2,1)S(1)}, u32[]{:S(2)}, u32[]{:S(2)}) collective-permute-start(bf16[352,2048]{1,0:T(8,128)(2,1)S(1)} %bitcast.109), channel_id=1, source_target_pairs={{0,1},{1,0},{2,3},{3,2},{4,5},{5,4},{6,7},{7,6},{8,9},{9,8},{10,11... | collective-permute-start | bytes 4325384 | tf_op jit(solution)/shard_map/down_weight/ppermute | solution.py:12
  85.7 15.0 %collective-permute-start.17 = (bf16[160,2048]{1,0:T(8,128)(2,1)S(1)}, bf16[160,2048]{1,0:T(8,128)(2,1)S(1)}, u32[]{:S(2)}, u32[]{:S(2)}) collective-permute-start(bf16[160,2048]{1,0:T(8,128)(2,1)S(1)} %pad_maximum_fusion.10), channel_id=1, source_target_pairs={{0,2},{1,3},{2,0},{3,1},{4,6},{5,7},{6,4},{7,5},{8,10},{9,11},{10,... | collective-permute-start | bytes 1966088 | tf_op jit(solution)/shard_map/grads_b/ppermute | solution.py:12
  100.6 13.6 %collective-permute-start.18 = (bf16[160,2048]{1,0:T(8,128)(2,1)S(1)}, bf16[160,2048]{1,0:T(8,128)(2,1)S(1)}, u32[]{:S(2)}, u32[]{:S(2)}) collective-permute-start(bf16[160,2048]{1,0:T(8,128)(2,1)S(1)} %slice.279), channel_id=1, source_target_pairs={{0,2},{1,3},{2,0},{3,1},{4,6},{5,7},{6,4},{7,5},{8,10},{9,11},{10,... | collective-permute-start | bytes 1966088 | tf_op jit(solution)/shard_map/sums_a/ppermute | solution.py:12
  114.4 13.3 %collective-permute-start.19 = (bf16[40,2048]{1,0:T(8,128)(2,1)S(1)}, bf16[40,2048]{1,0:T(8,128)(2,1)S(1)}, u32[]{:S(2)}, u32[]{:S(2)}) collective-permute-start(bf16[40,2048]{1,0:T(8,128)(2,1)S(1)} %get-tuple-element.58), channel_id=1, source_target_pairs={{0,4},{4,0},{8,12},{12,8},{16,20},{20,16},{24,28},{28,24},{1,5},{5... | collective-permute-start | bytes 491528 | tf_op jit(solution)/shard_map/returned_1/ppermute | solution.py:12
  115.4 15.3 %collective-permute-start.20 = (bf16[40,2048]{1,0:T(8,128)(2,1)S(1)}, bf16[40,2048]{1,0:T(8,128)(2,1)S(1)}, u32[]{:S(2)}, u32[]{:S(2)}) collective-permute-start(bf16[40,2048]{1,0:T(8,128)(2,1)S(1)} %get-tuple-element.59), channel_id=1, source_target_pairs={{0,16},{4,20},{8,24},{12,28},{16,0},{20,4},{24,8},{28,12},{1,17},{... | collective-permute-start | bytes 491528 | tf_op jit(solution)/shard_map/returned_4/ppermute | solution.py:12
  119.3 14.8 %collective-permute-start.21 = (bf16[40,2048]{1,0:T(8,128)(2,1)S(1)}, bf16[40,2048]{1,0:T(8,128)(2,1)S(1)}, u32[]{:S(2)}, u32[]{:S(2)}) collective-permute-start(bf16[40,2048]{1,0:T(8,128)(2,1)S(1)} %get-tuple-element.60), channel_id=1, source_target_pairs={{0,20},{4,16},{8,28},{12,24},{16,4},{20,0},{24,12},{28,8},{1,21},{... | collective-permute-start | bytes 491528 | tf_op jit(solution)/shard_map/returned_5/ppermute | solution.py:12
  121.1 15.0 %collective-permute-start.22 = (bf16[160,2048]{1,0:T(8,128)(2,1)S(1)}, bf16[160,2048]{1,0:T(8,128)(2,1)S(1)}, u32[]{:S(2)}, u32[]{:S(2)}) collective-permute-start(bf16[160,2048]{1,0:T(8,128)(2,1)S(1)} %slice.278), channel_id=1, source_target_pairs={{0,2},{1,3},{2,0},{3,1},{4,6},{5,7},{6,4},{7,5},{8,10},{9,11},{10,... | collective-permute-start | bytes 1966088 | tf_op jit(solution)/shard_map/sums_b/ppermute | solution.py:12
  136.1 7.3 %collective-permute-start.23 = (bf16[1056,2048]{1,0:T(8,128)(2,1)S(1)}, bf16[1056,2048]{1,0:T(8,128)(2,1)S(1)}, u32[]{:S(2)}, u32[]{:S(2)}) collective-permute-start(bf16[1056,2048]{1,0:T(8,128)(2,1)S(1)} %pad_maximum_fusion), channel_id=1, source_target_pairs={{0,1},{1,0},{2,3},{3,2},{4,5},{5,4},{6,7},{7,6},{8,9},{9,8},{10,11... | collective-permute-start | bytes 12976136 | tf_op jit(solution)/shard_map/weight_grads/ppermute | solution.py:12
  136.3 14.4 %collective-permute-start.24 = (bf16[40,2048]{1,0:T(8,128)(2,1)S(1)}, bf16[40,2048]{1,0:T(8,128)(2,1)S(1)}, u32[]{:S(2)}, u32[]{:S(2)}) collective-permute-start(bf16[40,2048]{1,0:T(8,128)(2,1)S(1)} %get-tuple-element.76), channel_id=1, source_target_pairs={{0,8},{4,12},{8,0},{12,4},{16,24},{20,28},{24,16},{28,20},{1,9},{5... | collective-permute-start | bytes 491528 | tf_op jit(solution)/shard_map/returned_2/ppermute | solution.py:12
  137.9 12.7 %collective-permute-start.25 = (bf16[40,2048]{1,0:T(8,128)(2,1)S(1)}, bf16[40,2048]{1,0:T(8,128)(2,1)S(1)}, u32[]{:S(2)}, u32[]{:S(2)}) collective-permute-start(bf16[40,2048]{1,0:T(8,128)(2,1)S(1)} %get-tuple-element.77), channel_id=1, source_target_pairs={{0,12},{4,8},{8,4},{12,0},{16,28},{20,24},{24,20},{28,16},{1,13},{... | collective-permute-start | bytes 491528 | tf_op jit(solution)/shard_map/returned_3/ppermute | solution.py:12
  138.4 15.3 %collective-permute-start.26 = (bf16[40,2048]{1,0:T(8,128)(2,1)S(1)}, bf16[40,2048]{1,0:T(8,128)(2,1)S(1)}, u32[]{:S(2)}, u32[]{:S(2)}) collective-permute-start(bf16[40,2048]{1,0:T(8,128)(2,1)S(1)} %get-tuple-element.78), channel_id=1, source_target_pairs={{0,24},{4,28},{8,16},{12,20},{16,8},{20,12},{24,0},{28,4},{1,25},{... | collective-permute-start | bytes 491528 | tf_op jit(solution)/shard_map/returned_6/ppermute | solution.py:12
  140.5 15.2 %collective-permute-start.27 = (bf16[40,2048]{1,0:T(8,128)(2,1)S(1)}, bf16[40,2048]{1,0:T(8,128)(2,1)S(1)}, u32[]{:S(2)}, u32[]{:S(2)}) collective-permute-start(bf16[40,2048]{1,0:T(8,128)(2,1)S(1)} %get-tuple-element.79), channel_id=1, source_target_pairs={{0,28},{4,24},{8,20},{12,16},{16,12},{20,8},{24,4},{28,0},{1,29},{... | collective-permute-start | bytes 491528 | tf_op jit(solution)/shard_map/returned_7/ppermute | solution.py:12
  (6 other events, 24.2 us)

commit v3 on v2

--- a/solution.py
+++ b/solution.py
@@ -20,16 +20,21 @@
     return lax.dot_general(left, right, (((0,), (0,)), ((), ())), preferred_element_type=F32)
 
 
-def slot_matrices(routes, route_weights, experts, capacity):
+def slot_weights(filled, routes, route_weights, experts):
     named = routes.T[None] == experts[:, None, None]
     weight = jnp.sum(jnp.where(named, route_weights.T[None].astype(F32), 0.0), axis=1)
+    return filled * weight[:, None, :].astype(BF16)
+
+
+def slot_matrices(routes, experts, capacity):
+    named = routes.T[None] == experts[:, None, None]
     member = jnp.any(named, axis=1)
     tokens = routes.shape[0]
     before = jnp.arange(tokens)[:, None] < jnp.arange(tokens)[None, :]
     earlier = jnp.dot(member.astype(BF16), before.astype(BF16), preferred_element_type=F32)
     slots = jnp.arange(capacity, dtype=F32)[None, :, None]
     filled = member[:, None, :] & (earlier[:, None, :] == slots)
-    return filled.astype(BF16), jnp.where(filled, weight[:, None, :], 0.0).astype(BF16)
+    return filled.astype(BF16)
 
 
 def after(block, *earlier):
@@ -83,7 +88,9 @@
     across = flip(teacher, "dp", 2, "teacher_across")
 
     experts = jnp.arange(expert_count, dtype=jnp.int32)
-    filled, weighted = slot_matrices(routes, route_weights, experts ^ me if small else experts, capacity)
+    experts = experts ^ me if small else experts
+    filled = slot_matrices(routes, experts, capacity)
+    weighted = slot_weights(filled, routes, after(route_weights, across), experts)
 
     def pick(matrices, shifts):
         return jnp.concatenate([matrices[k] for k in shifts], axis=0)
@@ -116,8 +123,10 @@
     if small:
         c = capacity
 
-        x_side = flip(spread(pick(filled, (1, 3, 7)), inputs), "expert", 1, "inputs_side")
-        x_far = [flip(spread(filled[k], inputs), "expert", k, f"inputs_far_{k}") for k in (4, 5)]
+        sent = [spread(pick(filled, (1, 3, 7)), inputs)] + [spread(filled[k], inputs) for k in (4, 5)]
+        sent = lax.optimization_barrier(sent)
+        x_side = flip(sent[0], "expert", 1, "inputs_side")
+        x_far = [flip(rows, "expert", k, f"inputs_far_{k}") for k, rows in zip((4, 5), sent[1:])]
         beside = flip(jnp.concatenate([teacher, across], axis=0), "dp", 1, "teacher_beside")
 
         x_own, near2, near6 = [spread(after(filled[k], across), inputs) for k in (0, 2, 6)]

time: 157 us -> 153 us (0.975)
  starting transfers between devices: 39.3 us -> 31.6 us
  waiting for transfers between devices: 78 us -> 82.9 us
    ppermute x28, starting transfers between devices: 39.3 us -> 31.6 us  [flip(): lax.ppermute(block, axis, [(i, i ^ shift) for i in range(lax.axis_size(ax...]
    ppermute x28, waiting for transfers between devices: 78 us -> 82.9 us  [flip(): lax.ppermute(block, axis, [(i, i ^ shift) for i in range(lax.axis_size(ax...]
  transfers between devices with their start and end apart: 28 -> 28, of which waited for: 17 -> 16; matrix products, arithmetic and copies ran while one was open for 20% -> 21% of each run, Pallas kernels for 0% -> 0%
where the time goes in v3:
time: 153 us
  waiting for transfers between devices  82.9 us (54%)
  starting transfers between devices  31.6 us (21%)
  matrix products  30.7 us (20%)
  local copies, waits for them, and re-layouts  3.33 us (2%)
  other arithmetic  2.23 us (1%)
  between operations  2.01 us (1%)
    ppermute x28, waiting for transfers between devices, flip(): lax.ppermute(block, axis, [(i, i ^ shift) for i in range(lax.axis_size(ax...  82.9 us
    ppermute x28, starting transfers between devices, flip(): lax.ppermute(block, axis, [(i, i ^ shift) for i in range(lax.axis_size(ax...  31.6 us
    dot_general x7, matrix products, by_rows(): lax.dot_general(left, right, (((0,), (0,)), ((), ())), preferred_element_...  12.7 us
    dot_general x6, matrix products, by_columns(): lax.dot_general(left, right, (((1,), (1,)), ((), ())), preferred_element_...  7.88 us
    dot_general x11, matrix products, spread(): return jnp.dot(matrices, rows, preferred_element_type=F32).astype(BF16)  4.67 us
  transfers between devices with their start and end apart: 28, of which 16 were waited for; matrix products, arithmetic and copies ran while one was open for 21% of the time, Pallas kernels for 0%

profile of v3, /device:TPU:0, one launch (start us, length us, event | category | flops | bytes accessed | tf_op | source)
XLA Modules:
  0.0 152.8 jit_solution(5904210805514559116)
XLA Ops:
  0.7 3.0 %collective-permute-start = (bf16[128,2048]{1,0:T(8,128)(2,1)}, bf16[128,2048]{1,0:T(8,128)(2,1)S(1)}, u32[]{:S(2)}, u32[]{:S(2)}) collective-permute-start(bf16[128,2048]{1,0:T(8,128)(2,1)} %param.12), channel_id=1, source_target_pairs={{0,2},{1,3},{2,0},{3,1},{4,6},{5,7},{6,4},{7,5},{8,10},{9,11},{10,... | collective-permute-start | bytes 1572872 | tf_op jit(solution)/shard_map/teacher_across/ppermute | solution.py:12
  6.7 2.7 %collective-permute-start.4 = (bf16[40,2048]{1,0:T(8,128)(2,1)}, bf16[40,2048]{1,0:T(8,128)(2,1)S(1)}, u32[]{:S(2)}, u32[]{:S(2)}) collective-permute-start(bf16[40,2048]{1,0:T(8,128)(2,1)} %convolution_convert_fusion.9), channel_id=1, source_target_pairs={{0,16},{4,20},{8,24},{12,28},{16,0},{20,4},{24,8},{28,12},{1,17},{... | collective-permute-start | bytes 491528 | tf_op jit(solution)/shard_map/inputs_far_4/ppermute | solution.py:12
  12.1 3.7 %collective-permute-done = bf16[128,2048]{1,0:T(8,128)(2,1)S(1)} collective-permute-done((bf16[128,2048]{1,0:T(8,128)(2,1)}, bf16[128,2048]{1,0:T(8,128)(2,1)S(1)}, u32[]{:S(2)}, u32[]{:S(2)}) %collective-permute-start) | collective-permute-done | bytes 524320 | tf_op jit(solution)/shard_map/teacher_across/ppermute | solution.py:12
  16.2 10.2 %collective-permute-done.3 = bf16[120,2048]{1,0:T(8,128)(2,1)} collective-permute-done((bf16[120,2048]{1,0:T(8,128)(2,1)S(1)}, bf16[120,2048]{1,0:T(8,128)(2,1)}, u32[]{:S(2)}, u32[]{:S(2)}) %collective-permute-start.3) | collective-permute-done | bytes 491552 | tf_op jit(solution)/shard_map/inputs_side/ppermute | solution.py:12
  30.7 1.6 %collective-permute-start.7 = (bf16[80,2048]{1,0:T(8,128)(2,1)S(1)}, bf16[80,2048]{1,0:T(8,128)(2,1)S(1)}, u32[]{:S(2)}, u32[]{:S(2)}) collective-permute-start(bf16[80,2048]{1,0:T(8,128)(2,1)S(1)} %get-tuple-element.53), channel_id=1, source_target_pairs={{0,8},{4,12},{8,0},{12,4},{16,24},{20,28},{24,16},{28,20},{1,9},{5... | collective-permute-start | bytes 983048 | tf_op jit(solution)/shard_map/inputs_z1/ppermute | solution.py:12
  32.3 2.5 %collective-permute-start.6 = (bf16[80,2048]{1,0:T(8,128)(2,1)S(1)}, bf16[80,2048]{1,0:T(8,128)(2,1)S(1)}, u32[]{:S(2)}, u32[]{:S(2)}) collective-permute-start(bf16[80,2048]{1,0:T(8,128)(2,1)S(1)} %get-tuple-element.51), channel_id=1, source_target_pairs={{0,24},{4,28},{8,16},{12,20},{16,8},{20,12},{24,0},{28,4},{1,25},{... | collective-permute-start | bytes 983048 | tf_op jit(solution)/shard_map/inputs_z3/ppermute | solution.py:12
  36.4 4.1 %collective-permute-done.7 = bf16[80,2048]{1,0:T(8,128)(2,1)S(1)} collective-permute-done((bf16[80,2048]{1,0:T(8,128)(2,1)S(1)}, bf16[80,2048]{1,0:T(8,128)(2,1)S(1)}, u32[]{:S(2)}, u32[]{:S(2)}) %collective-permute-start.7) | collective-permute-done | bytes 327712 | tf_op jit(solution)/shard_map/inputs_z1/ppermute | solution.py:12
  40.4 7.2 %collective-permute-done.6 = bf16[80,2048]{1,0:T(8,128)(2,1)S(1)} collective-permute-done((bf16[80,2048]{1,0:T(8,128)(2,1)S(1)}, bf16[80,2048]{1,0:T(8,128)(2,1)S(1)}, u32[]{:S(2)}, u32[]{:S(2)}) %collective-permute-start.6) | collective-permute-done | bytes 327712 | tf_op jit(solution)/shard_map/inputs_z3/ppermute | solution.py:12
  49.8 2.6 %collective-permute-done.9 = bf16[160,2048]{1,0:T(8,128)(2,1)S(1)} collective-permute-done((bf16[160,2048]{1,0:T(8,128)(2,1)S(1)}, bf16[160,2048]{1,0:T(8,128)(2,1)S(1)}, u32[]{:S(2)}, u32[]{:S(2)}) %collective-permute-start.9) | collective-permute-done | bytes 655392 | tf_op jit(solution)/shard_map/inputs_a/ppermute | solution.py:12
  53.5 8.4 %collective-permute-done.8 = bf16[80,2048]{1,0:T(8,128)(2,1)S(1)} collective-permute-done((bf16[80,2048]{1,0:T(8,128)(2,1)S(1)}, bf16[80,2048]{1,0:T(8,128)(2,1)S(1)}, u32[]{:S(2)}, u32[]{:S(2)}) %collective-permute-start.8) | collective-permute-done | bytes 327712 | tf_op jit(solution)/shard_map/grads_z2/ppermute | solution.py:12
  61.9 2.0 %collective-permute-start.16 = (bf16[80,2048]{1,0:T(8,128)(2,1)S(1)}, bf16[80,2048]{1,0:T(8,128)(2,1)S(1)}, u32[]{:S(2)}, u32[]{:S(2)}) collective-permute-start(bf16[80,2048]{1,0:T(8,128)(2,1)S(1)} %pad_maximum_fusion.15), channel_id=1, source_target_pairs={{0,24},{4,28},{8,16},{12,20},{16,8},{20,12},{24,0},{28,4},{1,25},{... | collective-permute-start | bytes 983048 | tf_op jit(solution)/shard_map/grads_z3/ppermute | solution.py:12
  64.0 4.7 %collective-permute-done.10 = bf16[160,2048]{1,0:T(8,128)(2,1)S(1)} collective-permute-done((bf16[160,2048]{1,0:T(8,128)(2,1)S(1)}, bf16[160,2048]{1,0:T(8,128)(2,1)S(1)}, u32[]{:S(2)}, u32[]{:S(2)}) %collective-permute-start.10) | collective-permute-done | bytes 655392 | tf_op jit(solution)/shard_map/inputs_b/ppermute | solution.py:12
  69.3 3.5 %collective-permute-done.16 = bf16[80,2048]{1,0:T(8,128)(2,1)S(1)} collective-permute-done((bf16[80,2048]{1,0:T(8,128)(2,1)S(1)}, bf16[80,2048]{1,0:T(8,128)(2,1)S(1)}, u32[]{:S(2)}, u32[]{:S(2)}) %collective-permute-start.16) | collective-permute-done | bytes 327712 | tf_op jit(solution)/shard_map/grads_z3/ppermute | solution.py:12
  75.6 8.5 %collective-permute-done.11 = bf16[160,2048]{1,0:T(8,128)(2,1)S(1)} collective-permute-done((bf16[160,2048]{1,0:T(8,128)(2,1)S(1)}, bf16[160,2048]{1,0:T(8,128)(2,1)S(1)}, u32[]{:S(2)}, u32[]{:S(2)}) %collective-permute-start.11) | collective-permute-done | bytes 655392 | tf_op jit(solution)/shard_map/grads_a/ppermute | solution.py:12
  87.4 1.4 multiply_convert_fusion.4
  90.0 1.4 convolution_add_fusion.4
  91.5 10.1 %collective-permute-done.17 = bf16[160,2048]{1,0:T(8,128)(2,1)S(1)} collective-permute-done((bf16[160,2048]{1,0:T(8,128)(2,1)S(1)}, bf16[160,2048]{1,0:T(8,128)(2,1)S(1)}, u32[]{:S(2)}, u32[]{:S(2)}) %collective-permute-start.17) | collective-permute-done | bytes 655392 | tf_op jit(solution)/shard_map/grads_b/ppermute | solution.py:12
  102.3 1.4 multiply_convert_fusion.2
  106.3 9.0 %collective-permute-done.18 = bf16[160,2048]{1,0:T(8,128)(2,1)S(1)} collective-permute-done((bf16[160,2048]{1,0:T(8,128)(2,1)S(1)}, bf16[160,2048]{1,0:T(8,128)(2,1)S(1)}, u32[]{:S(2)}, u32[]{:S(2)}) %collective-permute-start.18) | collective-permute-done | bytes 655392 | tf_op jit(solution)/shard_map/sums_a/ppermute | solution.py:12
  115.5 1.6 %collective-permute-start.19 = (bf16[40,2048]{1,0:T(8,128)(2,1)S(1)}, bf16[40,2048]{1,0:T(8,128)(2,1)S(1)}, u32[]{:S(2)}, u32[]{:S(2)}) collective-permute-start(bf16[40,2048]{1,0:T(8,128)(2,1)S(1)} %get-tuple-element.66), channel_id=1, source_target_pairs={{0,4},{4,0},{8,12},{12,8},{16,20},{20,16},{24,28},{28,24},{1,5},{5... | collective-permute-start | bytes 491528 | tf_op jit(solution)/shard_map/returned_1/ppermute | solution.py:12
  117.1 2.8 %collective-permute-start.21 = (bf16[40,2048]{1,0:T(8,128)(2,1)S(1)}, bf16[40,2048]{1,0:T(8,128)(2,1)S(1)}, u32[]{:S(2)}, u32[]{:S(2)}) collective-permute-start(bf16[40,2048]{1,0:T(8,128)(2,1)S(1)} %get-tuple-element.68), channel_id=1, source_target_pairs={{0,20},{4,16},{8,28},{12,24},{16,4},{20,0},{24,12},{28,8},{1,21},{... | collective-permute-start | bytes 491528 | tf_op jit(solution)/shard_map/returned_5/ppermute | solution.py:12
  121.4 1.4 convolution_convert_fusion.1
  122.8 2.6 %convolution_convert_fusion = bf16[704,2048]{1,0:T(8,128)(2,1)S(1)} fusion(bf16[640,2048]{1,0:T(8,128)(2,1)S(1)} %get-tuple-element.80, bf16[640,352]{1,0:T(8,128)(2,1)S(1)} %get-tuple-element.96, bf16[640,352]{1,0:T(8,128)(2,1)S(1)} %get-tuple-element.94), kind=kOutput, calls=%fused_computation.1 | convolution fusion | flops 1848737792 | bytes 6406144 | tf_op jit(solution)/shard_map/dot_general | solution.py:20
  126.0 2.5 %collective-permute-done.20 = bf16[40,2048]{1,0:T(8,128)(2,1)S(1)} collective-permute-done((bf16[40,2048]{1,0:T(8,128)(2,1)S(1)}, bf16[40,2048]{1,0:T(8,128)(2,1)S(1)}, u32[]{:S(2)}, u32[]{:S(2)}) %collective-permute-start.20) | collective-permute-done | bytes 163872 | tf_op jit(solution)/shard_map/returned_4/ppermute | solution.py:12
  128.6 1.8 %collective-permute-done.21 = bf16[40,2048]{1,0:T(8,128)(2,1)S(1)} collective-permute-done((bf16[40,2048]{1,0:T(8,128)(2,1)S(1)}, bf16[40,2048]{1,0:T(8,128)(2,1)S(1)}, u32[]{:S(2)}, u32[]{:S(2)}) %collective-permute-start.21) | collective-permute-done | bytes 163872 | tf_op jit(solution)/shard_map/returned_5/ppermute | solution.py:12
  130.3 1.9 %collective-permute-done.22 = bf16[160,2048]{1,0:T(8,128)(2,1)S(1)} collective-permute-done((bf16[160,2048]{1,0:T(8,128)(2,1)S(1)}, bf16[160,2048]{1,0:T(8,128)(2,1)S(1)}, u32[]{:S(2)}, u32[]{:S(2)}) %collective-permute-start.22) | collective-permute-done | bytes 655392 | tf_op jit(solution)/shard_map/sums_b/ppermute | solution.py:12
  133.1 2.3 %collective-permute-start.25 = (bf16[40,2048]{1,0:T(8,128)(2,1)S(1)}, bf16[40,2048]{1,0:T(8,128)(2,1)S(1)}, u32[]{:S(2)}, u32[]{:S(2)}) collective-permute-start(bf16[40,2048]{1,0:T(8,128)(2,1)S(1)} %get-tuple-element.85), channel_id=1, source_target_pairs={{0,12},{4,8},{8,4},{12,0},{16,28},{20,24},{24,20},{28,16},{1,13},{... | collective-permute-start | bytes 491528 | tf_op jit(solution)/shard_map/returned_3/ppermute | solution.py:12
  136.8 2.4 %collective-permute-start.27 = (bf16[40,2048]{1,0:T(8,128)(2,1)S(1)}, bf16[40,2048]{1,0:T(8,128)(2,1)S(1)}, u32[]{:S(2)}, u32[]{:S(2)}) collective-permute-start(bf16[40,2048]{1,0:T(8,128)(2,1)S(1)} %get-tuple-element.87), channel_id=1, source_target_pairs={{0,28},{4,24},{8,20},{12,16},{16,12},{20,8},{24,4},{28,0},{1,29},{... | collective-permute-start | bytes 491528 | tf_op jit(solution)/shard_map/returned_7/ppermute | solution.py:12
  139.5 2.4 %fusion.3 = bf16[1,352,2048]{2,1,0:T(8,128)(2,1)} fusion(bf16[640,352]{1,0:T(8,128)(2,1)S(1)} %slice.224, bf16[640,2048]{1,0:T(8,128)(2,1)S(1)} %constant_dynamic-update-slice_fusion.22, bf16[1056,2048]{1,0:T(8,128)(2,1)S(1)} %collective-permute-done.23), kind=kOutput, calls=%fused_computation.14 | convolution fusion | flops 924909568 | bytes 5955584 | tf_op jit(solution)/shard_map/dot_general | solution.py:20
  142.0 2.4 %fusion.4 = bf16[1,2048,352]{1,2,0:T(8,128)(2,1)} fusion(bf16[640,352]{1,0:T(8,128)(2,1)S(1)} %get-tuple-element.79, bf16[640,2048]{1,0:T(8,128)(2,1)S(1)} %get-tuple-element.80, bf16[1056,2048]{1,0:T(8,128)(2,1)S(1)} %collective-permute-done.23), kind=kOutput, calls=%fused_computation.15 | convolution fusion | flops 924909568 | bytes 5955584 | tf_op jit(solution)/shard_map/dot_general | solution.py:20
  144.4 2.4 %fusion.5 = bf16[1,2048,352]{1,2,0:T(8,128)(2,1)} fusion(bf16[640,352]{1,0:T(8,128)(2,1)S(1)} %get-tuple-element.76, bf16[640,2048]{1,0:T(8,128)(2,1)S(1)} %get-tuple-element.80, bf16[1056,2048]{1,0:T(8,128)(2,1)S(1)} %collective-permute-done.23), kind=kOutput, calls=%fused_computation.16 | convolution fusion | flops 924909568 | bytes 5955584 | tf_op jit(solution)/shard_map/dot_general | solution.py:20
  146.8 4.5 %collective-permute-done.27 = bf16[40,2048]{1,0:T(8,128)(2,1)S(1)} collective-permute-done((bf16[40,2048]{1,0:T(8,128)(2,1)S(1)}, bf16[40,2048]{1,0:T(8,128)(2,1)S(1)}, u32[]{:S(2)}, u32[]{:S(2)}) %collective-permute-start.27) | collective-permute-done | bytes 163872 | tf_op jit(solution)/shard_map/returned_7/ppermute | solution.py:12
  (122 shorter events, 31.9 us)
Async XLA Ops:
  0.6 15.2 %copy-start.4 = (bf16[128,2048]{1,0:T(8,128)(2,1)S(1)}, bf16[128,2048]{1,0:T(8,128)(2,1)}, u32[]{:S(2)}) copy-start(bf16[128,2048]{1,0:T(8,128)(2,1)} %param.12) | copy-start | bytes 1572868
  0.7 11.2 %copy-start.3 = (bf16[128,2048]{1,0:T(8,128)(2,1)S(1)}, bf16[128,2048]{1,0:T(8,128)(2,1)}, u32[]{:S(2)}) copy-start(bf16[128,2048]{1,0:T(8,128)(2,1)} %param.11) | copy-start | bytes 1572868
  0.7 15.2 %collective-permute-start = (bf16[128,2048]{1,0:T(8,128)(2,1)}, bf16[128,2048]{1,0:T(8,128)(2,1)S(1)}, u32[]{:S(2)}, u32[]{:S(2)}) collective-permute-start(bf16[128,2048]{1,0:T(8,128)(2,1)} %param.12), channel_id=1, source_target_pairs={{0,2},{1,3},{2,0},{3,1},{4,6},{5,7},{6,4},{7,5},{8,10},{9,11},{10,... | collective-permute-start | bytes 1572872 | tf_op jit(solution)/shard_map/teacher_across/ppermute | solution.py:12
  6.7 21.0 %collective-permute-start.4 = (bf16[40,2048]{1,0:T(8,128)(2,1)}, bf16[40,2048]{1,0:T(8,128)(2,1)S(1)}, u32[]{:S(2)}, u32[]{:S(2)}) collective-permute-start(bf16[40,2048]{1,0:T(8,128)(2,1)} %convolution_convert_fusion.9), channel_id=1, source_target_pairs={{0,16},{4,20},{8,24},{12,28},{16,0},{20,4},{24,8},{28,12},{1,17},{... | collective-permute-start | bytes 491528 | tf_op jit(solution)/shard_map/inputs_far_4/ppermute | solution.py:12
  9.4 18.4 %collective-permute-start.5 = (bf16[40,2048]{1,0:T(8,128)(2,1)}, bf16[40,2048]{1,0:T(8,128)(2,1)S(1)}, u32[]{:S(2)}, u32[]{:S(2)}) collective-permute-start(bf16[40,2048]{1,0:T(8,128)(2,1)} %convolution_convert_fusion.8), channel_id=1, source_target_pairs={{0,20},{4,16},{8,28},{12,24},{16,4},{20,0},{24,12},{28,8},{1,21},{... | collective-permute-start | bytes 491528 | tf_op jit(solution)/shard_map/inputs_far_5/ppermute | solution.py:12
  10.6 15.8 %collective-permute-start.3 = (bf16[120,2048]{1,0:T(8,128)(2,1)S(1)}, bf16[120,2048]{1,0:T(8,128)(2,1)}, u32[]{:S(2)}, u32[]{:S(2)}) collective-permute-start(bf16[120,2048]{1,0:T(8,128)(2,1)S(1)} %convolution_convert_fusion.3), channel_id=1, source_target_pairs={{0,4},{4,0},{8,12},{12,8},{16,20},{20,16},{24,28},{28,24},{1,5},{5... | collective-permute-start | bytes 1474568 | tf_op jit(solution)/shard_map/inputs_side/ppermute | solution.py:12
  11.8 15.8 %copy-start.5 = (s32[128,2]{0,1:T(2,128)S(1)}, s32[128,2]{0,1:T(2,128)}, u32[]{:S(2)}) copy-start(s32[128,2]{0,1:T(2,128)} %param.14) | copy-start | bytes 3076
  12.1 15.4 %copy-start.9 = (bf16[128,2]{0,1:T(2,128)(2,1)S(1)}, bf16[128,2]{0,1:T(2,128)(2,1)}, u32[]{:S(2)}) copy-start(bf16[128,2]{0,1:T(2,128)(2,1)} %param.15) | copy-start | bytes 1540
  15.9 12.5 %collective-permute-start.1 = (bf16[256,2048]{1,0:T(8,128)(2,1)S(1)}, bf16[256,2048]{1,0:T(8,128)(2,1)S(1)}, u32[]{:S(2)}, u32[]{:S(2)}) collective-permute-start(bf16[256,2048]{1,0:T(8,128)(2,1)S(1)} %pad_maximum_fusion.6), channel_id=1, source_target_pairs={{0,1},{1,0},{2,3},{3,2},{4,5},{5,4},{6,7},{7,6},{8,9},{9,8},{10,11... | collective-permute-start | bytes 3145736 | tf_op jit(solution)/shard_map/teacher_beside/ppermute | solution.py:12
  30.1 17.6 %collective-permute-start.2 = (bf16[160,2048]{1,0:T(8,128)(2,1)S(1)}, bf16[160,2048]{1,0:T(8,128)(2,1)S(1)}, u32[]{:S(2)}, u32[]{:S(2)}) collective-permute-start(bf16[160,2048]{1,0:T(8,128)(2,1)S(1)} %convolution_convert_fusion.2), channel_id=1, source_target_pairs={{0,4},{4,0},{8,12},{12,8},{16,20},{20,16},{24,28},{28,24},{1,5},{5... | collective-permute-start | bytes 1966088 | tf_op jit(solution)/shard_map/grads_side/ppermute | solution.py:12
  30.7 9.7 %collective-permute-start.7 = (bf16[80,2048]{1,0:T(8,128)(2,1)S(1)}, bf16[80,2048]{1,0:T(8,128)(2,1)S(1)}, u32[]{:S(2)}, u32[]{:S(2)}) collective-permute-start(bf16[80,2048]{1,0:T(8,128)(2,1)S(1)} %get-tuple-element.53), channel_id=1, source_target_pairs={{0,8},{4,12},{8,0},{12,4},{16,24},{20,28},{24,16},{28,20},{1,9},{5... | collective-permute-start | bytes 983048 | tf_op jit(solution)/shard_map/inputs_z1/ppermute | solution.py:12
  32.3 15.4 %collective-permute-start.6 = (bf16[80,2048]{1,0:T(8,128)(2,1)S(1)}, bf16[80,2048]{1,0:T(8,128)(2,1)S(1)}, u32[]{:S(2)}, u32[]{:S(2)}) collective-permute-start(bf16[80,2048]{1,0:T(8,128)(2,1)S(1)} %get-tuple-element.51), channel_id=1, source_target_pairs={{0,24},{4,28},{8,16},{12,20},{16,8},{20,12},{24,0},{28,4},{1,25},{... | collective-permute-start | bytes 983048 | tf_op jit(solution)/shard_map/inputs_z3/ppermute | solution.py:12
  35.2 18.2 %collective-permute-start.12 = (bf16[2048,352]{0,1:T(8,128)(2,1)S(1)}, bf16[2048,352]{0,1:T(8,128)(2,1)S(1)}, u32[]{:S(2)}, u32[]{:S(2)}) collective-permute-start(bf16[2048,352]{0,1:T(8,128)(2,1)S(1)} %bitcast.102), channel_id=1, source_target_pairs={{0,1},{1,0},{2,3},{3,2},{4,5},{5,4},{6,7},{7,6},{8,9},{9,8},{10,11... | collective-permute-start | bytes 4325384 | tf_op jit(solution)/shard_map/gate_weight/ppermute | solution.py:12
  35.2 17.1 %collective-permute-start.9 = (bf16[160,2048]{1,0:T(8,128)(2,1)S(1)}, bf16[160,2048]{1,0:T(8,128)(2,1)S(1)}, u32[]{:S(2)}, u32[]{:S(2)}) collective-permute-start(bf16[160,2048]{1,0:T(8,128)(2,1)S(1)} %pad_maximum_fusion.9), channel_id=1, source_target_pairs={{0,2},{1,3},{2,0},{3,1},{4,6},{5,7},{6,4},{7,5},{8,10},{9,11},{10,... | collective-permute-start | bytes 1966088 | tf_op jit(solution)/shard_map/inputs_a/ppermute | solution.py:12
  47.9 13.9 %collective-permute-start.8 = (bf16[80,2048]{1,0:T(8,128)(2,1)S(1)}, bf16[80,2048]{1,0:T(8,128)(2,1)S(1)}, u32[]{:S(2)}, u32[]{:S(2)}) collective-permute-start(bf16[80,2048]{1,0:T(8,128)(2,1)S(1)} %get-tuple-element.54), channel_id=1, source_target_pairs={{0,16},{4,20},{8,24},{12,28},{16,0},{20,4},{24,8},{28,12},{1,17},{... | collective-permute-start | bytes 983048 | tf_op jit(solution)/shard_map/grads_z2/ppermute | solution.py:12
  49.0 20.3 %collective-permute-start.15 = (bf16[80,2048]{1,0:T(8,128)(2,1)S(1)}, bf16[80,2048]{1,0:T(8,128)(2,1)S(1)}, u32[]{:S(2)}, u32[]{:S(2)}) collective-permute-start(bf16[80,2048]{1,0:T(8,128)(2,1)S(1)} %get-tuple-element.62), channel_id=1, source_target_pairs={{0,8},{4,12},{8,0},{12,4},{16,24},{20,28},{24,16},{28,20},{1,9},{5... | collective-permute-start | bytes 983048 | tf_op jit(solution)/shard_map/grads_z1/ppermute | solution.py:12
  52.4 16.3 %collective-permute-start.10 = (bf16[160,2048]{1,0:T(8,128)(2,1)S(1)}, bf16[160,2048]{1,0:T(8,128)(2,1)S(1)}, u32[]{:S(2)}, u32[]{:S(2)}) collective-permute-start(bf16[160,2048]{1,0:T(8,128)(2,1)S(1)} %pad_maximum_fusion.8), channel_id=1, source_target_pairs={{0,2},{1,3},{2,0},{3,1},{4,6},{5,7},{6,4},{7,5},{8,10},{9,11},{10,... | collective-permute-start | bytes 1966088 | tf_op jit(solution)/shard_map/inputs_b/ppermute | solution.py:12
  53.4 20.9 %collective-permute-start.13 = (bf16[2048,352]{0,1:T(8,128)(2,1)S(1)}, bf16[2048,352]{0,1:T(8,128)(2,1)S(1)}, u32[]{:S(2)}, u32[]{:S(2)}) collective-permute-start(bf16[2048,352]{0,1:T(8,128)(2,1)S(1)} %bitcast.112), channel_id=1, source_target_pairs={{0,1},{1,0},{2,3},{3,2},{4,5},{5,4},{6,7},{7,6},{8,9},{9,8},{10,11... | collective-permute-start | bytes 4325384 | tf_op jit(solution)/shard_map/up_weight/ppermute | solution.py:12
  61.9 10.9 %collective-permute-start.16 = (bf16[80,2048]{1,0:T(8,128)(2,1)S(1)}, bf16[80,2048]{1,0:T(8,128)(2,1)S(1)}, u32[]{:S(2)}, u32[]{:S(2)}) collective-permute-start(bf16[80,2048]{1,0:T(8,128)(2,1)S(1)} %pad_maximum_fusion.15), channel_id=1, source_target_pairs={{0,24},{4,28},{8,16},{12,20},{16,8},{20,12},{24,0},{28,4},{1,25},{... | collective-permute-start | bytes 983048 | tf_op jit(solution)/shard_map/grads_z3/ppermute | solution.py:12
  68.7 15.4 %collective-permute-start.11 = (bf16[160,2048]{1,0:T(8,128)(2,1)S(1)}, bf16[160,2048]{1,0:T(8,128)(2,1)S(1)}, u32[]{:S(2)}, u32[]{:S(2)}) collective-permute-start(bf16[160,2048]{1,0:T(8,128)(2,1)S(1)} %pad_maximum_fusion.7), channel_id=1, source_target_pairs={{0,2},{1,3},{2,0},{3,1},{4,6},{5,7},{6,4},{7,5},{8,10},{9,11},{10,... | collective-permute-start | bytes 1966088 | tf_op jit(solution)/shard_map/grads_a/ppermute | solution.py:12
  74.4 12.3 %collective-permute-start.14 = (bf16[352,2048]{1,0:T(8,128)(2,1)S(1)}, bf16[352,2048]{1,0:T(8,128)(2,1)S(1)}, u32[]{:S(2)}, u32[]{:S(2)}) collective-permute-start(bf16[352,2048]{1,0:T(8,128)(2,1)S(1)} %bitcast.109), channel_id=1, source_target_pairs={{0,1},{1,0},{2,3},{3,2},{4,5},{5,4},{6,7},{7,6},{8,9},{9,8},{10,11... | collective-permute-start | bytes 4325384 | tf_op jit(solution)/shard_map/down_weight/ppermute | solution.py:12
  86.7 15.0 %collective-permute-start.17 = (bf16[160,2048]{1,0:T(8,128)(2,1)S(1)}, bf16[160,2048]{1,0:T(8,128)(2,1)S(1)}, u32[]{:S(2)}, u32[]{:S(2)}) collective-permute-start(bf16[160,2048]{1,0:T(8,128)(2,1)S(1)} %pad_maximum_fusion.10), channel_id=1, source_target_pairs={{0,2},{1,3},{2,0},{3,1},{4,6},{5,7},{6,4},{7,5},{8,10},{9,11},{10,... | collective-permute-start | bytes 1966088 | tf_op jit(solution)/shard_map/grads_b/ppermute | solution.py:12
  101.6 13.6 %collective-permute-start.18 = (bf16[160,2048]{1,0:T(8,128)(2,1)S(1)}, bf16[160,2048]{1,0:T(8,128)(2,1)S(1)}, u32[]{:S(2)}, u32[]{:S(2)}) collective-permute-start(bf16[160,2048]{1,0:T(8,128)(2,1)S(1)} %slice.279), channel_id=1, source_target_pairs={{0,2},{1,3},{2,0},{3,1},{4,6},{5,7},{6,4},{7,5},{8,10},{9,11},{10,... | collective-permute-start | bytes 1966088 | tf_op jit(solution)/shard_map/sums_a/ppermute | solution.py:12
  115.5 10.6 %collective-permute-start.19 = (bf16[40,2048]{1,0:T(8,128)(2,1)S(1)}, bf16[40,2048]{1,0:T(8,128)(2,1)S(1)}, u32[]{:S(2)}, u32[]{:S(2)}) collective-permute-start(bf16[40,2048]{1,0:T(8,128)(2,1)S(1)} %get-tuple-element.66), channel_id=1, source_target_pairs={{0,4},{4,0},{8,12},{12,8},{16,20},{20,16},{24,28},{28,24},{1,5},{5... | collective-permute-start | bytes 491528 | tf_op jit(solution)/shard_map/returned_1/ppermute | solution.py:12
  117.0 11.5 %collective-permute-start.20 = (bf16[40,2048]{1,0:T(8,128)(2,1)S(1)}, bf16[40,2048]{1,0:T(8,128)(2,1)S(1)}, u32[]{:S(2)}, u32[]{:S(2)}) collective-permute-start(bf16[40,2048]{1,0:T(8,128)(2,1)S(1)} %get-tuple-element.67), channel_id=1, source_target_pairs={{0,16},{4,20},{8,24},{12,28},{16,0},{20,4},{24,8},{28,12},{1,17},{... | collective-permute-start | bytes 491528 | tf_op jit(solution)/shard_map/returned_4/ppermute | solution.py:12
  117.1 13.2 %collective-permute-start.21 = (bf16[40,2048]{1,0:T(8,128)(2,1)S(1)}, bf16[40,2048]{1,0:T(8,128)(2,1)S(1)}, u32[]{:S(2)}, u32[]{:S(2)}) collective-permute-start(bf16[40,2048]{1,0:T(8,128)(2,1)S(1)} %get-tuple-element.68), channel_id=1, source_target_pairs={{0,20},{4,16},{8,28},{12,24},{16,4},{20,0},{24,12},{28,8},{1,21},{... | collective-permute-start | bytes 491528 | tf_op jit(solution)/shard_map/returned_5/ppermute | solution.py:12
  120.3 11.9 %collective-permute-start.22 = (bf16[160,2048]{1,0:T(8,128)(2,1)S(1)}, bf16[160,2048]{1,0:T(8,128)(2,1)S(1)}, u32[]{:S(2)}, u32[]{:S(2)}) collective-permute-start(bf16[160,2048]{1,0:T(8,128)(2,1)S(1)} %slice.278), channel_id=1, source_target_pairs={{0,2},{1,3},{2,0},{3,1},{4,6},{5,7},{6,4},{7,5},{8,10},{9,11},{10,... | collective-permute-start | bytes 1966088 | tf_op jit(solution)/shard_map/sums_b/ppermute | solution.py:12
  132.2 7.3 %collective-permute-start.23 = (bf16[1056,2048]{1,0:T(8,128)(2,1)S(1)}, bf16[1056,2048]{1,0:T(8,128)(2,1)S(1)}, u32[]{:S(2)}, u32[]{:S(2)}) collective-permute-start(bf16[1056,2048]{1,0:T(8,128)(2,1)S(1)} %pad_maximum_fusion), channel_id=1, source_target_pairs={{0,1},{1,0},{2,3},{3,2},{4,5},{5,4},{6,7},{7,6},{8,9},{9,8},{10,11... | collective-permute-start | bytes 12976136 | tf_op jit(solution)/shard_map/weight_grads/ppermute | solution.py:12
  132.4 14.4 %collective-permute-start.24 = (bf16[40,2048]{1,0:T(8,128)(2,1)S(1)}, bf16[40,2048]{1,0:T(8,128)(2,1)S(1)}, u32[]{:S(2)}, u32[]{:S(2)}) collective-permute-start(bf16[40,2048]{1,0:T(8,128)(2,1)S(1)} %get-tuple-element.84), channel_id=1, source_target_pairs={{0,8},{4,12},{8,0},{12,4},{16,24},{20,28},{24,16},{28,20},{1,9},{5... | collective-permute-start | bytes 491528 | tf_op jit(solution)/shard_map/returned_2/ppermute | solution.py:12
  133.1 13.7 %collective-permute-start.25 = (bf16[40,2048]{1,0:T(8,128)(2,1)S(1)}, bf16[40,2048]{1,0:T(8,128)(2,1)S(1)}, u32[]{:S(2)}, u32[]{:S(2)}) collective-permute-start(bf16[40,2048]{1,0:T(8,128)(2,1)S(1)} %get-tuple-element.85), channel_id=1, source_target_pairs={{0,12},{4,8},{8,4},{12,0},{16,28},{20,24},{24,20},{28,16},{1,13},{... | collective-permute-start | bytes 491528 | tf_op jit(solution)/shard_map/returned_3/ppermute | solution.py:12
  135.4 11.4 %collective-permute-start.26 = (bf16[40,2048]{1,0:T(8,128)(2,1)S(1)}, bf16[40,2048]{1,0:T(8,128)(2,1)S(1)}, u32[]{:S(2)}, u32[]{:S(2)}) collective-permute-start(bf16[40,2048]{1,0:T(8,128)(2,1)S(1)} %get-tuple-element.86), channel_id=1, source_target_pairs={{0,24},{4,28},{8,16},{12,20},{16,8},{20,12},{24,0},{28,4},{1,25},{... | collective-permute-start | bytes 491528 | tf_op jit(solution)/shard_map/returned_6/ppermute | solution.py:12
  136.8 14.5 %collective-permute-start.27 = (bf16[40,2048]{1,0:T(8,128)(2,1)S(1)}, bf16[40,2048]{1,0:T(8,128)(2,1)S(1)}, u32[]{:S(2)}, u32[]{:S(2)}) collective-permute-start(bf16[40,2048]{1,0:T(8,128)(2,1)S(1)} %get-tuple-element.87), channel_id=1, source_target_pairs={{0,28},{4,24},{8,20},{12,16},{16,12},{20,8},{24,4},{28,0},{1,29},{... | collective-permute-start | bytes 491528 | tf_op jit(solution)/shard_map/returned_7/ppermute | solution.py:12
  (6 other events, 26.9 us)

commit v4 on v3

--- a/solution.py
+++ b/solution.py
@@ -90,7 +90,6 @@
     experts = jnp.arange(expert_count, dtype=jnp.int32)
     experts = experts ^ me if small else experts
     filled = slot_matrices(routes, experts, capacity)
-    weighted = slot_weights(filled, routes, after(route_weights, across), experts)
 
     def pick(matrices, shifts):
         return jnp.concatenate([matrices[k] for k in shifts], axis=0)
@@ -123,53 +122,56 @@
     if small:
         c = capacity
 
-        sent = [spread(pick(filled, (1, 3, 7)), inputs)] + [spread(filled[k], inputs) for k in (4, 5)]
-        sent = lax.optimization_barrier(sent)
+        sent = [spread(pick(filled, (1, 3, 7)), inputs)]
+        for k in (4, 5):
+            sent.append(spread(after(filled[k], sent[-1]), inputs))
+        weighted = slot_weights(filled, routes, after(route_weights, sent[0]), experts)
+        gate_other = flip(w_gate[0], "dp", 1, "gate_weight")
+        up_other = flip(after(w_up[0], gate_other), "dp", 1, "up_weight")
         x_side = flip(sent[0], "expert", 1, "inputs_side")
         x_far = [flip(rows, "expert", k, f"inputs_far_{k}") for k, rows in zip((4, 5), sent[1:])]
-        beside = flip(jnp.concatenate([teacher, across], axis=0), "dp", 1, "teacher_beside")
+        beside = flip(after(jnp.concatenate([teacher, across], axis=0), gate_other), "dp", 1, "teacher_beside")
 
         x_own, near2, near6 = [spread(after(filled[k], across), inputs) for k in (0, 2, 6)]
-        xa = jnp.concatenate([x_own, x_side[:c]] + x_far, axis=0)
         partner_teacher = partner_rows(teacher, across, beside, partner)
         aligned = jnp.dot(alignment, partner_teacher, preferred_element_type=F32)
         cotangent = (layer_out.astype(F32) - aligned).astype(BF16)
         g_send = spread(pick(weighted, (1, 3, 5, 7)), cotangent)
+        xa = jnp.concatenate(after([x_own, x_side[:c]] + x_far, g_send), axis=0)
         g_side = flip(g_send, "expert", 1, "grads_side")
-        ya = flip(after(xa, g_send), "dp", 2, "inputs_a")
+        ya = flip(xa, "dp", 2, "inputs_a")
         x_z3 = flip(after(jnp.concatenate([near6, x_side[2 * c :]], axis=0), x_far, g_send), "expert", 6, "inputs_z3")
         x_z1 = flip(after(jnp.concatenate([near2, x_side[c : 2 * c]], axis=0), x_far, g_send), "expert", 2, "inputs_z1")
         g_own, gear2, gear4, gear6 = [spread(weighted[k], cotangent) for k in (0, 2, 4, 6)]
-        gate_other = flip(after(w_gate[0], cotangent), "dp", 1, "gate_weight")
         xb = jnp.concatenate([x_z1, x_z3], axis=0)
 
-        yb = flip(after(xb, ya, g_side), "dp", 2, "inputs_b")
+        down_other = flip(after(w_down[0], cotangent), "dp", 1, "down_weight")
+        gate_weight, up_weight, down_weight = join_weights(gate_other, up_other, down_other)
+
+        yb = flip(after(xb, g_side), "dp", 2, "inputs_b")
         g_z2 = flip(after(jnp.concatenate([gear4, g_side[2 * c : 3 * c]], axis=0), x_z3, x_z1), "expert", 4, "grads_z2")
         g_z1 = flip(after(jnp.concatenate([gear2, g_side[c : 2 * c]], axis=0), x_z3, x_z1), "expert", 2, "grads_z1")
-        up_other = flip(after(w_up[0], gate_other, x_z3), "dp", 1, "up_weight")
 
         ga = jnp.concatenate([g_own, g_side[:c], g_z2], axis=0)
-        ha = flip(after(ga, yb), "dp", 2, "grads_a")
+        ha = flip(ga, "dp", 2, "grads_a")
         g_z3 = flip(after(jnp.concatenate([gear6, g_side[3 * c :]], axis=0), g_z2), "expert", 6, "grads_z3")
-        down_other = flip(after(w_down[0], up_other, yb), "dp", 1, "down_weight")
-        gate_weight, up_weight, down_weight = join_weights(gate_other, up_other, down_other)
 
         gb = jnp.concatenate([g_z1, g_z3], axis=0)
-        hb = flip(after(gb, ha, down_other), "dp", 2, "grads_b")
+        hb = flip(gb, "dp", 2, "grads_b")
         expert_inputs = [both(xa, ya), both(xb, yb)]
         expert_grads = [both(ga, ha), both(gb, hb)]
         kept, own_sums, other_sums = zip(
             *[expert_rows(r, r.shape[0] // 2, g) for r, g in zip(expert_inputs, expert_grads)]
         )
 
-        sa = flip(after(other_sums[0], hb), "dp", 2, "sums_a")
+        sa = flip(other_sums[0], "dp", 2, "sums_a")
         ra = total(own_sums[0], sa)
 
         step = (sa, other_sums[1])
-        sb = flip(after(other_sums[1], step), "dp", 2, "sums_b")
+        sb = flip(other_sums[1], "dp", 2, "sums_b")
         back = {0: ra[:c]}
         for n, k in enumerate((1, 4, 5), 1):
-            back[k] = flip(after(ra[n * c : (n + 1) * c], step), "expert", k, f"returned_{k}")
+            back[k] = flip(ra[n * c : (n + 1) * c], "expert", k, f"returned_{k}")
         rb = total(own_sums[1], sb)
         own, other = grad_halves(expert_inputs, expert_grads, after(kept, step))
         step = (sb, back[1], back[4], back[5], other)
@@ -183,6 +185,8 @@
             for ks, needed in (((0, 1, 4, 5), ()), ((2, 3, 6, 7), grads))
         ).astype(BF16)
     else:
+        weighted = slot_weights(filled, routes, route_weights, experts)
+
         def exchange(rows):
             got = lax.all_to_all(
                 rows.reshape(expert_count, capacity, features), "expert", split_axis=0, concat_axis=0, tiled=True

time: 153 us -> 147 us (0.961)
  waiting for transfers between devices: 82.9 us -> 69.4 us
  starting transfers between devices: 31.6 us -> 37.5 us
    ppermute x28, waiting for transfers between devices: 82.9 us -> 69.4 us  [flip(): lax.ppermute(block, axis, [(i, i ^ shift) for i in range(lax.axis_size(ax...]
    ppermute x28, starting transfers between devices: 31.6 us -> 37.5 us  [flip(): lax.ppermute(block, axis, [(i, i ^ shift) for i in range(lax.axis_size(ax...]
  transfers between devices with their start and end apart: 28 -> 28, of which waited for: 16 -> 14; matrix products, arithmetic and copies ran while one was open for 21% -> 25% of each run, Pallas kernels for 0% -> 0%
where the time goes in v4:
time: 147 us
  waiting for transfers between devices  69.4 us (47%)
  starting transfers between devices  37.5 us (26%)
  matrix products  31.6 us (21%)
  other arithmetic  3.39 us (2%)
  local copies, waits for them, and re-layouts  3.25 us (2%)
  between operations  2.03 us (1%)
    ppermute x28, waiting for transfers between devices, flip(): lax.ppermute(block, axis, [(i, i ^ shift) for i in range(lax.axis_size(ax...  69.4 us
    ppermute x28, starting transfers between devices, flip(): lax.ppermute(block, axis, [(i, i ^ shift) for i in range(lax.axis_size(ax...  37.5 us
    dot_general x7, matrix products, by_rows(): lax.dot_general(left, right, (((0,), (0,)), ((), ())), preferred_element_...  12.7 us
    dot_general x6, matrix products, by_columns(): lax.dot_general(left, right, (((1,), (1,)), ((), ())), preferred_element_...  7.9 us
    dot_general x11, matrix products, spread(): return jnp.dot(matrices, rows, preferred_element_type=F32).astype(BF16)  5.46 us
  transfers between devices with their start and end apart: 28, of which 14 were waited for; matrix products, arithmetic and copies ran while one was open for 25% of the time, Pallas kernels for 0%

profile of v4, /device:TPU:0, one launch (start us, length us, event | category | flops | bytes accessed | tf_op | source)
XLA Modules:
  0.0 147.2 jit_solution(7141141104995073592)
XLA Ops:
  1.2 2.6 %collective-permute-start = (bf16[128,2048]{1,0:T(8,128)(2,1)}, bf16[128,2048]{1,0:T(8,128)(2,1)}, u32[]{:S(2)}, u32[]{:S(2)}) collective-permute-start(bf16[128,2048]{1,0:T(8,128)(2,1)} %param.12), channel_id=1, source_target_pairs={{0,2},{1,3},{2,0},{3,1},{4,6},{5,7},{6,4},{7,5},{8,10},{9,11},{10,... | collective-permute-start | bytes 1572872 | tf_op jit(solution)/shard_map/teacher_across/ppermute | solution.py:12
  5.8 1.5 %collective-permute-start.4 = (bf16[120,2048]{1,0:T(8,128)(2,1)}, bf16[120,2048]{1,0:T(8,128)(2,1)}, u32[]{:S(2)}, u32[]{:S(2)}) collective-permute-start(bf16[120,2048]{1,0:T(8,128)(2,1)} %convolution_convert_fusion.3), channel_id=1, source_target_pairs={{0,4},{4,0},{8,12},{12,8},{16,20},{20,16},{24,28},{28,24},{1,5},{5... | collective-permute-start | bytes 1474568 | tf_op jit(solution)/shard_map/inputs_side/ppermute | solution.py:12
  8.2 2.6 %collective-permute-start.5 = (bf16[40,2048]{1,0:T(8,128)(2,1)}, bf16[40,2048]{1,0:T(8,128)(2,1)S(1)}, u32[]{:S(2)}, u32[]{:S(2)}) collective-permute-start(bf16[40,2048]{1,0:T(8,128)(2,1)} %convolution_convert_fusion.9), channel_id=1, source_target_pairs={{0,16},{4,20},{8,24},{12,28},{16,0},{20,4},{24,8},{28,12},{1,17},{... | collective-permute-start | bytes 491528 | tf_op jit(solution)/shard_map/inputs_far_4/ppermute | solution.py:12
  13.1 3.6 %collective-permute-done = bf16[128,2048]{1,0:T(8,128)(2,1)} collective-permute-done((bf16[128,2048]{1,0:T(8,128)(2,1)}, bf16[128,2048]{1,0:T(8,128)(2,1)}, u32[]{:S(2)}, u32[]{:S(2)}) %collective-permute-start) | collective-permute-done | bytes 524320 | tf_op jit(solution)/shard_map/teacher_across/ppermute | solution.py:12
  18.0 1.4 collective-permute-done.4
  23.1 1.6 %collective-permute-start.3 = (bf16[160,2048]{1,0:T(8,128)(2,1)S(1)}, bf16[160,2048]{1,0:T(8,128)(2,1)S(1)}, u32[]{:S(2)}, u32[]{:S(2)}) collective-permute-start(bf16[160,2048]{1,0:T(8,128)(2,1)S(1)} %convolution_convert_fusion.2), channel_id=1, source_target_pairs={{0,4},{4,0},{8,12},{12,8},{16,20},{20,16},{24,28},{28,24},{1,5},{5... | collective-permute-start | bytes 1966088 | tf_op jit(solution)/shard_map/grads_side/ppermute | solution.py:12
  25.8 3.5 %collective-permute-start.7 = (bf16[80,2048]{1,0:T(8,128)(2,1)S(1)}, bf16[80,2048]{1,0:T(8,128)(2,1)S(1)}, u32[]{:S(2)}, u32[]{:S(2)}) collective-permute-start(bf16[80,2048]{1,0:T(8,128)(2,1)S(1)} %get-tuple-element.46), channel_id=1, source_target_pairs={{0,24},{4,28},{8,16},{12,20},{16,8},{20,12},{24,0},{28,4},{1,25},{... | collective-permute-start | bytes 983048 | tf_op jit(solution)/shard_map/inputs_z3/ppermute | solution.py:12
  29.3 2.5 %collective-permute-start.8 = (bf16[80,2048]{1,0:T(8,128)(2,1)S(1)}, bf16[80,2048]{1,0:T(8,128)(2,1)S(1)}, u32[]{:S(2)}, u32[]{:S(2)}) collective-permute-start(bf16[80,2048]{1,0:T(8,128)(2,1)S(1)} %get-tuple-element.48), channel_id=1, source_target_pairs={{0,8},{4,12},{8,0},{12,4},{16,24},{20,28},{24,16},{28,20},{1,9},{5... | collective-permute-start | bytes 983048 | tf_op jit(solution)/shard_map/inputs_z1/ppermute | solution.py:12
  33.0 5.2 %collective-permute-done.7 = bf16[80,2048]{1,0:T(8,128)(2,1)S(1)} collective-permute-done((bf16[80,2048]{1,0:T(8,128)(2,1)S(1)}, bf16[80,2048]{1,0:T(8,128)(2,1)S(1)}, u32[]{:S(2)}, u32[]{:S(2)}) %collective-permute-start.7) | collective-permute-done | bytes 327712 | tf_op jit(solution)/shard_map/inputs_z3/ppermute | solution.py:12
  38.2 6.7 %collective-permute-done.8 = bf16[80,2048]{1,0:T(8,128)(2,1)S(1)} collective-permute-done((bf16[80,2048]{1,0:T(8,128)(2,1)S(1)}, bf16[80,2048]{1,0:T(8,128)(2,1)S(1)}, u32[]{:S(2)}, u32[]{:S(2)}) %collective-permute-start.8) | collective-permute-done | bytes 327712 | tf_op jit(solution)/shard_map/inputs_z1/ppermute | solution.py:12
  45.1 1.8 %collective-permute-start.19 = (bf16[80,2048]{1,0:T(8,128)(2,1)S(1)}, bf16[80,2048]{1,0:T(8,128)(2,1)S(1)}, u32[]{:S(2)}, u32[]{:S(2)}) collective-permute-start(bf16[80,2048]{1,0:T(8,128)(2,1)S(1)} %pad_maximum_fusion.14), channel_id=1, source_target_pairs={{0,8},{4,12},{8,0},{12,4},{16,24},{20,28},{24,16},{28,20},{1,9},{5... | collective-permute-start | bytes 983048 | tf_op jit(solution)/shard_map/grads_z1/ppermute | solution.py:12
  47.0 1.9 %collective-permute-start.9 = (bf16[80,2048]{1,0:T(8,128)(2,1)S(1)}, bf16[80,2048]{1,0:T(8,128)(2,1)S(1)}, u32[]{:S(2)}, u32[]{:S(2)}) collective-permute-start(bf16[80,2048]{1,0:T(8,128)(2,1)S(1)} %pad_maximum_fusion.11), channel_id=1, source_target_pairs={{0,16},{4,20},{8,24},{12,28},{16,0},{20,4},{24,8},{28,12},{1,17},{... | collective-permute-start | bytes 983048 | tf_op jit(solution)/shard_map/grads_z2/ppermute | solution.py:12
  52.0 9.0 %collective-permute-done.9 = bf16[80,2048]{1,0:T(8,128)(2,1)S(1)} collective-permute-done((bf16[80,2048]{1,0:T(8,128)(2,1)S(1)}, bf16[80,2048]{1,0:T(8,128)(2,1)S(1)}, u32[]{:S(2)}, u32[]{:S(2)}) %collective-permute-start.9) | collective-permute-done | bytes 327712 | tf_op jit(solution)/shard_map/grads_z2/ppermute | solution.py:12
  61.0 6.2 %collective-permute-start.20 = (bf16[80,2048]{1,0:T(8,128)(2,1)S(1)}, bf16[80,2048]{1,0:T(8,128)(2,1)S(1)}, u32[]{:S(2)}, u32[]{:S(2)}) collective-permute-start(bf16[80,2048]{1,0:T(8,128)(2,1)S(1)} %pad_maximum_fusion.15), channel_id=1, source_target_pairs={{0,24},{4,28},{8,16},{12,20},{16,8},{20,12},{24,0},{28,4},{1,25},{... | collective-permute-start | bytes 983048 | tf_op jit(solution)/shard_map/grads_z3/ppermute | solution.py:12
  70.0 4.6 %collective-permute-done.20 = bf16[80,2048]{1,0:T(8,128)(2,1)S(1)} collective-permute-done((bf16[80,2048]{1,0:T(8,128)(2,1)S(1)}, bf16[80,2048]{1,0:T(8,128)(2,1)S(1)}, u32[]{:S(2)}, u32[]{:S(2)}) %collective-permute-start.20) | collective-permute-done | bytes 327712 | tf_op jit(solution)/shard_map/grads_z3/ppermute | solution.py:12
  74.7 10.3 %collective-permute-done.10 = bf16[160,2048]{1,0:T(8,128)(2,1)S(1)} collective-permute-done((bf16[160,2048]{1,0:T(8,128)(2,1)S(1)}, bf16[160,2048]{1,0:T(8,128)(2,1)S(1)}, u32[]{:S(2)}, u32[]{:S(2)}) %collective-permute-start.10) | collective-permute-done | bytes 655392 | tf_op jit(solution)/shard_map/grads_a/ppermute | solution.py:12
  85.0 1.4 multiply_convert_fusion.4
  87.6 1.4 convolution_add_fusion.4
  89.3 9.7 %collective-permute-done.21 = bf16[160,2048]{1,0:T(8,128)(2,1)S(1)} collective-permute-done((bf16[160,2048]{1,0:T(8,128)(2,1)S(1)}, bf16[160,2048]{1,0:T(8,128)(2,1)S(1)}, u32[]{:S(2)}, u32[]{:S(2)}) %collective-permute-start.21) | collective-permute-done | bytes 655392 | tf_op jit(solution)/shard_map/grads_b/ppermute | solution.py:12
  99.0 1.4 multiply_convert_fusion
  103.1 9.9 %collective-permute-done.14 = bf16[160,2048]{1,0:T(8,128)(2,1)S(1)} collective-permute-done((bf16[160,2048]{1,0:T(8,128)(2,1)S(1)}, bf16[160,2048]{1,0:T(8,128)(2,1)S(1)}, u32[]{:S(2)}, u32[]{:S(2)}) %collective-permute-start.14) | collective-permute-done | bytes 655392 | tf_op jit(solution)/shard_map/sums_a/ppermute | solution.py:12
  114.1 3.6 %collective-permute-start.17 = (bf16[40,2048]{1,0:T(8,128)(2,1)S(1)}, bf16[40,2048]{1,0:T(8,128)(2,1)S(1)}, u32[]{:S(2)}, u32[]{:S(2)}) collective-permute-start(bf16[40,2048]{1,0:T(8,128)(2,1)S(1)} %get-tuple-element.89), channel_id=1, source_target_pairs={{0,20},{4,16},{8,28},{12,24},{16,4},{20,0},{24,12},{28,8},{1,21},{... | collective-permute-start | bytes 491528 | tf_op jit(solution)/shard_map/returned_5/ppermute | solution.py:12
  118.5 1.4 convolution_convert_fusion.1
  119.9 2.6 %convolution_convert_fusion = bf16[704,2048]{1,0:T(8,128)(2,1)S(1)} fusion(bf16[640,2048]{1,0:T(8,128)(2,1)S(1)} %get-tuple-element.70, bf16[640,352]{1,0:T(8,128)(2,1)S(1)} %get-tuple-element.86, bf16[640,352]{1,0:T(8,128)(2,1)S(1)} %get-tuple-element.84), kind=kOutput, calls=%fused_computation.1 | convolution fusion | flops 1848737792 | bytes 6406144 | tf_op jit(solution)/shard_map/dot_general | solution.py:20
  123.1 2.1 %collective-permute-done.16 = bf16[40,2048]{1,0:T(8,128)(2,1)S(1)} collective-permute-done((bf16[40,2048]{1,0:T(8,128)(2,1)S(1)}, bf16[40,2048]{1,0:T(8,128)(2,1)S(1)}, u32[]{:S(2)}, u32[]{:S(2)}) %collective-permute-start.16) | collective-permute-done | bytes 163872 | tf_op jit(solution)/shard_map/returned_4/ppermute | solution.py:12
  125.3 2.8 %collective-permute-done.17 = bf16[40,2048]{1,0:T(8,128)(2,1)S(1)} collective-permute-done((bf16[40,2048]{1,0:T(8,128)(2,1)S(1)}, bf16[40,2048]{1,0:T(8,128)(2,1)S(1)}, u32[]{:S(2)}, u32[]{:S(2)}) %collective-permute-start.17) | collective-permute-done | bytes 163872 | tf_op jit(solution)/shard_map/returned_5/ppermute | solution.py:12
  128.4 2.2 %collective-permute-start.25 = (bf16[40,2048]{1,0:T(8,128)(2,1)S(1)}, bf16[40,2048]{1,0:T(8,128)(2,1)S(1)}, u32[]{:S(2)}, u32[]{:S(2)}) collective-permute-start(bf16[40,2048]{1,0:T(8,128)(2,1)S(1)} %get-tuple-element.75), channel_id=1, source_target_pairs={{0,12},{4,8},{8,4},{12,0},{16,28},{20,24},{24,20},{28,16},{1,13},{... | collective-permute-start | bytes 491528 | tf_op jit(solution)/shard_map/returned_3/ppermute | solution.py:12
  131.4 3.8 %collective-permute-start.27 = (bf16[40,2048]{1,0:T(8,128)(2,1)S(1)}, bf16[40,2048]{1,0:T(8,128)(2,1)S(1)}, u32[]{:S(2)}, u32[]{:S(2)}) collective-permute-start(bf16[40,2048]{1,0:T(8,128)(2,1)S(1)} %get-tuple-element.77), channel_id=1, source_target_pairs={{0,28},{4,24},{8,20},{12,16},{16,12},{20,8},{24,4},{28,0},{1,29},{... | collective-permute-start | bytes 491528 | tf_op jit(solution)/shard_map/returned_7/ppermute | solution.py:12
  135.5 2.4 %fusion.3 = bf16[1,352,2048]{2,1,0:T(8,128)(2,1)} fusion(bf16[640,352]{1,0:T(8,128)(2,1)S(1)} %slice.216, bf16[640,2048]{1,0:T(8,128)(2,1)S(1)} %constant_dynamic-update-slice_fusion.22, bf16[1056,2048]{1,0:T(8,128)(2,1)S(1)} %collective-permute-done.23), kind=kOutput, calls=%fused_computation.14 | convolution fusion | flops 924909568 | bytes 5955584 | tf_op jit(solution)/shard_map/dot_general | solution.py:20
  137.9 2.4 %fusion.4 = bf16[1,2048,352]{1,2,0:T(8,128)(2,1)} fusion(bf16[640,352]{1,0:T(8,128)(2,1)S(1)} %get-tuple-element.69, bf16[640,2048]{1,0:T(8,128)(2,1)S(1)} %get-tuple-element.70, bf16[1056,2048]{1,0:T(8,128)(2,1)S(1)} %collective-permute-done.23), kind=kOutput, calls=%fused_computation.15 | convolution fusion | flops 924909568 | bytes 5955584 | tf_op jit(solution)/shard_map/dot_general | solution.py:20
  140.3 2.4 %fusion.5 = bf16[1,2048,352]{1,2,0:T(8,128)(2,1)} fusion(bf16[640,352]{1,0:T(8,128)(2,1)S(1)} %get-tuple-element.66, bf16[640,2048]{1,0:T(8,128)(2,1)S(1)} %get-tuple-element.70, bf16[1056,2048]{1,0:T(8,128)(2,1)S(1)} %collective-permute-done.23), kind=kOutput, calls=%fused_computation.16 | convolution fusion | flops 924909568 | bytes 5955584 | tf_op jit(solution)/shard_map/dot_general | solution.py:20
  142.7 3.0 %collective-permute-done.25 = bf16[40,2048]{1,0:T(8,128)(2,1)S(1)} collective-permute-done((bf16[40,2048]{1,0:T(8,128)(2,1)S(1)}, bf16[40,2048]{1,0:T(8,128)(2,1)S(1)}, u32[]{:S(2)}, u32[]{:S(2)}) %collective-permute-start.25) | collective-permute-done | bytes 163872 | tf_op jit(solution)/shard_map/returned_3/ppermute | solution.py:12
  (125 shorter events, 27.5 us)
Async XLA Ops:
  0.6 11.3 %copy-start.5 = (s32[128,2]{0,1:T(2,128)S(1)}, s32[128,2]{0,1:T(2,128)}, u32[]{:S(2)}) copy-start(s32[128,2]{0,1:T(2,128)} %param.14) | copy-start | bytes 3076
  0.7 11.3 %copy-start.9 = (bf16[128,2]{0,1:T(2,128)(2,1)S(1)}, bf16[128,2]{0,1:T(2,128)(2,1)}, u32[]{:S(2)}) copy-start(bf16[128,2]{0,1:T(2,128)(2,1)} %param.15) | copy-start | bytes 1540
  0.7 12.1 %copy-start.3 = (bf16[128,2048]{1,0:T(8,128)(2,1)S(1)}, bf16[128,2048]{1,0:T(8,128)(2,1)}, u32[]{:S(2)}) copy-start(bf16[128,2048]{1,0:T(8,128)(2,1)} %param.11) | copy-start | bytes 1572868
  0.7 17.3 %collective-permute-start.1 = (bf16[2048,352]{0,1:T(8,128)(2,1)}, bf16[2048,352]{0,1:T(8,128)(2,1)S(1)}, u32[]{:S(2)}, u32[]{:S(2)}) collective-permute-start(bf16[2048,352]{0,1:T(8,128)(2,1)} %bitcast.98), channel_id=1, source_target_pairs={{0,1},{1,0},{2,3},{3,2},{4,5},{5,4},{6,7},{7,6},{8,9},{9,8},{10,11... | collective-permute-start | bytes 4325384 | tf_op jit(solution)/shard_map/gate_weight/ppermute | solution.py:12
  1.2 15.4 %collective-permute-start = (bf16[128,2048]{1,0:T(8,128)(2,1)}, bf16[128,2048]{1,0:T(8,128)(2,1)}, u32[]{:S(2)}, u32[]{:S(2)}) collective-permute-start(bf16[128,2048]{1,0:T(8,128)(2,1)} %param.12), channel_id=1, source_target_pairs={{0,2},{1,3},{2,0},{3,1},{4,6},{5,7},{6,4},{7,5},{8,10},{9,11},{10,... | collective-permute-start | bytes 1572872 | tf_op jit(solution)/shard_map/teacher_across/ppermute | solution.py:12
  5.8 13.6 %collective-permute-start.4 = (bf16[120,2048]{1,0:T(8,128)(2,1)}, bf16[120,2048]{1,0:T(8,128)(2,1)}, u32[]{:S(2)}, u32[]{:S(2)}) collective-permute-start(bf16[120,2048]{1,0:T(8,128)(2,1)} %convolution_convert_fusion.3), channel_id=1, source_target_pairs={{0,4},{4,0},{8,12},{12,8},{16,20},{20,16},{24,28},{28,24},{1,5},{5... | collective-permute-start | bytes 1474568 | tf_op jit(solution)/shard_map/inputs_side/ppermute | solution.py:12
  8.2 17.6 %collective-permute-start.5 = (bf16[40,2048]{1,0:T(8,128)(2,1)}, bf16[40,2048]{1,0:T(8,128)(2,1)S(1)}, u32[]{:S(2)}, u32[]{:S(2)}) collective-permute-start(bf16[40,2048]{1,0:T(8,128)(2,1)} %convolution_convert_fusion.9), channel_id=1, source_target_pairs={{0,16},{4,20},{8,24},{12,28},{16,0},{20,4},{24,8},{28,12},{1,17},{... | collective-permute-start | bytes 491528 | tf_op jit(solution)/shard_map/inputs_far_4/ppermute | solution.py:12
  11.7 14.1 %collective-permute-start.6 = (bf16[40,2048]{1,0:T(8,128)(2,1)}, bf16[40,2048]{1,0:T(8,128)(2,1)S(1)}, u32[]{:S(2)}, u32[]{:S(2)}) collective-permute-start(bf16[40,2048]{1,0:T(8,128)(2,1)} %convolution_convert_fusion.8), channel_id=1, source_target_pairs={{0,20},{4,16},{8,28},{12,24},{16,4},{20,0},{24,12},{28,8},{1,21},{... | collective-permute-start | bytes 491528 | tf_op jit(solution)/shard_map/inputs_far_5/ppermute | solution.py:12
  17.9 3.4 %collective-permute-start.2 = (bf16[256,2048]{1,0:T(8,128)(2,1)S(1)}, bf16[256,2048]{1,0:T(8,128)(2,1)S(1)}, u32[]{:S(2)}, u32[]{:S(2)}) collective-permute-start(bf16[256,2048]{1,0:T(8,128)(2,1)S(1)} %pad_maximum_fusion.6), channel_id=1, source_target_pairs={{0,1},{1,0},{2,3},{3,2},{4,5},{5,4},{6,7},{7,6},{8,9},{9,8},{10,11... | collective-permute-start | bytes 3145736 | tf_op jit(solution)/shard_map/teacher_beside/ppermute | solution.py:12
  21.3 29.4 %collective-permute-start.13 = (bf16[2048,352]{0,1:T(8,128)(2,1)S(1)}, bf16[2048,352]{0,1:T(8,128)(2,1)S(1)}, u32[]{:S(2)}, u32[]{:S(2)}) collective-permute-start(bf16[2048,352]{0,1:T(8,128)(2,1)S(1)} %bitcast.108), channel_id=1, source_target_pairs={{0,1},{1,0},{2,3},{3,2},{4,5},{5,4},{6,7},{7,6},{8,9},{9,8},{10,11... | collective-permute-start | bytes 4325384 | tf_op jit(solution)/shard_map/up_weight/ppermute | solution.py:12
  23.1 15.1 %copy-start.6 = (bf16[1,352,2048]{2,1,0:T(8,128)(2,1)S(1)}, bf16[1,352,2048]{2,1,0:T(8,128)(2,1)}, u32[]{:S(2)}) copy-start(bf16[1,352,2048]{2,1,0:T(8,128)(2,1)} %param.19) | copy-start | bytes 4325380
  23.1 21.9 %collective-permute-start.3 = (bf16[160,2048]{1,0:T(8,128)(2,1)S(1)}, bf16[160,2048]{1,0:T(8,128)(2,1)S(1)}, u32[]{:S(2)}, u32[]{:S(2)}) collective-permute-start(bf16[160,2048]{1,0:T(8,128)(2,1)S(1)} %convolution_convert_fusion.2), channel_id=1, source_target_pairs={{0,4},{4,0},{8,12},{12,8},{16,20},{20,16},{24,28},{28,24},{1,5},{5... | collective-permute-start | bytes 1966088 | tf_op jit(solution)/shard_map/grads_side/ppermute | solution.py:12
  25.8 12.4 %collective-permute-start.7 = (bf16[80,2048]{1,0:T(8,128)(2,1)S(1)}, bf16[80,2048]{1,0:T(8,128)(2,1)S(1)}, u32[]{:S(2)}, u32[]{:S(2)}) collective-permute-start(bf16[80,2048]{1,0:T(8,128)(2,1)S(1)} %get-tuple-element.46), channel_id=1, source_target_pairs={{0,24},{4,28},{8,16},{12,20},{16,8},{20,12},{24,0},{28,4},{1,25},{... | collective-permute-start | bytes 983048 | tf_op jit(solution)/shard_map/inputs_z3/ppermute | solution.py:12
  29.3 15.6 %collective-permute-start.8 = (bf16[80,2048]{1,0:T(8,128)(2,1)S(1)}, bf16[80,2048]{1,0:T(8,128)(2,1)S(1)}, u32[]{:S(2)}, u32[]{:S(2)}) collective-permute-start(bf16[80,2048]{1,0:T(8,128)(2,1)S(1)} %get-tuple-element.48), channel_id=1, source_target_pairs={{0,8},{4,12},{8,0},{12,4},{16,24},{20,28},{24,16},{28,20},{1,9},{5... | collective-permute-start | bytes 983048 | tf_op jit(solution)/shard_map/inputs_z1/ppermute | solution.py:12
  31.9 17.0 %collective-permute-start.12 = (bf16[160,2048]{1,0:T(8,128)(2,1)S(1)}, bf16[160,2048]{1,0:T(8,128)(2,1)S(1)}, u32[]{:S(2)}, u32[]{:S(2)}) collective-permute-start(bf16[160,2048]{1,0:T(8,128)(2,1)S(1)} %pad_maximum_fusion.8), channel_id=1, source_target_pairs={{0,2},{1,3},{2,0},{3,1},{4,6},{5,7},{6,4},{7,5},{8,10},{9,11},{10,... | collective-permute-start | bytes 1966088 | tf_op jit(solution)/shard_map/inputs_a/ppermute | solution.py:12
  38.2 36.4 %collective-permute-start.11 = (bf16[352,2048]{1,0:T(8,128)(2,1)S(1)}, bf16[352,2048]{1,0:T(8,128)(2,1)S(1)}, u32[]{:S(2)}, u32[]{:S(2)}) collective-permute-start(bf16[352,2048]{1,0:T(8,128)(2,1)S(1)} %bitcast.105), channel_id=1, source_target_pairs={{0,1},{1,0},{2,3},{3,2},{4,5},{5,4},{6,7},{7,6},{8,9},{9,8},{10,11... | collective-permute-start | bytes 4325384 | tf_op jit(solution)/shard_map/down_weight/ppermute | solution.py:12
  45.1 24.9 %collective-permute-start.19 = (bf16[80,2048]{1,0:T(8,128)(2,1)S(1)}, bf16[80,2048]{1,0:T(8,128)(2,1)S(1)}, u32[]{:S(2)}, u32[]{:S(2)}) collective-permute-start(bf16[80,2048]{1,0:T(8,128)(2,1)S(1)} %pad_maximum_fusion.14), channel_id=1, source_target_pairs={{0,8},{4,12},{8,0},{12,4},{16,24},{20,28},{24,16},{28,20},{1,9},{5... | collective-permute-start | bytes 983048 | tf_op jit(solution)/shard_map/grads_z1/ppermute | solution.py:12
  47.0 14.0 %collective-permute-start.9 = (bf16[80,2048]{1,0:T(8,128)(2,1)S(1)}, bf16[80,2048]{1,0:T(8,128)(2,1)S(1)}, u32[]{:S(2)}, u32[]{:S(2)}) collective-permute-start(bf16[80,2048]{1,0:T(8,128)(2,1)S(1)} %pad_maximum_fusion.11), channel_id=1, source_target_pairs={{0,16},{4,20},{8,24},{12,28},{16,0},{20,4},{24,8},{28,12},{1,17},{... | collective-permute-start | bytes 983048 | tf_op jit(solution)/shard_map/grads_z2/ppermute | solution.py:12
  48.9 18.4 %collective-permute-start.18 = (bf16[160,2048]{1,0:T(8,128)(2,1)S(1)}, bf16[160,2048]{1,0:T(8,128)(2,1)S(1)}, u32[]{:S(2)}, u32[]{:S(2)}) collective-permute-start(bf16[160,2048]{1,0:T(8,128)(2,1)S(1)} %pad_maximum_fusion.9), channel_id=1, source_target_pairs={{0,2},{1,3},{2,0},{3,1},{4,6},{5,7},{6,4},{7,5},{8,10},{9,11},{10,... | collective-permute-start | bytes 1966088 | tf_op jit(solution)/shard_map/inputs_b/ppermute | solution.py:12
  61.0 13.5 %collective-permute-start.20 = (bf16[80,2048]{1,0:T(8,128)(2,1)S(1)}, bf16[80,2048]{1,0:T(8,128)(2,1)S(1)}, u32[]{:S(2)}, u32[]{:S(2)}) collective-permute-start(bf16[80,2048]{1,0:T(8,128)(2,1)S(1)} %pad_maximum_fusion.15), channel_id=1, source_target_pairs={{0,24},{4,28},{8,16},{12,20},{16,8},{20,12},{24,0},{28,4},{1,25},{... | collective-permute-start | bytes 983048 | tf_op jit(solution)/shard_map/grads_z3/ppermute | solution.py:12
  67.2 17.7 %collective-permute-start.10 = (bf16[160,2048]{1,0:T(8,128)(2,1)S(1)}, bf16[160,2048]{1,0:T(8,128)(2,1)S(1)}, u32[]{:S(2)}, u32[]{:S(2)}) collective-permute-start(bf16[160,2048]{1,0:T(8,128)(2,1)S(1)} %pad_maximum_fusion.7), channel_id=1, source_target_pairs={{0,2},{1,3},{2,0},{3,1},{4,6},{5,7},{6,4},{7,5},{8,10},{9,11},{10,... | collective-permute-start | bytes 1966088 | tf_op jit(solution)/shard_map/grads_a/ppermute | solution.py:12
  74.6 24.4 %collective-permute-start.21 = (bf16[160,2048]{1,0:T(8,128)(2,1)S(1)}, bf16[160,2048]{1,0:T(8,128)(2,1)S(1)}, u32[]{:S(2)}, u32[]{:S(2)}) collective-permute-start(bf16[160,2048]{1,0:T(8,128)(2,1)S(1)} %pad_maximum_fusion.10), channel_id=1, source_target_pairs={{0,2},{1,3},{2,0},{3,1},{4,6},{5,7},{6,4},{7,5},{8,10},{9,11},{10,... | collective-permute-start | bytes 1966088 | tf_op jit(solution)/shard_map/grads_b/ppermute | solution.py:12
  89.1 23.9 %collective-permute-start.14 = (bf16[160,2048]{1,0:T(8,128)(2,1)S(1)}, bf16[160,2048]{1,0:T(8,128)(2,1)S(1)}, u32[]{:S(2)}, u32[]{:S(2)}) collective-permute-start(bf16[160,2048]{1,0:T(8,128)(2,1)S(1)} %slice.265), channel_id=1, source_target_pairs={{0,2},{1,3},{2,0},{3,1},{4,6},{5,7},{6,4},{7,5},{8,10},{9,11},{10,... | collective-permute-start | bytes 1966088 | tf_op jit(solution)/shard_map/sums_a/ppermute | solution.py:12
  103.0 25.1 %collective-permute-start.22 = (bf16[160,2048]{1,0:T(8,128)(2,1)S(1)}, bf16[160,2048]{1,0:T(8,128)(2,1)S(1)}, u32[]{:S(2)}, u32[]{:S(2)}) collective-permute-start(bf16[160,2048]{1,0:T(8,128)(2,1)S(1)} %slice.264), channel_id=1, source_target_pairs={{0,2},{1,3},{2,0},{3,1},{4,6},{5,7},{6,4},{7,5},{8,10},{9,11},{10,... | collective-permute-start | bytes 1966088 | tf_op jit(solution)/shard_map/sums_b/ppermute | solution.py:12
  113.3 9.9 %collective-permute-start.15 = (bf16[40,2048]{1,0:T(8,128)(2,1)S(1)}, bf16[40,2048]{1,0:T(8,128)(2,1)S(1)}, u32[]{:S(2)}, u32[]{:S(2)}) collective-permute-start(bf16[40,2048]{1,0:T(8,128)(2,1)S(1)} %get-tuple-element.91), channel_id=1, source_target_pairs={{0,4},{4,0},{8,12},{12,8},{16,20},{20,16},{24,28},{28,24},{1,5},{5... | collective-permute-start | bytes 491528 | tf_op jit(solution)/shard_map/returned_1/ppermute | solution.py:12
  114.1 11.1 %collective-permute-start.16 = (bf16[40,2048]{1,0:T(8,128)(2,1)S(1)}, bf16[40,2048]{1,0:T(8,128)(2,1)S(1)}, u32[]{:S(2)}, u32[]{:S(2)}) collective-permute-start(bf16[40,2048]{1,0:T(8,128)(2,1)S(1)} %get-tuple-element.90), channel_id=1, source_target_pairs={{0,16},{4,20},{8,24},{12,28},{16,0},{20,4},{24,8},{28,12},{1,17},{... | collective-permute-start | bytes 491528 | tf_op jit(solution)/shard_map/returned_4/ppermute | solution.py:12
  114.1 14.0 %collective-permute-start.17 = (bf16[40,2048]{1,0:T(8,128)(2,1)S(1)}, bf16[40,2048]{1,0:T(8,128)(2,1)S(1)}, u32[]{:S(2)}, u32[]{:S(2)}) collective-permute-start(bf16[40,2048]{1,0:T(8,128)(2,1)S(1)} %get-tuple-element.89), channel_id=1, source_target_pairs={{0,20},{4,16},{8,28},{12,24},{16,4},{20,0},{24,12},{28,8},{1,21},{... | collective-permute-start | bytes 491528 | tf_op jit(solution)/shard_map/returned_5/ppermute | solution.py:12
  128.1 7.3 %collective-permute-start.23 = (bf16[1056,2048]{1,0:T(8,128)(2,1)S(1)}, bf16[1056,2048]{1,0:T(8,128)(2,1)S(1)}, u32[]{:S(2)}, u32[]{:S(2)}) collective-permute-start(bf16[1056,2048]{1,0:T(8,128)(2,1)S(1)} %pad_maximum_fusion), channel_id=1, source_target_pairs={{0,1},{1,0},{2,3},{3,2},{4,5},{5,4},{6,7},{7,6},{8,9},{9,8},{10,11... | collective-permute-start | bytes 12976136 | tf_op jit(solution)/shard_map/weight_grads/ppermute | solution.py:12
  128.3 14.4 %collective-permute-start.24 = (bf16[40,2048]{1,0:T(8,128)(2,1)S(1)}, bf16[40,2048]{1,0:T(8,128)(2,1)S(1)}, u32[]{:S(2)}, u32[]{:S(2)}) collective-permute-start(bf16[40,2048]{1,0:T(8,128)(2,1)S(1)} %get-tuple-element.74), channel_id=1, source_target_pairs={{0,8},{4,12},{8,0},{12,4},{16,24},{20,28},{24,16},{28,20},{1,9},{5... | collective-permute-start | bytes 491528 | tf_op jit(solution)/shard_map/returned_2/ppermute | solution.py:12
  128.4 17.3 %collective-permute-start.25 = (bf16[40,2048]{1,0:T(8,128)(2,1)S(1)}, bf16[40,2048]{1,0:T(8,128)(2,1)S(1)}, u32[]{:S(2)}, u32[]{:S(2)}) collective-permute-start(bf16[40,2048]{1,0:T(8,128)(2,1)S(1)} %get-tuple-element.75), channel_id=1, source_target_pairs={{0,12},{4,8},{8,4},{12,0},{16,28},{20,24},{24,20},{28,16},{1,13},{... | collective-permute-start | bytes 491528 | tf_op jit(solution)/shard_map/returned_3/ppermute | solution.py:12
  130.6 15.1 %collective-permute-start.26 = (bf16[40,2048]{1,0:T(8,128)(2,1)S(1)}, bf16[40,2048]{1,0:T(8,128)(2,1)S(1)}, u32[]{:S(2)}, u32[]{:S(2)}) collective-permute-start(bf16[40,2048]{1,0:T(8,128)(2,1)S(1)} %get-tuple-element.76), channel_id=1, source_target_pairs={{0,24},{4,28},{8,16},{12,20},{16,8},{20,12},{24,0},{28,4},{1,25},{... | collective-permute-start | bytes 491528 | tf_op jit(solution)/shard_map/returned_6/ppermute | solution.py:12
  131.4 14.4 %collective-permute-start.27 = (bf16[40,2048]{1,0:T(8,128)(2,1)S(1)}, bf16[40,2048]{1,0:T(8,128)(2,1)S(1)}, u32[]{:S(2)}, u32[]{:S(2)}) collective-permute-start(bf16[40,2048]{1,0:T(8,128)(2,1)S(1)} %get-tuple-element.77), channel_id=1, source_target_pairs={{0,28},{4,24},{8,20},{12,16},{16,12},{20,8},{24,4},{28,0},{1,29},{... | collective-permute-start | bytes 491528 | tf_op jit(solution)/shard_map/returned_7/ppermute | solution.py:12
  (6 other events, 25.7 us)

commit v5 on v4

--- a/solution.py
+++ b/solution.py
@@ -154,7 +154,7 @@
 
         ga = jnp.concatenate([g_own, g_side[:c], g_z2], axis=0)
         ha = flip(ga, "dp", 2, "grads_a")
-        g_z3 = flip(after(jnp.concatenate([gear6, g_side[3 * c :]], axis=0), g_z2), "expert", 6, "grads_z3")
+        g_z3 = flip(after(jnp.concatenate([gear6, g_side[3 * c :]], axis=0), ga), "expert", 6, "grads_z3")
 
         gb = jnp.concatenate([g_z1, g_z3], axis=0)
         hb = flip(gb, "dp", 2, "grads_b")
@@ -164,22 +164,23 @@
             *[expert_rows(r, r.shape[0] // 2, g) for r, g in zip(expert_inputs, expert_grads)]
         )
 
-        sa = flip(other_sums[0], "dp", 2, "sums_a")
-        ra = total(own_sums[0], sa)
-
-        step = (sa, other_sums[1])
-        sb = flip(other_sums[1], "dp", 2, "sums_b")
-        back = {0: ra[:c]}
-        for n, k in enumerate((1, 4, 5), 1):
-            back[k] = flip(ra[n * c : (n + 1) * c], "expert", k, f"returned_{k}")
-        rb = total(own_sums[1], sb)
-        own, other = grad_halves(expert_inputs, expert_grads, after(kept, step))
-        step = (sb, back[1], back[4], back[5], other)
-
-        for n, k in enumerate((2, 3, 6, 7)):
-            back[k] = flip(after(rb[n * c : (n + 1) * c], step), "expert", k, f"returned_{k}")
-        own, other = after((own, other), step)
-        grads = grad_totals(own, flip(other, "dp", 1, "weight_grads"))
+        s_z2 = flip(other_sums[0][2 * c :], "dp", 2, "sums_z2")
+        r_z2 = total(own_sums[0][2 * c :], s_z2)
+        s_z3 = flip(other_sums[1][2 * c :], "dp", 2, "sums_z3")
+        r_z3 = total(own_sums[1][2 * c :], s_z3)
+        s_near = jnp.concatenate([other_sums[0][: 2 * c], other_sums[1][: 2 * c]], axis=0)
+        s_near = flip(after(s_near, s_z3, s_z2), "dp", 2, "sums_near")
+        s_near = after(s_near, r_z2, r_z3)
+        r_near = [total(own_sums[n][: 2 * c], s_near[2 * n * c : 2 * (n + 1) * c]) for n in range(2)]
+        back = {0: r_near[0][:c]}
+        for rows, first in ((r_z2, 4), (r_z3, 6)):
+            for n in range(2):
+                back[first + n] = flip(rows[n * c : (n + 1) * c], "expert", first + n, f"R{first + n}")
+        own, other = grad_halves(expert_inputs, expert_grads, after(kept, other_sums[1]))
+        other = flip(after(other, back[4], back[5], s_near), "dp", 1, "weight_grads")
+        for rows, k in ((r_near[0][c:], 1), (r_near[1][:c], 2), (r_near[1][c:], 3)):
+            back[k] = flip(after(rows, back[4], back[5]), "expert", k, f"returned_{k}")
+        grads = grad_totals(own, other)
         grad_inputs = sum(
             by_rows(after(pick(filled, ks), needed), jnp.concatenate([back[k] for k in ks], axis=0))
             for ks, needed in (((0, 1, 4, 5), ()), ((2, 3, 6, 7), grads))

time: 147 us -> 145 us (0.986)
  waiting for transfers between devices: 69.4 us -> 66.9 us
    ppermute x28 -> x29, waiting for transfers between devices: 69.4 us -> 66.9 us  [flip(): lax.ppermute(block, axis, [(i, i ^ shift) for i in range(lax.axis_size(ax...]
    ppermute x28 -> x29, starting transfers between devices: 37.5 us -> 38.7 us  [flip(): lax.ppermute(block, axis, [(i, i ^ shift) for i in range(lax.axis_size(ax...]
  transfers between devices with their start and end apart: 28 -> 29, of which waited for: 14 -> 15; matrix products, arithmetic and copies ran while one was open for 25% -> 25% of each run, Pallas kernels for 0% -> 0%
where the time goes in v5:
time: 145 us; the launch traced here: 146 us
  waiting for transfers between devices  66.9 us (46%)
  starting transfers between devices  38.7 us (27%)
  matrix products  31.8 us (22%)
  other arithmetic  3.44 us (2%)
  local copies, waits for them, and re-layouts  3 us (2%)
  between operations  2.02 us (1%)
    ppermute x29, waiting for transfers between devices, flip(): lax.ppermute(block, axis, [(i, i ^ shift) for i in range(lax.axis_size(ax...  66.9 us
    ppermute x29, starting transfers between devices, flip(): lax.ppermute(block, axis, [(i, i ^ shift) for i in range(lax.axis_size(ax...  38.7 us
    dot_general x7, matrix products, by_rows(): lax.dot_general(left, right, (((0,), (0,)), ((), ())), preferred_element_...  12.7 us
    dot_general x6, matrix products, by_columns(): lax.dot_general(left, right, (((1,), (1,)), ((), ())), preferred_element_...  7.89 us
    dot_general x11, matrix products, spread(): return jnp.dot(matrices, rows, preferred_element_type=F32).astype(BF16)  5.46 us
  transfers between devices with their start and end apart: 29, of which 15 were waited for; matrix products, arithmetic and copies ran while one was open for 25% of the time, Pallas kernels for 0%

profile of v5, /device:TPU:0, one launch (start us, length us, event | category | flops | bytes accessed | tf_op | source)
XLA Modules:
  0.0 145.8 jit_solution(7179920058547274225)
XLA Ops:
  1.2 2.6 %collective-permute-start = (bf16[128,2048]{1,0:T(8,128)(2,1)}, bf16[128,2048]{1,0:T(8,128)(2,1)}, u32[]{:S(2)}, u32[]{:S(2)}) collective-permute-start(bf16[128,2048]{1,0:T(8,128)(2,1)} %param.12), channel_id=1, source_target_pairs={{0,2},{1,3},{2,0},{3,1},{4,6},{5,7},{6,4},{7,5},{8,10},{9,11},{10,... | collective-permute-start | bytes 1572872 | tf_op jit(solution)/shard_map/teacher_across/ppermute | solution.py:12
  5.8 1.5 %collective-permute-start.4 = (bf16[120,2048]{1,0:T(8,128)(2,1)}, bf16[120,2048]{1,0:T(8,128)(2,1)}, u32[]{:S(2)}, u32[]{:S(2)}) collective-permute-start(bf16[120,2048]{1,0:T(8,128)(2,1)} %convolution_convert_fusion.3), channel_id=1, source_target_pairs={{0,4},{4,0},{8,12},{12,8},{16,20},{20,16},{24,28},{28,24},{1,5},{5... | collective-permute-start | bytes 1474568 | tf_op jit(solution)/shard_map/inputs_side/ppermute | solution.py:12
  8.2 2.6 %collective-permute-start.5 = (bf16[40,2048]{1,0:T(8,128)(2,1)}, bf16[40,2048]{1,0:T(8,128)(2,1)S(1)}, u32[]{:S(2)}, u32[]{:S(2)}) collective-permute-start(bf16[40,2048]{1,0:T(8,128)(2,1)} %convolution_convert_fusion.9), channel_id=1, source_target_pairs={{0,16},{4,20},{8,24},{12,28},{16,0},{20,4},{24,8},{28,12},{1,17},{... | collective-permute-start | bytes 491528 | tf_op jit(solution)/shard_map/inputs_far_4/ppermute | solution.py:12
  13.1 3.6 %collective-permute-done = bf16[128,2048]{1,0:T(8,128)(2,1)} collective-permute-done((bf16[128,2048]{1,0:T(8,128)(2,1)}, bf16[128,2048]{1,0:T(8,128)(2,1)}, u32[]{:S(2)}, u32[]{:S(2)}) %collective-permute-start) | collective-permute-done | bytes 524320 | tf_op jit(solution)/shard_map/teacher_across/ppermute | solution.py:12
  23.1 1.6 %collective-permute-start.3 = (bf16[160,2048]{1,0:T(8,128)(2,1)S(1)}, bf16[160,2048]{1,0:T(8,128)(2,1)S(1)}, u32[]{:S(2)}, u32[]{:S(2)}) collective-permute-start(bf16[160,2048]{1,0:T(8,128)(2,1)S(1)} %convolution_convert_fusion.2), channel_id=1, source_target_pairs={{0,4},{4,0},{8,12},{12,8},{16,20},{20,16},{24,28},{28,24},{1,5},{5... | collective-permute-start | bytes 1966088 | tf_op jit(solution)/shard_map/grads_side/ppermute | solution.py:12
  25.8 3.5 %collective-permute-start.7 = (bf16[80,2048]{1,0:T(8,128)(2,1)S(1)}, bf16[80,2048]{1,0:T(8,128)(2,1)S(1)}, u32[]{:S(2)}, u32[]{:S(2)}) collective-permute-start(bf16[80,2048]{1,0:T(8,128)(2,1)S(1)} %get-tuple-element.41), channel_id=1, source_target_pairs={{0,24},{4,28},{8,16},{12,20},{16,8},{20,12},{24,0},{28,4},{1,25},{... | collective-permute-start | bytes 983048 | tf_op jit(solution)/shard_map/inputs_z3/ppermute | solution.py:12
  29.3 2.6 %collective-permute-start.8 = (bf16[80,2048]{1,0:T(8,128)(2,1)S(1)}, bf16[80,2048]{1,0:T(8,128)(2,1)S(1)}, u32[]{:S(2)}, u32[]{:S(2)}) collective-permute-start(bf16[80,2048]{1,0:T(8,128)(2,1)S(1)} %get-tuple-element.43), channel_id=1, source_target_pairs={{0,8},{4,12},{8,0},{12,4},{16,24},{20,28},{24,16},{28,20},{1,9},{5... | collective-permute-start | bytes 983048 | tf_op jit(solution)/shard_map/inputs_z1/ppermute | solution.py:12
  33.0 5.2 %collective-permute-done.7 = bf16[80,2048]{1,0:T(8,128)(2,1)S(1)} collective-permute-done((bf16[80,2048]{1,0:T(8,128)(2,1)S(1)}, bf16[80,2048]{1,0:T(8,128)(2,1)S(1)}, u32[]{:S(2)}, u32[]{:S(2)}) %collective-permute-start.7) | collective-permute-done | bytes 327712 | tf_op jit(solution)/shard_map/inputs_z3/ppermute | solution.py:12
  38.2 6.0 %collective-permute-done.8 = bf16[80,2048]{1,0:T(8,128)(2,1)S(1)} collective-permute-done((bf16[80,2048]{1,0:T(8,128)(2,1)S(1)}, bf16[80,2048]{1,0:T(8,128)(2,1)S(1)}, u32[]{:S(2)}, u32[]{:S(2)}) %collective-permute-start.8) | collective-permute-done | bytes 327712 | tf_op jit(solution)/shard_map/inputs_z1/ppermute | solution.py:12
  44.4 2.9 %collective-permute-start.9 = (bf16[80,2048]{1,0:T(8,128)(2,1)S(1)}, bf16[80,2048]{1,0:T(8,128)(2,1)S(1)}, u32[]{:S(2)}, u32[]{:S(2)}) collective-permute-start(bf16[80,2048]{1,0:T(8,128)(2,1)S(1)} %pad_maximum_fusion.12), channel_id=1, source_target_pairs={{0,16},{4,20},{8,24},{12,28},{16,0},{20,4},{24,8},{28,12},{1,17},{... | collective-permute-start | bytes 983048 | tf_op jit(solution)/shard_map/grads_z2/ppermute | solution.py:12
  52.4 10.2 %collective-permute-done.9 = bf16[80,2048]{1,0:T(8,128)(2,1)S(1)} collective-permute-done((bf16[80,2048]{1,0:T(8,128)(2,1)S(1)}, bf16[80,2048]{1,0:T(8,128)(2,1)S(1)}, u32[]{:S(2)}, u32[]{:S(2)}) %collective-permute-start.9) | collective-permute-done | bytes 327712 | tf_op jit(solution)/shard_map/grads_z2/ppermute | solution.py:12
  63.2 3.0 %collective-permute-start.15 = (bf16[80,2048]{1,0:T(8,128)(2,1)S(1)}, bf16[80,2048]{1,0:T(8,128)(2,1)S(1)}, u32[]{:S(2)}, u32[]{:S(2)}) collective-permute-start(bf16[80,2048]{1,0:T(8,128)(2,1)S(1)} %pad_maximum_fusion.16), channel_id=1, source_target_pairs={{0,24},{4,28},{8,16},{12,20},{16,8},{20,12},{24,0},{28,4},{1,25},{... | collective-permute-start | bytes 983048 | tf_op jit(solution)/shard_map/grads_z3/ppermute | solution.py:12
  69.2 5.0 %collective-permute-done.15 = bf16[80,2048]{1,0:T(8,128)(2,1)S(1)} collective-permute-done((bf16[80,2048]{1,0:T(8,128)(2,1)S(1)}, bf16[80,2048]{1,0:T(8,128)(2,1)S(1)}, u32[]{:S(2)}, u32[]{:S(2)}) %collective-permute-start.15) | collective-permute-done | bytes 327712 | tf_op jit(solution)/shard_map/grads_z3/ppermute | solution.py:12
  74.2 1.6 %collective-permute-start.16 = (bf16[160,2048]{1,0:T(8,128)(2,1)S(1)}, bf16[160,2048]{1,0:T(8,128)(2,1)S(1)}, u32[]{:S(2)}, u32[]{:S(2)}) collective-permute-start(bf16[160,2048]{1,0:T(8,128)(2,1)S(1)} %pad_maximum_fusion.9), channel_id=1, source_target_pairs={{0,2},{1,3},{2,0},{3,1},{4,6},{5,7},{6,4},{7,5},{8,10},{9,11},{10,... | collective-permute-start | bytes 1966088 | tf_op jit(solution)/shard_map/grads_b/ppermute | solution.py:12
  75.8 4.7 %collective-permute-done.10 = bf16[160,2048]{1,0:T(8,128)(2,1)S(1)} collective-permute-done((bf16[160,2048]{1,0:T(8,128)(2,1)S(1)}, bf16[160,2048]{1,0:T(8,128)(2,1)S(1)}, u32[]{:S(2)}, u32[]{:S(2)}) %collective-permute-start.10) | collective-permute-done | bytes 655392 | tf_op jit(solution)/shard_map/grads_a/ppermute | solution.py:12
  80.5 1.4 multiply_convert_fusion.4
  83.1 1.4 fusion.94
  85.2 9.4 %collective-permute-done.16 = bf16[160,2048]{1,0:T(8,128)(2,1)S(1)} collective-permute-done((bf16[160,2048]{1,0:T(8,128)(2,1)S(1)}, bf16[160,2048]{1,0:T(8,128)(2,1)S(1)}, u32[]{:S(2)}, u32[]{:S(2)}) %collective-permute-start.16) | collective-permute-done | bytes 655392 | tf_op jit(solution)/shard_map/grads_b/ppermute | solution.py:12
  94.6 1.4 multiply_convert_fusion.2
  98.9 2.7 %collective-permute-done.19 = bf16[80,2048]{1,0:T(8,128)(2,1)S(1)} collective-permute-done((bf16[80,2048]{1,0:T(8,128)(2,1)S(1)}, bf16[80,2048]{1,0:T(8,128)(2,1)S(1)}, u32[]{:S(2)}, u32[]{:S(2)}) %collective-permute-start.19) | collective-permute-done | bytes 327712 | tf_op jit(solution)/shard_map/sums_z2/ppermute | solution.py:12
  101.7 2.3 %collective-permute-start.21 = (bf16[40,2048]{1,0:T(8,128)(2,1)S(1)}, bf16[40,2048]{1,0:T(8,128)(2,1)S(1)}, u32[]{:S(2)}, u32[]{:S(2)}) collective-permute-start(bf16[40,2048]{1,0:T(8,128)(2,1)S(1)} %get-tuple-element.99), channel_id=1, source_target_pairs={{0,16},{4,20},{8,24},{12,28},{16,0},{20,4},{24,8},{28,12},{1,17},{... | collective-permute-start | bytes 491528 | tf_op jit(solution)/shard_map/R4/ppermute | solution.py:12
  104.0 1.4 collective-permute-start.22
  106.2 2.6 %convolution_convert_fusion = bf16[704,2048]{1,0:T(8,128)(2,1)S(1)} fusion(bf16[640,2048]{1,0:T(8,128)(2,1)S(1)} %get-tuple-element.81, bf16[640,352]{1,0:T(8,128)(2,1)S(1)} %slice.256, bf16[640,352]{1,0:T(8,128)(2,1)S(1)} %slice.255), kind=kOutput, calls=%fused_computation.1 | convolution fusion | flops 1848737792 | bytes 6406144 | tf_op jit(solution)/shard_map/dot_general | solution.py:20
  112.2 11.6 %collective-permute-done.20 = bf16[160,2048]{1,0:T(8,128)(2,1)S(1)} collective-permute-done((bf16[160,2048]{1,0:T(8,128)(2,1)S(1)}, bf16[160,2048]{1,0:T(8,128)(2,1)S(1)}, u32[]{:S(2)}, u32[]{:S(2)}) %collective-permute-start.20) | collective-permute-done | bytes 655392 | tf_op jit(solution)/shard_map/sums_near/ppermute | solution.py:12
  123.9 3.1 %collective-permute-start.27 = (bf16[40,2048]{1,0:T(8,128)(2,1)S(1)}, bf16[40,2048]{1,0:T(8,128)(2,1)S(1)}, u32[]{:S(2)}, u32[]{:S(2)}) collective-permute-start(bf16[40,2048]{1,0:T(8,128)(2,1)S(1)} %get-tuple-element.96), channel_id=1, source_target_pairs={{0,24},{4,28},{8,16},{12,20},{16,8},{20,12},{24,0},{28,4},{1,25},{... | collective-permute-start | bytes 491528 | tf_op jit(solution)/shard_map/R6/ppermute | solution.py:12
  126.9 2.2 %collective-permute-start.28 = (bf16[40,2048]{1,0:T(8,128)(2,1)S(1)}, bf16[40,2048]{1,0:T(8,128)(2,1)S(1)}, u32[]{:S(2)}, u32[]{:S(2)}) collective-permute-start(bf16[40,2048]{1,0:T(8,128)(2,1)S(1)} %get-tuple-element.97), channel_id=1, source_target_pairs={{0,28},{4,24},{8,20},{12,16},{16,12},{20,8},{24,4},{28,0},{1,29},{... | collective-permute-start | bytes 491528 | tf_op jit(solution)/shard_map/R7/ppermute | solution.py:12
  129.6 1.6 %collective-permute-done.24 = bf16[1056,2048]{1,0:T(8,128)(2,1)S(1)} collective-permute-done((bf16[1056,2048]{1,0:T(8,128)(2,1)S(1)}, bf16[1056,2048]{1,0:T(8,128)(2,1)S(1)}, u32[]{:S(2)}, u32[]{:S(2)}) %collective-permute-start.24) | collective-permute-done | bytes 4325408 | tf_op jit(solution)/shard_map/weight_grads/ppermute | solution.py:12
  131.1 1.9 %collective-permute-start.26 = (bf16[40,2048]{1,0:T(8,128)(2,1)S(1)}, bf16[40,2048]{1,0:T(8,128)(2,1)S(1)}, u32[]{:S(2)}, u32[]{:S(2)}) collective-permute-start(bf16[40,2048]{1,0:T(8,128)(2,1)S(1)} %get-tuple-element.67), channel_id=1, source_target_pairs={{0,12},{4,8},{8,4},{12,0},{16,28},{20,24},{24,20},{28,16},{1,13},{... | collective-permute-start | bytes 491528 | tf_op jit(solution)/shard_map/returned_3/ppermute | solution.py:12
  133.0 2.4 %fusion.3 = bf16[1,352,2048]{2,1,0:T(8,128)(2,1)} fusion(bf16[640,2048]{1,0:T(8,128)(2,1)S(1)} %constant_dynamic-update-slice_fusion.22, bf16[1056,2048]{1,0:T(8,128)(2,1)S(1)} %collective-permute-done.24, bf16[640,704]{1,0:T(8,128)(2,1)S(1)} %constant_dynamic-update-slice_fusion.20), kind=kOutput, calls=%fused_computation.14 | convolution fusion | flops 924909568 | bytes 5996544 | tf_op jit(solution)/shard_map/dot_general | solution.py:20
  135.4 2.4 %fusion.4 = bf16[1,2048,352]{1,2,0:T(8,128)(2,1)} fusion(bf16[640,2048]{1,0:T(8,128)(2,1)S(1)} %get-tuple-element.81, bf16[1056,2048]{1,0:T(8,128)(2,1)S(1)} %collective-permute-done.24, bf16[640,704]{1,0:T(8,128)(2,1)S(1)} %constant_dynamic-update-slice_fusion.18), kind=kOutput, calls=%fused_computation.15 | convolution fusion | flops 924909568 | bytes 5996544 | tf_op jit(solution)/shard_map/dot_general | solution.py:20
  137.9 2.4 %fusion.5 = bf16[1,2048,352]{1,2,0:T(8,128)(2,1)} fusion(bf16[640,2048]{1,0:T(8,128)(2,1)S(1)} %get-tuple-element.81, bf16[1056,2048]{1,0:T(8,128)(2,1)S(1)} %collective-permute-done.24, bf16[640,704]{1,0:T(8,128)(2,1)S(1)} %constant_dynamic-update-slice_fusion.8), kind=kOutput, calls=%fused_computation.16 | convolution fusion | flops 924909568 | bytes 5996544 | tf_op jit(solution)/shard_map/dot_general | solution.py:20
  140.3 4.0 %collective-permute-done.26 = bf16[40,2048]{1,0:T(8,128)(2,1)S(1)} collective-permute-done((bf16[40,2048]{1,0:T(8,128)(2,1)S(1)}, bf16[40,2048]{1,0:T(8,128)(2,1)S(1)}, u32[]{:S(2)}, u32[]{:S(2)}) %collective-permute-start.26) | collective-permute-done | bytes 163872 | tf_op jit(solution)/shard_map/returned_3/ppermute | solution.py:12
  (130 shorter events, 33.2 us)
Async XLA Ops:
  0.6 11.3 %copy-start.5 = (s32[128,2]{0,1:T(2,128)S(1)}, s32[128,2]{0,1:T(2,128)}, u32[]{:S(2)}) copy-start(s32[128,2]{0,1:T(2,128)} %param.14) | copy-start | bytes 3076
  0.7 12.1 %copy-start.3 = (bf16[128,2048]{1,0:T(8,128)(2,1)S(1)}, bf16[128,2048]{1,0:T(8,128)(2,1)}, u32[]{:S(2)}) copy-start(bf16[128,2048]{1,0:T(8,128)(2,1)} %param.11) | copy-start | bytes 1572868
  0.7 17.3 %collective-permute-start.1 = (bf16[2048,352]{0,1:T(8,128)(2,1)}, bf16[2048,352]{0,1:T(8,128)(2,1)S(1)}, u32[]{:S(2)}, u32[]{:S(2)}) collective-permute-start(bf16[2048,352]{0,1:T(8,128)(2,1)} %bitcast.95), channel_id=1, source_target_pairs={{0,1},{1,0},{2,3},{3,2},{4,5},{5,4},{6,7},{7,6},{8,9},{9,8},{10,11... | collective-permute-start | bytes 4325384 | tf_op jit(solution)/shard_map/gate_weight/ppermute | solution.py:12
  1.2 15.4 %collective-permute-start = (bf16[128,2048]{1,0:T(8,128)(2,1)}, bf16[128,2048]{1,0:T(8,128)(2,1)}, u32[]{:S(2)}, u32[]{:S(2)}) collective-permute-start(bf16[128,2048]{1,0:T(8,128)(2,1)} %param.12), channel_id=1, source_target_pairs={{0,2},{1,3},{2,0},{3,1},{4,6},{5,7},{6,4},{7,5},{8,10},{9,11},{10,... | collective-permute-start | bytes 1572872 | tf_op jit(solution)/shard_map/teacher_across/ppermute | solution.py:12
  5.8 13.6 %collective-permute-start.4 = (bf16[120,2048]{1,0:T(8,128)(2,1)}, bf16[120,2048]{1,0:T(8,128)(2,1)}, u32[]{:S(2)}, u32[]{:S(2)}) collective-permute-start(bf16[120,2048]{1,0:T(8,128)(2,1)} %convolution_convert_fusion.3), channel_id=1, source_target_pairs={{0,4},{4,0},{8,12},{12,8},{16,20},{20,16},{24,28},{28,24},{1,5},{5... | collective-permute-start | bytes 1474568 | tf_op jit(solution)/shard_map/inputs_side/ppermute | solution.py:12
  8.2 17.6 %collective-permute-start.5 = (bf16[40,2048]{1,0:T(8,128)(2,1)}, bf16[40,2048]{1,0:T(8,128)(2,1)S(1)}, u32[]{:S(2)}, u32[]{:S(2)}) collective-permute-start(bf16[40,2048]{1,0:T(8,128)(2,1)} %convolution_convert_fusion.9), channel_id=1, source_target_pairs={{0,16},{4,20},{8,24},{12,28},{16,0},{20,4},{24,8},{28,12},{1,17},{... | collective-permute-start | bytes 491528 | tf_op jit(solution)/shard_map/inputs_far_4/ppermute | solution.py:12
  11.7 14.1 %collective-permute-start.6 = (bf16[40,2048]{1,0:T(8,128)(2,1)}, bf16[40,2048]{1,0:T(8,128)(2,1)S(1)}, u32[]{:S(2)}, u32[]{:S(2)}) collective-permute-start(bf16[40,2048]{1,0:T(8,128)(2,1)} %convolution_convert_fusion.8), channel_id=1, source_target_pairs={{0,20},{4,16},{8,28},{12,24},{16,4},{20,0},{24,12},{28,8},{1,21},{... | collective-permute-start | bytes 491528 | tf_op jit(solution)/shard_map/inputs_far_5/ppermute | solution.py:12
  17.9 3.4 %collective-permute-start.2 = (bf16[256,2048]{1,0:T(8,128)(2,1)S(1)}, bf16[256,2048]{1,0:T(8,128)(2,1)S(1)}, u32[]{:S(2)}, u32[]{:S(2)}) collective-permute-start(bf16[256,2048]{1,0:T(8,128)(2,1)S(1)} %pad_maximum_fusion.6), channel_id=1, source_target_pairs={{0,1},{1,0},{2,3},{3,2},{4,5},{5,4},{6,7},{7,6},{8,9},{9,8},{10,11... | collective-permute-start | bytes 3145736 | tf_op jit(solution)/shard_map/teacher_beside/ppermute | solution.py:12
  21.3 29.8 %collective-permute-start.13 = (bf16[2048,352]{0,1:T(8,128)(2,1)S(1)}, bf16[2048,352]{0,1:T(8,128)(2,1)S(1)}, u32[]{:S(2)}, u32[]{:S(2)}) collective-permute-start(bf16[2048,352]{0,1:T(8,128)(2,1)S(1)} %bitcast.105), channel_id=1, source_target_pairs={{0,1},{1,0},{2,3},{3,2},{4,5},{5,4},{6,7},{7,6},{8,9},{9,8},{10,11... | collective-permute-start | bytes 4325384 | tf_op jit(solution)/shard_map/up_weight/ppermute | solution.py:12
  23.1 15.1 %copy-start.6 = (bf16[1,352,2048]{2,1,0:T(8,128)(2,1)S(1)}, bf16[1,352,2048]{2,1,0:T(8,128)(2,1)}, u32[]{:S(2)}) copy-start(bf16[1,352,2048]{2,1,0:T(8,128)(2,1)} %param.19) | copy-start | bytes 4325380
  23.1 21.1 %collective-permute-start.3 = (bf16[160,2048]{1,0:T(8,128)(2,1)S(1)}, bf16[160,2048]{1,0:T(8,128)(2,1)S(1)}, u32[]{:S(2)}, u32[]{:S(2)}) collective-permute-start(bf16[160,2048]{1,0:T(8,128)(2,1)S(1)} %convolution_convert_fusion.2), channel_id=1, source_target_pairs={{0,4},{4,0},{8,12},{12,8},{16,20},{20,16},{24,28},{28,24},{1,5},{5... | collective-permute-start | bytes 1966088 | tf_op jit(solution)/shard_map/grads_side/ppermute | solution.py:12
  25.8 12.4 %collective-permute-start.7 = (bf16[80,2048]{1,0:T(8,128)(2,1)S(1)}, bf16[80,2048]{1,0:T(8,128)(2,1)S(1)}, u32[]{:S(2)}, u32[]{:S(2)}) collective-permute-start(bf16[80,2048]{1,0:T(8,128)(2,1)S(1)} %get-tuple-element.41), channel_id=1, source_target_pairs={{0,24},{4,28},{8,16},{12,20},{16,8},{20,12},{24,0},{28,4},{1,25},{... | collective-permute-start | bytes 983048 | tf_op jit(solution)/shard_map/inputs_z3/ppermute | solution.py:12
  29.3 14.9 %collective-permute-start.8 = (bf16[80,2048]{1,0:T(8,128)(2,1)S(1)}, bf16[80,2048]{1,0:T(8,128)(2,1)S(1)}, u32[]{:S(2)}, u32[]{:S(2)}) collective-permute-start(bf16[80,2048]{1,0:T(8,128)(2,1)S(1)} %get-tuple-element.43), channel_id=1, source_target_pairs={{0,8},{4,12},{8,0},{12,4},{16,24},{20,28},{24,16},{28,20},{1,9},{5... | collective-permute-start | bytes 983048 | tf_op jit(solution)/shard_map/inputs_z1/ppermute | solution.py:12
  31.9 17.4 %collective-permute-start.12 = (bf16[160,2048]{1,0:T(8,128)(2,1)S(1)}, bf16[160,2048]{1,0:T(8,128)(2,1)S(1)}, u32[]{:S(2)}, u32[]{:S(2)}) collective-permute-start(bf16[160,2048]{1,0:T(8,128)(2,1)S(1)} %pad_maximum_fusion.8), channel_id=1, source_target_pairs={{0,2},{1,3},{2,0},{3,1},{4,6},{5,7},{6,4},{7,5},{8,10},{9,11},{10,... | collective-permute-start | bytes 1966088 | tf_op jit(solution)/shard_map/inputs_a/ppermute | solution.py:12
  38.2 37.5 %collective-permute-start.11 = (bf16[352,2048]{1,0:T(8,128)(2,1)S(1)}, bf16[352,2048]{1,0:T(8,128)(2,1)S(1)}, u32[]{:S(2)}, u32[]{:S(2)}) collective-permute-start(bf16[352,2048]{1,0:T(8,128)(2,1)S(1)} %bitcast.102), channel_id=1, source_target_pairs={{0,1},{1,0},{2,3},{3,2},{4,5},{5,4},{6,7},{7,6},{8,9},{9,8},{10,11... | collective-permute-start | bytes 4325384 | tf_op jit(solution)/shard_map/down_weight/ppermute | solution.py:12
  44.4 18.2 %collective-permute-start.9 = (bf16[80,2048]{1,0:T(8,128)(2,1)S(1)}, bf16[80,2048]{1,0:T(8,128)(2,1)S(1)}, u32[]{:S(2)}, u32[]{:S(2)}) collective-permute-start(bf16[80,2048]{1,0:T(8,128)(2,1)S(1)} %pad_maximum_fusion.12), channel_id=1, source_target_pairs={{0,16},{4,20},{8,24},{12,28},{16,0},{20,4},{24,8},{28,12},{1,17},{... | collective-permute-start | bytes 983048 | tf_op jit(solution)/shard_map/grads_z2/ppermute | solution.py:12
  47.3 21.9 %collective-permute-start.14 = (bf16[80,2048]{1,0:T(8,128)(2,1)S(1)}, bf16[80,2048]{1,0:T(8,128)(2,1)S(1)}, u32[]{:S(2)}, u32[]{:S(2)}) collective-permute-start(bf16[80,2048]{1,0:T(8,128)(2,1)S(1)} %pad_maximum_fusion.15), channel_id=1, source_target_pairs={{0,8},{4,12},{8,0},{12,4},{16,24},{20,28},{24,16},{28,20},{1,9},{5... | collective-permute-start | bytes 983048 | tf_op jit(solution)/shard_map/grads_z1/ppermute | solution.py:12
  49.3 17.2 %collective-permute-start.17 = (bf16[160,2048]{1,0:T(8,128)(2,1)S(1)}, bf16[160,2048]{1,0:T(8,128)(2,1)S(1)}, u32[]{:S(2)}, u32[]{:S(2)}) collective-permute-start(bf16[160,2048]{1,0:T(8,128)(2,1)S(1)} %pad_maximum_fusion.10), channel_id=1, source_target_pairs={{0,2},{1,3},{2,0},{3,1},{4,6},{5,7},{6,4},{7,5},{8,10},{9,11},{10,... | collective-permute-start | bytes 1966088 | tf_op jit(solution)/shard_map/inputs_b/ppermute | solution.py:12
  62.6 17.9 %collective-permute-start.10 = (bf16[160,2048]{1,0:T(8,128)(2,1)S(1)}, bf16[160,2048]{1,0:T(8,128)(2,1)S(1)}, u32[]{:S(2)}, u32[]{:S(2)}) collective-permute-start(bf16[160,2048]{1,0:T(8,128)(2,1)S(1)} %pad_maximum_fusion.7), channel_id=1, source_target_pairs={{0,2},{1,3},{2,0},{3,1},{4,6},{5,7},{6,4},{7,5},{8,10},{9,11},{10,... | collective-permute-start | bytes 1966088 | tf_op jit(solution)/shard_map/grads_a/ppermute | solution.py:12
  63.2 10.9 %collective-permute-start.15 = (bf16[80,2048]{1,0:T(8,128)(2,1)S(1)}, bf16[80,2048]{1,0:T(8,128)(2,1)S(1)}, u32[]{:S(2)}, u32[]{:S(2)}) collective-permute-start(bf16[80,2048]{1,0:T(8,128)(2,1)S(1)} %pad_maximum_fusion.16), channel_id=1, source_target_pairs={{0,24},{4,28},{8,16},{12,20},{16,8},{20,12},{24,0},{28,4},{1,25},{... | collective-permute-start | bytes 983048 | tf_op jit(solution)/shard_map/grads_z3/ppermute | solution.py:12
  74.2 20.4 %collective-permute-start.16 = (bf16[160,2048]{1,0:T(8,128)(2,1)S(1)}, bf16[160,2048]{1,0:T(8,128)(2,1)S(1)}, u32[]{:S(2)}, u32[]{:S(2)}) collective-permute-start(bf16[160,2048]{1,0:T(8,128)(2,1)S(1)} %pad_maximum_fusion.9), channel_id=1, source_target_pairs={{0,2},{1,3},{2,0},{3,1},{4,6},{5,7},{6,4},{7,5},{8,10},{9,11},{10,... | collective-permute-start | bytes 1966088 | tf_op jit(solution)/shard_map/grads_b/ppermute | solution.py:12
  84.6 16.9 %collective-permute-start.19 = (bf16[80,2048]{1,0:T(8,128)(2,1)S(1)}, bf16[80,2048]{1,0:T(8,128)(2,1)S(1)}, u32[]{:S(2)}, u32[]{:S(2)}) collective-permute-start(bf16[80,2048]{1,0:T(8,128)(2,1)S(1)} %get-tuple-element.77), channel_id=1, source_target_pairs={{0,2},{1,3},{2,0},{3,1},{4,6},{5,7},{6,4},{7,5},{8,10},{9,11},{10,... | collective-permute-start | bytes 983048 | tf_op jit(solution)/shard_map/sums_z2/ppermute | solution.py:12
  98.5 11.8 %collective-permute-start.18 = (bf16[80,2048]{1,0:T(8,128)(2,1)S(1)}, bf16[80,2048]{1,0:T(8,128)(2,1)S(1)}, u32[]{:S(2)}, u32[]{:S(2)}) collective-permute-start(bf16[80,2048]{1,0:T(8,128)(2,1)S(1)} %get-tuple-element.74), channel_id=1, source_target_pairs={{0,2},{1,3},{2,0},{3,1},{4,6},{5,7},{6,4},{7,5},{8,10},{9,11},{10,... | collective-permute-start | bytes 983048 | tf_op jit(solution)/shard_map/sums_z3/ppermute | solution.py:12
  101.7 22.1 %collective-permute-start.21 = (bf16[40,2048]{1,0:T(8,128)(2,1)S(1)}, bf16[40,2048]{1,0:T(8,128)(2,1)S(1)}, u32[]{:S(2)}, u32[]{:S(2)}) collective-permute-start(bf16[40,2048]{1,0:T(8,128)(2,1)S(1)} %get-tuple-element.99), channel_id=1, source_target_pairs={{0,16},{4,20},{8,24},{12,28},{16,0},{20,4},{24,8},{28,12},{1,17},{... | collective-permute-start | bytes 491528 | tf_op jit(solution)/shard_map/R4/ppermute | solution.py:12
  104.0 19.8 %collective-permute-start.22 = (bf16[40,2048]{1,0:T(8,128)(2,1)S(1)}, bf16[40,2048]{1,0:T(8,128)(2,1)S(1)}, u32[]{:S(2)}, u32[]{:S(2)}) collective-permute-start(bf16[40,2048]{1,0:T(8,128)(2,1)S(1)} %get-tuple-element.98), channel_id=1, source_target_pairs={{0,20},{4,16},{8,28},{12,24},{16,4},{20,0},{24,12},{28,8},{1,21},{... | collective-permute-start | bytes 491528 | tf_op jit(solution)/shard_map/R5/ppermute | solution.py:12
  110.3 13.5 %collective-permute-start.20 = (bf16[160,2048]{1,0:T(8,128)(2,1)S(1)}, bf16[160,2048]{1,0:T(8,128)(2,1)S(1)}, u32[]{:S(2)}, u32[]{:S(2)}) collective-permute-start(bf16[160,2048]{1,0:T(8,128)(2,1)S(1)} %pad_maximum_fusion.11), channel_id=1, source_target_pairs={{0,2},{1,3},{2,0},{3,1},{4,6},{5,7},{6,4},{7,5},{8,10},{9,11},{10,... | collective-permute-start | bytes 1966088 | tf_op jit(solution)/shard_map/sums_near/ppermute | solution.py:12
  123.8 7.3 %collective-permute-start.24 = (bf16[1056,2048]{1,0:T(8,128)(2,1)S(1)}, bf16[1056,2048]{1,0:T(8,128)(2,1)S(1)}, u32[]{:S(2)}, u32[]{:S(2)}) collective-permute-start(bf16[1056,2048]{1,0:T(8,128)(2,1)S(1)} %pad_maximum_fusion), channel_id=1, source_target_pairs={{0,1},{1,0},{2,3},{3,2},{4,5},{5,4},{6,7},{7,6},{8,9},{9,8},{10,11... | collective-permute-start | bytes 12976136 | tf_op jit(solution)/shard_map/weight_grads/ppermute | solution.py:12
  123.9 16.5 %collective-permute-start.27 = (bf16[40,2048]{1,0:T(8,128)(2,1)S(1)}, bf16[40,2048]{1,0:T(8,128)(2,1)S(1)}, u32[]{:S(2)}, u32[]{:S(2)}) collective-permute-start(bf16[40,2048]{1,0:T(8,128)(2,1)S(1)} %get-tuple-element.96), channel_id=1, source_target_pairs={{0,24},{4,28},{8,16},{12,20},{16,8},{20,12},{24,0},{28,4},{1,25},{... | collective-permute-start | bytes 491528 | tf_op jit(solution)/shard_map/R6/ppermute | solution.py:12
  126.9 13.4 %collective-permute-start.28 = (bf16[40,2048]{1,0:T(8,128)(2,1)S(1)}, bf16[40,2048]{1,0:T(8,128)(2,1)S(1)}, u32[]{:S(2)}, u32[]{:S(2)}) collective-permute-start(bf16[40,2048]{1,0:T(8,128)(2,1)S(1)} %get-tuple-element.97), channel_id=1, source_target_pairs={{0,28},{4,24},{8,20},{12,16},{16,12},{20,8},{24,4},{28,0},{1,29},{... | collective-permute-start | bytes 491528 | tf_op jit(solution)/shard_map/R7/ppermute | solution.py:12
  129.3 15.3 %collective-permute-start.23 = (bf16[40,2048]{1,0:T(8,128)(2,1)S(1)}, bf16[40,2048]{1,0:T(8,128)(2,1)S(1)}, u32[]{:S(2)}, u32[]{:S(2)}) collective-permute-start(bf16[40,2048]{1,0:T(8,128)(2,1)S(1)} %get-tuple-element.57), channel_id=1, source_target_pairs={{0,4},{4,0},{8,12},{12,8},{16,20},{20,16},{24,28},{28,24},{1,5},{5... | collective-permute-start | bytes 491528 | tf_op jit(solution)/shard_map/returned_1/ppermute | solution.py:12
  129.5 10.8 %collective-permute-start.25 = (bf16[40,2048]{1,0:T(8,128)(2,1)S(1)}, bf16[40,2048]{1,0:T(8,128)(2,1)S(1)}, u32[]{:S(2)}, u32[]{:S(2)}) collective-permute-start(bf16[40,2048]{1,0:T(8,128)(2,1)S(1)} %get-tuple-element.66), channel_id=1, source_target_pairs={{0,8},{4,12},{8,0},{12,4},{16,24},{20,28},{24,16},{28,20},{1,9},{5... | collective-permute-start | bytes 491528 | tf_op jit(solution)/shard_map/returned_2/ppermute | solution.py:12
  131.1 13.2 %collective-permute-start.26 = (bf16[40,2048]{1,0:T(8,128)(2,1)S(1)}, bf16[40,2048]{1,0:T(8,128)(2,1)S(1)}, u32[]{:S(2)}, u32[]{:S(2)}) collective-permute-start(bf16[40,2048]{1,0:T(8,128)(2,1)S(1)} %get-tuple-element.67), channel_id=1, source_target_pairs={{0,12},{4,8},{8,4},{12,0},{16,28},{20,24},{24,20},{28,16},{1,13},{... | collective-permute-start | bytes 491528 | tf_op jit(solution)/shard_map/returned_3/ppermute | solution.py:12
  (7 other events, 39.2 us)

commit v6 on v5

--- a/solution.py
+++ b/solution.py
@@ -140,8 +140,8 @@
         xa = jnp.concatenate(after([x_own, x_side[:c]] + x_far, g_send), axis=0)
         g_side = flip(g_send, "expert", 1, "grads_side")
         ya = flip(xa, "dp", 2, "inputs_a")
-        x_z3 = flip(after(jnp.concatenate([near6, x_side[2 * c :]], axis=0), x_far, g_send), "expert", 6, "inputs_z3")
-        x_z1 = flip(after(jnp.concatenate([near2, x_side[c : 2 * c]], axis=0), x_far, g_send), "expert", 2, "inputs_z1")
+        x_z3 = flip(after(jnp.concatenate([near6, x_side[2 * c :]], axis=0), g_send), "expert", 6, "inputs_z3")
+        x_z1 = flip(after(jnp.concatenate([near2, x_side[c : 2 * c]], axis=0), g_send), "expert", 2, "inputs_z1")
         g_own, gear2, gear4, gear6 = [spread(weighted[k], cotangent) for k in (0, 2, 4, 6)]
         xb = jnp.concatenate([x_z1, x_z3], axis=0)
 

time: 145 us -> 145 us (level)
  waiting for transfers between devices: 66.9 us -> 65.2 us
    ppermute x29, waiting for transfers between devices: 66.9 us -> 65.2 us  [flip(): lax.ppermute(block, axis, [(i, i ^ shift) for i in range(lax.axis_size(ax...]
  transfers between devices with their start and end apart: 29 -> 29, of which waited for: 15 -> 13; matrix products, arithmetic and copies ran while one was open for 25% -> 26% of each run, Pallas kernels for 0% -> 0%
where the time goes in v6:
time: 145 us; the launch traced here: 144 us
  waiting for transfers between devices  65.2 us (45%)
  starting transfers between devices  37.9 us (26%)
  matrix products  32.8 us (23%)
  other arithmetic  3.44 us (2%)
  local copies, waits for them, and re-layouts  3 us (2%)
  between operations  2.04 us (1%)
    ppermute x29, waiting for transfers between devices, flip(): lax.ppermute(block, axis, [(i, i ^ shift) for i in range(lax.axis_size(ax...  65.2 us
    ppermute x29, starting transfers between devices, flip(): lax.ppermute(block, axis, [(i, i ^ shift) for i in range(lax.axis_size(ax...  37.9 us
    dot_general x7, matrix products, by_rows(): lax.dot_general(left, right, (((0,), (0,)), ((), ())), preferred_element_...  12.7 us
    dot_general x6, matrix products, by_columns(): lax.dot_general(left, right, (((1,), (1,)), ((), ())), preferred_element_...  7.89 us
    dot_general x11, matrix products, spread(): return jnp.dot(matrices, rows, preferred_element_type=F32).astype(BF16)  5.46 us
  transfers between devices with their start and end apart: 29, of which 13 were waited for; matrix products, arithmetic and copies ran while one was open for 26% of the time, Pallas kernels for 0%

profile of v6, /device:TPU:0, one launch (start us, length us, event | category | flops | bytes accessed | tf_op | source)
XLA Modules:
  0.0 144.4 jit_solution(8477352910393283866)
XLA Ops:
  1.2 2.6 %collective-permute-start = (bf16[128,2048]{1,0:T(8,128)(2,1)}, bf16[128,2048]{1,0:T(8,128)(2,1)}, u32[]{:S(2)}, u32[]{:S(2)}) collective-permute-start(bf16[128,2048]{1,0:T(8,128)(2,1)} %param.12), channel_id=1, source_target_pairs={{0,2},{1,3},{2,0},{3,1},{4,6},{5,7},{6,4},{7,5},{8,10},{9,11},{10,... | collective-permute-start | bytes 1572872 | tf_op jit(solution)/shard_map/teacher_across/ppermute | solution.py:12
  5.8 1.5 %collective-permute-start.4 = (bf16[120,2048]{1,0:T(8,128)(2,1)}, bf16[120,2048]{1,0:T(8,128)(2,1)}, u32[]{:S(2)}, u32[]{:S(2)}) collective-permute-start(bf16[120,2048]{1,0:T(8,128)(2,1)} %convolution_convert_fusion.3), channel_id=1, source_target_pairs={{0,4},{4,0},{8,12},{12,8},{16,20},{20,16},{24,28},{28,24},{1,5},{5... | collective-permute-start | bytes 1474568 | tf_op jit(solution)/shard_map/inputs_side/ppermute | solution.py:12
  8.2 2.6 %collective-permute-start.10 = (bf16[40,2048]{1,0:T(8,128)(2,1)}, bf16[40,2048]{1,0:T(8,128)(2,1)S(1)}, u32[]{:S(2)}, u32[]{:S(2)}) collective-permute-start(bf16[40,2048]{1,0:T(8,128)(2,1)} %convolution_convert_fusion.7), channel_id=1, source_target_pairs={{0,16},{4,20},{8,24},{12,28},{16,0},{20,4},{24,8},{28,12},{1,17},{... | collective-permute-start | bytes 491528 | tf_op jit(solution)/shard_map/inputs_far_4/ppermute | solution.py:12
  13.1 3.6 %collective-permute-done = bf16[128,2048]{1,0:T(8,128)(2,1)} collective-permute-done((bf16[128,2048]{1,0:T(8,128)(2,1)}, bf16[128,2048]{1,0:T(8,128)(2,1)}, u32[]{:S(2)}, u32[]{:S(2)}) %collective-permute-start) | collective-permute-done | bytes 524320 | tf_op jit(solution)/shard_map/teacher_across/ppermute | solution.py:12
  18.0 1.4 collective-permute-done.4
  21.4 1.6 %fusion.7 = bf16[128,2048]{0,1:T(8,128)(2,1)S(1)} fusion(bf16[128,128]{1,0:T(8,128)(2,1)S(1)} %copy-done.8, bf16[128,2048]{0,1:T(8,128)(2,1)S(1)} %copy.15, bf16[128,2048]{1,0:T(8,128)(2,1)} %collective-permute-done, bf16[256,2048]{1,0:T(8,128)(2,1)S(1)} %collective-permute-done.2, bf16[128,2048]{1,0:T(8,128)(2,1)S(1)} %copy-done.4, pred[]{:T(512)S(6)} %eq.46, ...), kind=kOutput, calls=%fused_computation.21 | convolution fusion | flops 68681728 | bytes 3178499 | tf_op jit(solution)/shard_map/dot_general | solution.py:137
  24.7 3.6 %collective-permute-start.5 = (bf16[80,2048]{1,0:T(8,128)(2,1)S(1)}, bf16[80,2048]{1,0:T(8,128)(2,1)S(1)}, u32[]{:S(2)}, u32[]{:S(2)}) collective-permute-start(bf16[80,2048]{1,0:T(8,128)(2,1)S(1)} %get-tuple-element.39), channel_id=1, source_target_pairs={{0,24},{4,28},{8,16},{12,20},{16,8},{20,12},{24,0},{28,4},{1,25},{... | collective-permute-start | bytes 983048 | tf_op jit(solution)/shard_map/inputs_z3/ppermute | solution.py:12
  28.7 3.1 %collective-permute-start.6 = (bf16[80,2048]{1,0:T(8,128)(2,1)S(1)}, bf16[80,2048]{1,0:T(8,128)(2,1)S(1)}, u32[]{:S(2)}, u32[]{:S(2)}) collective-permute-start(bf16[80,2048]{1,0:T(8,128)(2,1)S(1)} %get-tuple-element.41), channel_id=1, source_target_pairs={{0,8},{4,12},{8,0},{12,4},{16,24},{20,28},{24,16},{28,20},{1,9},{5... | collective-permute-start | bytes 983048 | tf_op jit(solution)/shard_map/inputs_z1/ppermute | solution.py:12
  33.0 3.9 %collective-permute-done.5 = bf16[80,2048]{1,0:T(8,128)(2,1)S(1)} collective-permute-done((bf16[80,2048]{1,0:T(8,128)(2,1)S(1)}, bf16[80,2048]{1,0:T(8,128)(2,1)S(1)}, u32[]{:S(2)}, u32[]{:S(2)}) %collective-permute-start.5) | collective-permute-done | bytes 327712 | tf_op jit(solution)/shard_map/inputs_z3/ppermute | solution.py:12
  37.2 6.9 %collective-permute-done.6 = bf16[80,2048]{1,0:T(8,128)(2,1)S(1)} collective-permute-done((bf16[80,2048]{1,0:T(8,128)(2,1)S(1)}, bf16[80,2048]{1,0:T(8,128)(2,1)S(1)}, u32[]{:S(2)}, u32[]{:S(2)}) %collective-permute-start.6) | collective-permute-done | bytes 327712 | tf_op jit(solution)/shard_map/inputs_z1/ppermute | solution.py:12
  44.3 2.8 %collective-permute-start.7 = (bf16[80,2048]{1,0:T(8,128)(2,1)S(1)}, bf16[80,2048]{1,0:T(8,128)(2,1)S(1)}, u32[]{:S(2)}, u32[]{:S(2)}) collective-permute-start(bf16[80,2048]{1,0:T(8,128)(2,1)S(1)} %pad_maximum_fusion.12), channel_id=1, source_target_pairs={{0,16},{4,20},{8,24},{12,28},{16,0},{20,4},{24,8},{28,12},{1,17},{... | collective-permute-start | bytes 983048 | tf_op jit(solution)/shard_map/grads_z2/ppermute | solution.py:12
  47.1 1.5 %collective-permute-start.14 = (bf16[80,2048]{1,0:T(8,128)(2,1)S(1)}, bf16[80,2048]{1,0:T(8,128)(2,1)S(1)}, u32[]{:S(2)}, u32[]{:S(2)}) collective-permute-start(bf16[80,2048]{1,0:T(8,128)(2,1)S(1)} %pad_maximum_fusion.15), channel_id=1, source_target_pairs={{0,8},{4,12},{8,0},{12,4},{16,24},{20,28},{24,16},{28,20},{1,9},{5... | collective-permute-start | bytes 983048 | tf_op jit(solution)/shard_map/grads_z1/ppermute | solution.py:12
  52.2 10.4 %collective-permute-done.7 = bf16[80,2048]{1,0:T(8,128)(2,1)S(1)} collective-permute-done((bf16[80,2048]{1,0:T(8,128)(2,1)S(1)}, bf16[80,2048]{1,0:T(8,128)(2,1)S(1)}, u32[]{:S(2)}, u32[]{:S(2)}) %collective-permute-start.7) | collective-permute-done | bytes 327712 | tf_op jit(solution)/shard_map/grads_z2/ppermute | solution.py:12
  63.7 2.6 %collective-permute-start.15 = (bf16[80,2048]{1,0:T(8,128)(2,1)S(1)}, bf16[80,2048]{1,0:T(8,128)(2,1)S(1)}, u32[]{:S(2)}, u32[]{:S(2)}) collective-permute-start(bf16[80,2048]{1,0:T(8,128)(2,1)S(1)} %pad_maximum_fusion.16), channel_id=1, source_target_pairs={{0,24},{4,28},{8,16},{12,20},{16,8},{20,12},{24,0},{28,4},{1,25},{... | collective-permute-start | bytes 983048 | tf_op jit(solution)/shard_map/grads_z3/ppermute | solution.py:12
  69.0 5.5 %collective-permute-done.15 = bf16[80,2048]{1,0:T(8,128)(2,1)S(1)} collective-permute-done((bf16[80,2048]{1,0:T(8,128)(2,1)S(1)}, bf16[80,2048]{1,0:T(8,128)(2,1)S(1)}, u32[]{:S(2)}, u32[]{:S(2)}) %collective-permute-start.15) | collective-permute-done | bytes 327712 | tf_op jit(solution)/shard_map/grads_z3/ppermute | solution.py:12
  75.8 4.6 %collective-permute-done.8 = bf16[160,2048]{1,0:T(8,128)(2,1)S(1)} collective-permute-done((bf16[160,2048]{1,0:T(8,128)(2,1)S(1)}, bf16[160,2048]{1,0:T(8,128)(2,1)S(1)}, u32[]{:S(2)}, u32[]{:S(2)}) %collective-permute-start.8) | collective-permute-done | bytes 655392 | tf_op jit(solution)/shard_map/grads_a/ppermute | solution.py:12
  80.3 1.4 multiply_convert_fusion.4
  82.9 1.4 fusion.94
  85.6 8.8 %collective-permute-done.16 = bf16[160,2048]{1,0:T(8,128)(2,1)S(1)} collective-permute-done((bf16[160,2048]{1,0:T(8,128)(2,1)S(1)}, bf16[160,2048]{1,0:T(8,128)(2,1)S(1)}, u32[]{:S(2)}, u32[]{:S(2)}) %collective-permute-start.16) | collective-permute-done | bytes 655392 | tf_op jit(solution)/shard_map/grads_b/ppermute | solution.py:12
  94.4 1.4 multiply_convert_fusion.2
  99.4 2.0 %collective-permute-done.19 = bf16[80,2048]{1,0:T(8,128)(2,1)S(1)} collective-permute-done((bf16[80,2048]{1,0:T(8,128)(2,1)S(1)}, bf16[80,2048]{1,0:T(8,128)(2,1)S(1)}, u32[]{:S(2)}, u32[]{:S(2)}) %collective-permute-start.19) | collective-permute-done | bytes 327712 | tf_op jit(solution)/shard_map/sums_z2/ppermute | solution.py:12
  101.5 2.7 %collective-permute-start.21 = (bf16[40,2048]{1,0:T(8,128)(2,1)S(1)}, bf16[40,2048]{1,0:T(8,128)(2,1)S(1)}, u32[]{:S(2)}, u32[]{:S(2)}) collective-permute-start(bf16[40,2048]{1,0:T(8,128)(2,1)S(1)} %get-tuple-element.99), channel_id=1, source_target_pairs={{0,16},{4,20},{8,24},{12,28},{16,0},{20,4},{24,8},{28,12},{1,17},{... | collective-permute-start | bytes 491528 | tf_op jit(solution)/shard_map/R4/ppermute | solution.py:12
  105.5 2.6 %convolution_convert_fusion = bf16[704,2048]{1,0:T(8,128)(2,1)S(1)} fusion(bf16[640,2048]{1,0:T(8,128)(2,1)S(1)} %get-tuple-element.81, bf16[640,352]{1,0:T(8,128)(2,1)S(1)} %slice.256, bf16[640,352]{1,0:T(8,128)(2,1)S(1)} %slice.255), kind=kOutput, calls=%fused_computation.1 | convolution fusion | flops 1848737792 | bytes 6406144 | tf_op jit(solution)/shard_map/dot_general | solution.py:20
  111.3 12.9 %collective-permute-done.20 = bf16[160,2048]{1,0:T(8,128)(2,1)S(1)} collective-permute-done((bf16[160,2048]{1,0:T(8,128)(2,1)S(1)}, bf16[160,2048]{1,0:T(8,128)(2,1)S(1)}, u32[]{:S(2)}, u32[]{:S(2)}) %collective-permute-start.20) | collective-permute-done | bytes 655392 | tf_op jit(solution)/shard_map/sums_near/ppermute | solution.py:12
  124.3 1.7 %collective-permute-start.27 = (bf16[40,2048]{1,0:T(8,128)(2,1)S(1)}, bf16[40,2048]{1,0:T(8,128)(2,1)S(1)}, u32[]{:S(2)}, u32[]{:S(2)}) collective-permute-start(bf16[40,2048]{1,0:T(8,128)(2,1)S(1)} %get-tuple-element.96), channel_id=1, source_target_pairs={{0,24},{4,28},{8,16},{12,20},{16,8},{20,12},{24,0},{28,4},{1,25},{... | collective-permute-start | bytes 491528 | tf_op jit(solution)/shard_map/R6/ppermute | solution.py:12
  126.0 1.8 %collective-permute-start.28 = (bf16[40,2048]{1,0:T(8,128)(2,1)S(1)}, bf16[40,2048]{1,0:T(8,128)(2,1)S(1)}, u32[]{:S(2)}, u32[]{:S(2)}) collective-permute-start(bf16[40,2048]{1,0:T(8,128)(2,1)S(1)} %get-tuple-element.97), channel_id=1, source_target_pairs={{0,28},{4,24},{8,20},{12,16},{16,12},{20,8},{24,4},{28,0},{1,29},{... | collective-permute-start | bytes 491528 | tf_op jit(solution)/shard_map/R7/ppermute | solution.py:12
  127.9 1.9 %collective-permute-start.23 = (bf16[40,2048]{1,0:T(8,128)(2,1)S(1)}, bf16[40,2048]{1,0:T(8,128)(2,1)S(1)}, u32[]{:S(2)}, u32[]{:S(2)}) collective-permute-start(bf16[40,2048]{1,0:T(8,128)(2,1)S(1)} %get-tuple-element.57), channel_id=1, source_target_pairs={{0,4},{4,0},{8,12},{12,8},{16,20},{20,16},{24,28},{28,24},{1,5},{5... | collective-permute-start | bytes 491528 | tf_op jit(solution)/shard_map/returned_1/ppermute | solution.py:12
  130.0 1.6 %collective-permute-done.24 = bf16[1056,2048]{1,0:T(8,128)(2,1)S(1)} collective-permute-done((bf16[1056,2048]{1,0:T(8,128)(2,1)S(1)}, bf16[1056,2048]{1,0:T(8,128)(2,1)S(1)}, u32[]{:S(2)}, u32[]{:S(2)}) %collective-permute-start.24) | collective-permute-done | bytes 4325408 | tf_op jit(solution)/shard_map/weight_grads/ppermute | solution.py:12
  131.8 2.4 %fusion.3 = bf16[1,352,2048]{2,1,0:T(8,128)(2,1)} fusion(bf16[640,2048]{1,0:T(8,128)(2,1)S(1)} %constant_dynamic-update-slice_fusion.22, bf16[1056,2048]{1,0:T(8,128)(2,1)S(1)} %collective-permute-done.24, bf16[640,704]{1,0:T(8,128)(2,1)S(1)} %constant_dynamic-update-slice_fusion.20), kind=kOutput, calls=%fused_computation.14 | convolution fusion | flops 924909568 | bytes 5996544 | tf_op jit(solution)/shard_map/dot_general | solution.py:20
  134.2 2.4 %fusion.4 = bf16[1,2048,352]{1,2,0:T(8,128)(2,1)} fusion(bf16[640,2048]{1,0:T(8,128)(2,1)S(1)} %get-tuple-element.81, bf16[1056,2048]{1,0:T(8,128)(2,1)S(1)} %collective-permute-done.24, bf16[640,704]{1,0:T(8,128)(2,1)S(1)} %constant_dynamic-update-slice_fusion.18), kind=kOutput, calls=%fused_computation.15 | convolution fusion | flops 924909568 | bytes 5996544 | tf_op jit(solution)/shard_map/dot_general | solution.py:20
  136.7 2.4 %fusion.5 = bf16[1,2048,352]{1,2,0:T(8,128)(2,1)} fusion(bf16[640,2048]{1,0:T(8,128)(2,1)S(1)} %get-tuple-element.81, bf16[1056,2048]{1,0:T(8,128)(2,1)S(1)} %collective-permute-done.24, bf16[640,704]{1,0:T(8,128)(2,1)S(1)} %constant_dynamic-update-slice_fusion.8), kind=kOutput, calls=%fused_computation.16 | convolution fusion | flops 924909568 | bytes 5996544 | tf_op jit(solution)/shard_map/dot_general | solution.py:20
  139.9 3.0 %collective-permute-done.26 = bf16[40,2048]{1,0:T(8,128)(2,1)S(1)} collective-permute-done((bf16[40,2048]{1,0:T(8,128)(2,1)S(1)}, bf16[40,2048]{1,0:T(8,128)(2,1)S(1)}, u32[]{:S(2)}, u32[]{:S(2)}) %collective-permute-start.26) | collective-permute-done | bytes 163872 | tf_op jit(solution)/shard_map/returned_3/ppermute | solution.py:12
  (130 shorter events, 33.9 us)
Async XLA Ops:
  0.6 11.3 %copy-start.5 = (s32[128,2]{0,1:T(2,128)S(1)}, s32[128,2]{0,1:T(2,128)}, u32[]{:S(2)}) copy-start(s32[128,2]{0,1:T(2,128)} %param.14) | copy-start | bytes 3076
  0.7 12.1 %copy-start.3 = (bf16[128,2048]{1,0:T(8,128)(2,1)S(1)}, bf16[128,2048]{1,0:T(8,128)(2,1)}, u32[]{:S(2)}) copy-start(bf16[128,2048]{1,0:T(8,128)(2,1)} %param.11) | copy-start | bytes 1572868
  0.7 17.3 %collective-permute-start.1 = (bf16[2048,352]{0,1:T(8,128)(2,1)}, bf16[2048,352]{0,1:T(8,128)(2,1)S(1)}, u32[]{:S(2)}, u32[]{:S(2)}) collective-permute-start(bf16[2048,352]{0,1:T(8,128)(2,1)} %bitcast.95), channel_id=1, source_target_pairs={{0,1},{1,0},{2,3},{3,2},{4,5},{5,4},{6,7},{7,6},{8,9},{9,8},{10,11... | collective-permute-start | bytes 4325384 | tf_op jit(solution)/shard_map/gate_weight/ppermute | solution.py:12
  1.2 15.4 %collective-permute-start = (bf16[128,2048]{1,0:T(8,128)(2,1)}, bf16[128,2048]{1,0:T(8,128)(2,1)}, u32[]{:S(2)}, u32[]{:S(2)}) collective-permute-start(bf16[128,2048]{1,0:T(8,128)(2,1)} %param.12), channel_id=1, source_target_pairs={{0,2},{1,3},{2,0},{3,1},{4,6},{5,7},{6,4},{7,5},{8,10},{9,11},{10,... | collective-permute-start | bytes 1572872 | tf_op jit(solution)/shard_map/teacher_across/ppermute | solution.py:12
  5.8 13.6 %collective-permute-start.4 = (bf16[120,2048]{1,0:T(8,128)(2,1)}, bf16[120,2048]{1,0:T(8,128)(2,1)}, u32[]{:S(2)}, u32[]{:S(2)}) collective-permute-start(bf16[120,2048]{1,0:T(8,128)(2,1)} %convolution_convert_fusion.3), channel_id=1, source_target_pairs={{0,4},{4,0},{8,12},{12,8},{16,20},{20,16},{24,28},{28,24},{1,5},{5... | collective-permute-start | bytes 1474568 | tf_op jit(solution)/shard_map/inputs_side/ppermute | solution.py:12
  8.2 23.7 %collective-permute-start.10 = (bf16[40,2048]{1,0:T(8,128)(2,1)}, bf16[40,2048]{1,0:T(8,128)(2,1)S(1)}, u32[]{:S(2)}, u32[]{:S(2)}) collective-permute-start(bf16[40,2048]{1,0:T(8,128)(2,1)} %convolution_convert_fusion.7), channel_id=1, source_target_pairs={{0,16},{4,20},{8,24},{12,28},{16,0},{20,4},{24,8},{28,12},{1,17},{... | collective-permute-start | bytes 491528 | tf_op jit(solution)/shard_map/inputs_far_4/ppermute | solution.py:12
  11.7 17.1 %collective-permute-start.11 = (bf16[40,2048]{1,0:T(8,128)(2,1)}, bf16[40,2048]{1,0:T(8,128)(2,1)S(1)}, u32[]{:S(2)}, u32[]{:S(2)}) collective-permute-start(bf16[40,2048]{1,0:T(8,128)(2,1)} %convolution_convert_fusion.6), channel_id=1, source_target_pairs={{0,20},{4,16},{8,28},{12,24},{16,4},{20,0},{24,12},{28,8},{1,21},{... | collective-permute-start | bytes 491528 | tf_op jit(solution)/shard_map/inputs_far_5/ppermute | solution.py:12
  17.9 3.4 %collective-permute-start.2 = (bf16[256,2048]{1,0:T(8,128)(2,1)S(1)}, bf16[256,2048]{1,0:T(8,128)(2,1)S(1)}, u32[]{:S(2)}, u32[]{:S(2)}) collective-permute-start(bf16[256,2048]{1,0:T(8,128)(2,1)S(1)} %pad_maximum_fusion.6), channel_id=1, source_target_pairs={{0,1},{1,0},{2,3},{3,2},{4,5},{5,4},{6,7},{7,6},{8,9},{9,8},{10,11... | collective-permute-start | bytes 3145736 | tf_op jit(solution)/shard_map/teacher_beside/ppermute | solution.py:12
  21.3 29.6 %collective-permute-start.13 = (bf16[2048,352]{0,1:T(8,128)(2,1)S(1)}, bf16[2048,352]{0,1:T(8,128)(2,1)S(1)}, u32[]{:S(2)}, u32[]{:S(2)}) collective-permute-start(bf16[2048,352]{0,1:T(8,128)(2,1)S(1)} %bitcast.105), channel_id=1, source_target_pairs={{0,1},{1,0},{2,3},{3,2},{4,5},{5,4},{6,7},{7,6},{8,9},{9,8},{10,11... | collective-permute-start | bytes 4325384 | tf_op jit(solution)/shard_map/up_weight/ppermute | solution.py:12
  24.1 12.7 %copy-start.6 = (bf16[1,352,2048]{2,1,0:T(8,128)(2,1)S(1)}, bf16[1,352,2048]{2,1,0:T(8,128)(2,1)}, u32[]{:S(2)}) copy-start(bf16[1,352,2048]{2,1,0:T(8,128)(2,1)} %param.19) | copy-start | bytes 4325380
  24.1 20.0 %collective-permute-start.3 = (bf16[160,2048]{1,0:T(8,128)(2,1)S(1)}, bf16[160,2048]{1,0:T(8,128)(2,1)S(1)}, u32[]{:S(2)}, u32[]{:S(2)}) collective-permute-start(bf16[160,2048]{1,0:T(8,128)(2,1)S(1)} %convolution_convert_fusion.2), channel_id=1, source_target_pairs={{0,4},{4,0},{8,12},{12,8},{16,20},{20,16},{24,28},{28,24},{1,5},{5... | collective-permute-start | bytes 1966088 | tf_op jit(solution)/shard_map/grads_side/ppermute | solution.py:12
  24.7 12.2 %collective-permute-start.5 = (bf16[80,2048]{1,0:T(8,128)(2,1)S(1)}, bf16[80,2048]{1,0:T(8,128)(2,1)S(1)}, u32[]{:S(2)}, u32[]{:S(2)}) collective-permute-start(bf16[80,2048]{1,0:T(8,128)(2,1)S(1)} %get-tuple-element.39), channel_id=1, source_target_pairs={{0,24},{4,28},{8,16},{12,20},{16,8},{20,12},{24,0},{28,4},{1,25},{... | collective-permute-start | bytes 983048 | tf_op jit(solution)/shard_map/inputs_z3/ppermute | solution.py:12
  28.7 15.4 %collective-permute-start.6 = (bf16[80,2048]{1,0:T(8,128)(2,1)S(1)}, bf16[80,2048]{1,0:T(8,128)(2,1)S(1)}, u32[]{:S(2)}, u32[]{:S(2)}) collective-permute-start(bf16[80,2048]{1,0:T(8,128)(2,1)S(1)} %get-tuple-element.41), channel_id=1, source_target_pairs={{0,8},{4,12},{8,0},{12,4},{16,24},{20,28},{24,16},{28,20},{1,9},{5... | collective-permute-start | bytes 983048 | tf_op jit(solution)/shard_map/inputs_z1/ppermute | solution.py:12
  31.9 16.7 %collective-permute-start.12 = (bf16[160,2048]{1,0:T(8,128)(2,1)S(1)}, bf16[160,2048]{1,0:T(8,128)(2,1)S(1)}, u32[]{:S(2)}, u32[]{:S(2)}) collective-permute-start(bf16[160,2048]{1,0:T(8,128)(2,1)S(1)} %pad_maximum_fusion.8), channel_id=1, source_target_pairs={{0,2},{1,3},{2,0},{3,1},{4,6},{5,7},{6,4},{7,5},{8,10},{9,11},{10,... | collective-permute-start | bytes 1966088 | tf_op jit(solution)/shard_map/inputs_a/ppermute | solution.py:12
  36.9 38.9 %collective-permute-start.9 = (bf16[352,2048]{1,0:T(8,128)(2,1)S(1)}, bf16[352,2048]{1,0:T(8,128)(2,1)S(1)}, u32[]{:S(2)}, u32[]{:S(2)}) collective-permute-start(bf16[352,2048]{1,0:T(8,128)(2,1)S(1)} %bitcast.102), channel_id=1, source_target_pairs={{0,1},{1,0},{2,3},{3,2},{4,5},{5,4},{6,7},{7,6},{8,9},{9,8},{10,11... | collective-permute-start | bytes 4325384 | tf_op jit(solution)/shard_map/down_weight/ppermute | solution.py:12
  44.3 18.2 %collective-permute-start.7 = (bf16[80,2048]{1,0:T(8,128)(2,1)S(1)}, bf16[80,2048]{1,0:T(8,128)(2,1)S(1)}, u32[]{:S(2)}, u32[]{:S(2)}) collective-permute-start(bf16[80,2048]{1,0:T(8,128)(2,1)S(1)} %pad_maximum_fusion.12), channel_id=1, source_target_pairs={{0,16},{4,20},{8,24},{12,28},{16,0},{20,4},{24,8},{28,12},{1,17},{... | collective-permute-start | bytes 983048 | tf_op jit(solution)/shard_map/grads_z2/ppermute | solution.py:12
  47.1 21.9 %collective-permute-start.14 = (bf16[80,2048]{1,0:T(8,128)(2,1)S(1)}, bf16[80,2048]{1,0:T(8,128)(2,1)S(1)}, u32[]{:S(2)}, u32[]{:S(2)}) collective-permute-start(bf16[80,2048]{1,0:T(8,128)(2,1)S(1)} %pad_maximum_fusion.15), channel_id=1, source_target_pairs={{0,8},{4,12},{8,0},{12,4},{16,24},{20,28},{24,16},{28,20},{1,9},{5... | collective-permute-start | bytes 983048 | tf_op jit(solution)/shard_map/grads_z1/ppermute | solution.py:12
  48.6 17.7 %collective-permute-start.17 = (bf16[160,2048]{1,0:T(8,128)(2,1)S(1)}, bf16[160,2048]{1,0:T(8,128)(2,1)S(1)}, u32[]{:S(2)}, u32[]{:S(2)}) collective-permute-start(bf16[160,2048]{1,0:T(8,128)(2,1)S(1)} %pad_maximum_fusion.10), channel_id=1, source_target_pairs={{0,2},{1,3},{2,0},{3,1},{4,6},{5,7},{6,4},{7,5},{8,10},{9,11},{10,... | collective-permute-start | bytes 1966088 | tf_op jit(solution)/shard_map/inputs_b/ppermute | solution.py:12
  62.6 17.7 %collective-permute-start.8 = (bf16[160,2048]{1,0:T(8,128)(2,1)S(1)}, bf16[160,2048]{1,0:T(8,128)(2,1)S(1)}, u32[]{:S(2)}, u32[]{:S(2)}) collective-permute-start(bf16[160,2048]{1,0:T(8,128)(2,1)S(1)} %pad_maximum_fusion.7), channel_id=1, source_target_pairs={{0,2},{1,3},{2,0},{3,1},{4,6},{5,7},{6,4},{7,5},{8,10},{9,11},{10,... | collective-permute-start | bytes 1966088 | tf_op jit(solution)/shard_map/grads_a/ppermute | solution.py:12
  63.7 10.9 %collective-permute-start.15 = (bf16[80,2048]{1,0:T(8,128)(2,1)S(1)}, bf16[80,2048]{1,0:T(8,128)(2,1)S(1)}, u32[]{:S(2)}, u32[]{:S(2)}) collective-permute-start(bf16[80,2048]{1,0:T(8,128)(2,1)S(1)} %pad_maximum_fusion.16), channel_id=1, source_target_pairs={{0,24},{4,28},{8,16},{12,20},{16,8},{20,12},{24,0},{28,4},{1,25},{... | collective-permute-start | bytes 983048 | tf_op jit(solution)/shard_map/grads_z3/ppermute | solution.py:12
  74.6 19.8 %collective-permute-start.16 = (bf16[160,2048]{1,0:T(8,128)(2,1)S(1)}, bf16[160,2048]{1,0:T(8,128)(2,1)S(1)}, u32[]{:S(2)}, u32[]{:S(2)}) collective-permute-start(bf16[160,2048]{1,0:T(8,128)(2,1)S(1)} %pad_maximum_fusion.9), channel_id=1, source_target_pairs={{0,2},{1,3},{2,0},{3,1},{4,6},{5,7},{6,4},{7,5},{8,10},{9,11},{10,... | collective-permute-start | bytes 1966088 | tf_op jit(solution)/shard_map/grads_b/ppermute | solution.py:12
  84.4 16.9 %collective-permute-start.19 = (bf16[80,2048]{1,0:T(8,128)(2,1)S(1)}, bf16[80,2048]{1,0:T(8,128)(2,1)S(1)}, u32[]{:S(2)}, u32[]{:S(2)}) collective-permute-start(bf16[80,2048]{1,0:T(8,128)(2,1)S(1)} %get-tuple-element.77), channel_id=1, source_target_pairs={{0,2},{1,3},{2,0},{3,1},{4,6},{5,7},{6,4},{7,5},{8,10},{9,11},{10,... | collective-permute-start | bytes 983048 | tf_op jit(solution)/shard_map/sums_z2/ppermute | solution.py:12
  98.3 11.2 %collective-permute-start.18 = (bf16[80,2048]{1,0:T(8,128)(2,1)S(1)}, bf16[80,2048]{1,0:T(8,128)(2,1)S(1)}, u32[]{:S(2)}, u32[]{:S(2)}) collective-permute-start(bf16[80,2048]{1,0:T(8,128)(2,1)S(1)} %get-tuple-element.74), channel_id=1, source_target_pairs={{0,2},{1,3},{2,0},{3,1},{4,6},{5,7},{6,4},{7,5},{8,10},{9,11},{10,... | collective-permute-start | bytes 983048 | tf_op jit(solution)/shard_map/sums_z3/ppermute | solution.py:12
  101.5 22.7 %collective-permute-start.21 = (bf16[40,2048]{1,0:T(8,128)(2,1)S(1)}, bf16[40,2048]{1,0:T(8,128)(2,1)S(1)}, u32[]{:S(2)}, u32[]{:S(2)}) collective-permute-start(bf16[40,2048]{1,0:T(8,128)(2,1)S(1)} %get-tuple-element.99), channel_id=1, source_target_pairs={{0,16},{4,20},{8,24},{12,28},{16,0},{20,4},{24,8},{28,12},{1,17},{... | collective-permute-start | bytes 491528 | tf_op jit(solution)/shard_map/R4/ppermute | solution.py:12
  104.2 20.1 %collective-permute-start.22 = (bf16[40,2048]{1,0:T(8,128)(2,1)S(1)}, bf16[40,2048]{1,0:T(8,128)(2,1)S(1)}, u32[]{:S(2)}, u32[]{:S(2)}) collective-permute-start(bf16[40,2048]{1,0:T(8,128)(2,1)S(1)} %get-tuple-element.98), channel_id=1, source_target_pairs={{0,20},{4,16},{8,28},{12,24},{16,4},{20,0},{24,12},{28,8},{1,21},{... | collective-permute-start | bytes 491528 | tf_op jit(solution)/shard_map/R5/ppermute | solution.py:12
  109.5 14.7 %collective-permute-start.20 = (bf16[160,2048]{1,0:T(8,128)(2,1)S(1)}, bf16[160,2048]{1,0:T(8,128)(2,1)S(1)}, u32[]{:S(2)}, u32[]{:S(2)}) collective-permute-start(bf16[160,2048]{1,0:T(8,128)(2,1)S(1)} %pad_maximum_fusion.11), channel_id=1, source_target_pairs={{0,2},{1,3},{2,0},{3,1},{4,6},{5,7},{6,4},{7,5},{8,10},{9,11},{10,... | collective-permute-start | bytes 1966088 | tf_op jit(solution)/shard_map/sums_near/ppermute | solution.py:12
  124.2 7.3 %collective-permute-start.24 = (bf16[1056,2048]{1,0:T(8,128)(2,1)S(1)}, bf16[1056,2048]{1,0:T(8,128)(2,1)S(1)}, u32[]{:S(2)}, u32[]{:S(2)}) collective-permute-start(bf16[1056,2048]{1,0:T(8,128)(2,1)S(1)} %pad_maximum_fusion), channel_id=1, source_target_pairs={{0,1},{1,0},{2,3},{3,2},{4,5},{5,4},{6,7},{7,6},{8,9},{9,8},{10,11... | collective-permute-start | bytes 12976136 | tf_op jit(solution)/shard_map/weight_grads/ppermute | solution.py:12
  124.3 14.8 %collective-permute-start.27 = (bf16[40,2048]{1,0:T(8,128)(2,1)S(1)}, bf16[40,2048]{1,0:T(8,128)(2,1)S(1)}, u32[]{:S(2)}, u32[]{:S(2)}) collective-permute-start(bf16[40,2048]{1,0:T(8,128)(2,1)S(1)} %get-tuple-element.96), channel_id=1, source_target_pairs={{0,24},{4,28},{8,16},{12,20},{16,8},{20,12},{24,0},{28,4},{1,25},{... | collective-permute-start | bytes 491528 | tf_op jit(solution)/shard_map/R6/ppermute | solution.py:12
  126.0 13.2 %collective-permute-start.28 = (bf16[40,2048]{1,0:T(8,128)(2,1)S(1)}, bf16[40,2048]{1,0:T(8,128)(2,1)S(1)}, u32[]{:S(2)}, u32[]{:S(2)}) collective-permute-start(bf16[40,2048]{1,0:T(8,128)(2,1)S(1)} %get-tuple-element.97), channel_id=1, source_target_pairs={{0,28},{4,24},{8,20},{12,16},{16,12},{20,8},{24,4},{28,0},{1,29},{... | collective-permute-start | bytes 491528 | tf_op jit(solution)/shard_map/R7/ppermute | solution.py:12
  127.9 15.3 %collective-permute-start.23 = (bf16[40,2048]{1,0:T(8,128)(2,1)S(1)}, bf16[40,2048]{1,0:T(8,128)(2,1)S(1)}, u32[]{:S(2)}, u32[]{:S(2)}) collective-permute-start(bf16[40,2048]{1,0:T(8,128)(2,1)S(1)} %get-tuple-element.57), channel_id=1, source_target_pairs={{0,4},{4,0},{8,12},{12,8},{16,20},{20,16},{24,28},{28,24},{1,5},{5... | collective-permute-start | bytes 491528 | tf_op jit(solution)/shard_map/returned_1/ppermute | solution.py:12
  129.9 10.0 %collective-permute-start.25 = (bf16[40,2048]{1,0:T(8,128)(2,1)S(1)}, bf16[40,2048]{1,0:T(8,128)(2,1)S(1)}, u32[]{:S(2)}, u32[]{:S(2)}) collective-permute-start(bf16[40,2048]{1,0:T(8,128)(2,1)S(1)} %get-tuple-element.66), channel_id=1, source_target_pairs={{0,8},{4,12},{8,0},{12,4},{16,24},{20,28},{24,16},{28,20},{1,9},{5... | collective-permute-start | bytes 491528 | tf_op jit(solution)/shard_map/returned_2/ppermute | solution.py:12
  131.6 11.4 %collective-permute-start.26 = (bf16[40,2048]{1,0:T(8,128)(2,1)S(1)}, bf16[40,2048]{1,0:T(8,128)(2,1)S(1)}, u32[]{:S(2)}, u32[]{:S(2)}) collective-permute-start(bf16[40,2048]{1,0:T(8,128)(2,1)S(1)} %get-tuple-element.67), channel_id=1, source_target_pairs={{0,12},{4,8},{8,4},{12,0},{16,28},{20,24},{24,20},{28,16},{1,13},{... | collective-permute-start | bytes 491528 | tf_op jit(solution)/shard_map/returned_3/ppermute | solution.py:12
  (7 other events, 38.9 us)
